TPU v7x, 512 devices: a whole 4x8x8 slice. The times are simulated.
512 devices in a mesh: dp: 16 (over y, core), mp: 32 (over x, z).
Axes of the slice: x: 4, y: 8, z: 8, core: 2. Of those that a mesh axis runs over, the one named last changes fastest.
Arguments:
- layer_input: bfloat16 [8192, 4096], P('dp', 'mp'), may hold values from -6 to 6
- gate_pre: bfloat16 [8192, 14336], P('dp', 'mp'), may hold values from -6 to 6
- up_pre: bfloat16 [8192, 14336], P('dp', 'mp'), may hold values from -6 to 6
- out_grad: bfloat16 [8192, 4096], P('dp', 'mp'), may hold values from -36 to 36
- w_down: bfloat16 [14336, 4096], P('mp'), may hold values from -0.09375 to 0.09375
- proj_input: bfloat16 [4096, 64], P('mp'), may hold values from -4 to 4
- proj_hidden: bfloat16 [14336, 64], P('mp'), may hold values from -4 to 4
- proj_gate: bfloat16 [14336, 64], P('mp'), may hold values from -0.046875 to 0.046875
- proj_upward: bfloat16 [14336, 64], P('mp'), may hold values from -0.046875 to 0.046875
- proj_output: bfloat16 [64, 4096], P(None, 'mp'), may hold values from -0.09375 to 0.09375
- seq_ids: int32 [16, 512], P('dp'), may hold values from 0 to 7, never falling along the last dimension, each value on 1 to 128 neighbouring positions
Outputs:
- features: float32 [128, 3, 4096], P('dp', None, 'mp')
Inputs may be any that keep to these rules, and one draw needn't show every extreme that they name: `seq_ids`: within each row the ids never fall and every id appears; every sequence has 1 to 128 tokens and some sequence of each row has exactly 128.
All inputs are finite; a program needn't handle non-finite values.
Results may differ from a plain program's by a relative error of at most 0.0029.
Values may be sent and summed in bfloat16 or wider, within the bound.
No kernel may reach another device: no remote copies, remote signals or barrier semaphores. Data moves between devices by JAX's collectives and lax.ppermute only.
A program may use at most 64 MiB of HBM per device.

v0:
```python
import jax
import jax.numpy as jnp
from jax import lax
from jax.sharding import PartitionSpec as P

SEQ_DEV = 8


def silu_parts(gate_value):
    sigmoid_v = jax.nn.sigmoid(gate_value)
    return (gate_value * sigmoid_v, sigmoid_v * (1.0 + gate_value * (1.0 - sigmoid_v)))


def layer_features(member, left_in, left_hid, gate_factor, up_factor, out_factor):
    seq_count = member.shape[0]
    tok_rows = member.shape[1]
    left_width = left_in.shape[1]
    rank_dim = out_factor.shape[1]
    weighted_in = (member[:, None, :] * left_in.T[None, :, :]).reshape(
        seq_count * left_width, tok_rows
    )
    weighted_hid = (member[:, None, :] * left_hid.T[None, :, :]).reshape(
        seq_count * left_width, tok_rows
    )
    paired = jnp.dot(
        weighted_in,
        jnp.concatenate([gate_factor, up_factor], axis=1),
        precision=lax.Precision.HIGHEST,
    )
    paired = paired.reshape(seq_count, left_width, 2, rank_dim)
    gate_feat = paired[:, :, 0, :].reshape(seq_count, left_width * rank_dim)
    up_feat = paired[:, :, 1, :].reshape(seq_count, left_width * rank_dim)
    down_feat = jnp.dot(weighted_hid, out_factor, precision=lax.Precision.HIGHEST).reshape(
        seq_count, left_width * rank_dim
    )
    return jnp.stack([gate_feat, up_feat, down_feat], axis=1)


def per_device(
    layer_input,
    gate_pre,
    up_pre,
    out_grad,
    w_down,
    proj_input,
    proj_hidden,
    proj_gate,
    proj_upward,
    proj_output,
    seq_ids,
):
    contract = (((1,), (1,)), ((), ()))
    rank_dim = proj_input.shape[1]
    own_width = rank_dim // lax.axis_size("mp")
    position = lax.axis_index("mp")
    gate_value = gate_pre.astype(jnp.float32)
    up_value = up_pre.astype(jnp.float32)
    activated, slope_value = silu_parts(gate_value)
    hidden = (activated * up_value).astype(jnp.bfloat16)
    in_part = jnp.dot(layer_input, proj_input, preferred_element_type=jnp.float32)
    hid_part = jnp.dot(hidden, proj_hidden, preferred_element_type=jnp.float32)
    hidden_grad = lax.dot_general(
        lax.all_gather(out_grad, "mp", axis=1, tiled=True),
        w_down,
        contract,
        preferred_element_type=jnp.float32,
    )
    out_part = lax.dot_general(out_grad, proj_output, contract, preferred_element_type=jnp.float32)
    gate_grad = (hidden_grad * up_value * slope_value).astype(jnp.bfloat16)
    upward_grad = (hidden_grad * activated).astype(jnp.bfloat16)
    gate_part = jnp.dot(gate_grad, proj_gate, preferred_element_type=jnp.float32)
    up_part = jnp.dot(upward_grad, proj_upward, preferred_element_type=jnp.float32)
    gate_part, up_part = (gate_part, up_part)
    in_factor, hid_factor, gate_factor, up_factor, out_factor = lax.psum(
        (in_part, hid_part, gate_part, up_part, out_part), "mp"
    )
    member = (seq_ids[0][None, :] == jnp.arange(SEQ_DEV, dtype=jnp.int32)[:, None]).astype(
        jnp.float32
    )
    own_in = lax.dynamic_slice_in_dim(in_factor, position * own_width, own_width, 1)
    own_hid = lax.dynamic_slice_in_dim(hid_factor, position * own_width, own_width, 1)
    raw_feat = layer_features(member, own_in, own_hid, gate_factor, up_factor, out_factor)
    squares = jnp.sum(raw_feat * raw_feat, axis=(0, 2))
    total_sq = lax.psum(squares, ("dp", "mp"))
    entries = raw_feat.shape[0] * lax.axis_size("dp") * rank_dim * rank_dim
    scale_value = lax.rsqrt(total_sq / entries + 1e-06)
    return raw_feat * scale_value[None, :, None]


def solution(mesh):
    in_specs = (
        P("dp", "mp"),
        P("dp", "mp"),
        P("dp", "mp"),
        P("dp", "mp"),
        P("mp", None),
        P("mp", None),
        P("mp", None),
        P("mp", None),
        P("mp", None),
        P(None, "mp"),
        P("dp", None),
    )
    out_specs = P("dp", None, "mp")
    return jax.shard_map(
        per_device, mesh=mesh, in_specs=in_specs, out_specs=out_specs, check_vma=False
    )
```

profile of v0, /device:TPU:1, one launch (start us, length us, event | category | flops | bytes accessed | tf_op | source)
XLA Modules:
  0.0 380.8 jit_solution(3173501299218017881)
XLA Ops:
  6.5 0.0 copy-start
  6.5 0.0 all-gather.2.cloned.1.call-start
  6.5 0.7 all-gather.2.cloned.1.call-update
  7.3 0.0 all-reduce.3.cloned.1.call-start
  7.3 0.1 copy-done
  7.4 1.5 fusion.20
  9.0 1.8 fusion.22
  10.8 2.3 fusion.9
  13.1 0.0 copy-start.2
  13.1 0.0 copy-start.3
  13.1 0.0 copy-start.4
  13.1 89.2 %all-gather.2.cloned.1.call-done = bf16[512,4096]{1,0:T(8,128)(2,1)} async-done(((bf16[512,128]{1,0:T(8,128)(2,1)}), bf16[512,4096]{1,0:T(8,128)(2,1)}) %all-gather.2.cloned.1.call-update) | async-done | bytes 4194320 | tf_op jit(solution)/shard_map/all_gather | solution.py:63
  102.3 5.4 %fusion.21 = f32[512,448]{0,1:T(8,128)S(1)} fusion(bf16[512,4096]{1,0:T(8,128)(2,1)} %all-gather.2.cloned.1.call-done, bf16[448,4096]{1,0:T(8,128)(2,1)} %param.15), kind=kOutput, calls=%fused_computation.37 | convolution fusion | flops 1879048192 | bytes 8781824 | tf_op jit(solution)/shard_map/dot_general | solution.py:62
  107.7 0.0 copy-done.2
  107.7 0.0 copy-done.3
  107.7 0.0 copy-done.4
  107.7 0.0 copy-start.5
  107.7 0.0 copy-start.1
  107.7 1.2 fusion.11
  108.9 0.0 copy-done.5
  108.9 1.1 fusion.8
  110.0 0.0 all-reduce.3.cloned.1.call-update
  110.0 0.0 copy-done.1
  110.0 159.6 %all-reduce.3.cloned.1.call-done = (f32[512,64]{0,1:T(8,128)}, f32[512,64]{0,1:T(8,128)}, f32[512,64]{0,1:T(8,128)}, f32[512,64]{0,1:T(8,128)}, f32[512,64]{1,0:T(8,128)}) async-done(((f32[512,64]{0,1:T(8,128)}, f32[512,64]{0,1:T(8,128)}, f32[512,64]{0,1:T(8,128)}, f32[512,64]{0,1:T(8,128)}, f32[512,64]{1,0:T(8,128)}), (f32[512,64]{0,1:T(8,128)}, f32[512,64]{0,1:T(8,128)}, f32[512,64]{0,1:T(8,128)}, ...) | async-done | bytes 655376 | tf_op jit(solution)/shard_map/psum | solution.py:74
  269.6 1.0 pad_maximum_fusion
  270.6 0.8 dynamic-slice_bitcast_fusion
  271.4 0.4 fusion.13
  271.8 0.1 stack_reshape_squeeze.6
  271.9 0.1 stack_reshape_squeeze.7
  272.0 1.2 fusion.23
  273.2 0.1 stack_reshape.3
  273.3 0.1 multiply_reduce_fusion
  273.4 99.9 %psum.47 = f32[3]{0:T(128)S(1)} all-reduce(f32[3]{0:T(128)S(1)} %multiply_reduce_fusion), channel_id=1, replica_groups=mesh['dp'=16,'mp'=32] {'dp','mp'}, use_global_device_ids=true, to_apply=%region_6.0 | all-reduce | flops 3 | bytes 24 | tf_op jit(solution)/shard_map/psum | solution.py:84
  373.3 0.7 broadcast_multiply_fusion.1
  (10 shorter events, 0.1 us)
Async XLA Ops:
  6.5 0.9 copy-start
  6.5 95.7 %all-gather.2.cloned.1.call-start = ((), (), s32[]{:S(2)}) async-start(), calls=%async_computation | async-start | bytes 4325376 | tf_op jit(solution)/shard_map/all_gather | solution.py:63
  7.3 262.4 %all-reduce.3.cloned.1.call-start = ((), (), s32[]{:S(2)}) async-start(), calls=%async_computation.1 | async-start | bytes 1572864 | tf_op jit(solution)/shard_map/psum | solution.py:74
  13.1 94.6 %copy-start.2 = (bf16[512,448]{0,1:T(8,128)(2,1)S(1)}, bf16[512,448]{0,1:T(8,128)(2,1)}, u32[]{:S(2)}) copy-start(bf16[512,448]{0,1:T(8,128)(2,1)} %param.13) | copy-start | bytes 1376260
  13.1 94.6 %copy-start.3 = (bf16[512,448]{0,1:T(8,128)(2,1)S(1)}, bf16[512,448]{0,1:T(8,128)(2,1)}, u32[]{:S(2)}) copy-start(bf16[512,448]{0,1:T(8,128)(2,1)} %param.12) | copy-start | bytes 1376260
  13.1 94.6 %copy-start.4 = (bf16[448,64]{0,1:T(8,128)(2,1)S(1)}, bf16[448,64]{0,1:T(8,128)(2,1)}, u32[]{:S(2)}) copy-start(bf16[448,64]{0,1:T(8,128)(2,1)} %param.18) | copy-start | bytes 172036
  107.7 1.2 copy-start.5
  107.7 2.3 copy-start.1
Sparse Core Ops, SparseCore 0:
  10.4 91.8 all-gather.1
  110.1 159.4 all-reduce.2
where the time goes:
time: 381 us
  waiting for transfers between devices  250 us (66%)
  blocking collectives  99.9 us (26%)
  matrix products  14.8 us (4%)
  between operations  13.5 us (4%)
    psum x1, waiting for transfers between devices, per_device(): lax.psum((in_part, hid_part, gate_part, up_part, out_part), 'mp')  160 us
    psum x1, blocking collectives, per_device(): total_sq = lax.psum(squares, ('dp', 'mp'))  99.9 us
    all_gather x1, waiting for transfers between devices, per_device(): lax.all_gather(out_grad, 'mp', axis=1, tiled=True)  89.2 us
  transfers between devices with their start and end apart: 2, of which 2 were waited for; matrix products, arithmetic and copies ran while one was open for 1% of the time, Pallas kernels for 0%

commit v1 on v0

v1 whole, which is shorter than its diff:
```python
import jax
import jax.numpy as jnp
from jax import lax
from jax.sharding import PartitionSpec as P

SEQ_DEV = 8
NX = 4
NZ = 8
X_GROUPS = [[x * NZ + z for x in range(NX)] for z in range(NZ)]
Z_GROUPS = [[x * NZ + z for z in range(NZ)] for x in range(NX)]
CONTRACT = (((1,), (1,)), ((), ()))


def split_hi_lo(value):
    high = lax.reduce_precision(value, 8, 7)
    return high.astype(jnp.bfloat16), (value - high).astype(jnp.bfloat16)


def x_shift(step):
    return [
        (x * NZ + z, ((x + step) % NX) * NZ + z) for x in range(NX) for z in range(NZ)
    ]


def hidden_part(gate_pre, up_pre):
    gate_value = gate_pre.astype(jnp.float32)
    up_value = up_pre.astype(jnp.float32)
    sigmoid_v = jax.nn.sigmoid(gate_value)
    activated = gate_value * sigmoid_v
    slope = sigmoid_v * (1.0 + gate_value * (1.0 - sigmoid_v))
    return activated, slope, up_value


def per_device(
    layer_input,
    gate_pre,
    up_pre,
    out_grad,
    w_down,
    proj_input,
    proj_hidden,
    proj_gate,
    proj_upward,
    proj_output,
    seq_ids,
):
    tokens, width = out_grad.shape
    half = tokens // 2
    rank = proj_input.shape[1]
    mp_size = lax.axis_size("mp")
    dp_size = lax.axis_size("dp")
    own_tokens = tokens // mp_size
    position = lax.axis_index("mp")
    x_pos = position // NZ

    in_part = jnp.dot(layer_input, proj_input, preferred_element_type=jnp.float32)
    out_part = lax.dot_general(out_grad, proj_output, CONTRACT, preferred_element_type=jnp.float32)
    both = jnp.concatenate([in_part, out_part], axis=1)

    high, low = split_hi_lo(both)
    share = tokens // NX
    sent = jnp.concatenate(
        [
            jnp.broadcast_to(out_grad[None, half:], (NX, half, width)),
            high.reshape(NX, share, 2 * rank),
            low.reshape(NX, share, 2 * rank),
        ],
        axis=1,
    )
    got = lax.all_to_all(sent, "mp", 0, 0, axis_index_groups=X_GROUPS)
    late_x = got[:, :half]
    both = jnp.sum(
        got[:, half : half + share].astype(jnp.float32) + got[:, half + share :].astype(jnp.float32), axis=0
    )
    late = lax.all_gather(late_x, "mp", axis=0, axis_index_groups=Z_GROUPS)

    high, low = split_hi_lo(both)
    sent = jnp.concatenate(
        [
            jnp.broadcast_to(out_grad[None, :half], (NZ, half, width)),
            high.reshape(NZ, own_tokens, 2 * rank),
            low.reshape(NZ, own_tokens, 2 * rank),
        ],
        axis=1,
    )
    got = lax.all_to_all(sent, "mp", 0, 0, axis_index_groups=Z_GROUPS)
    early_z = got[:, :half]
    both = jnp.sum(
        got[:, half : half + own_tokens].astype(jnp.float32) + got[:, half + own_tokens :].astype(jnp.float32),
        axis=0,
    )
    early = [early_z] + [lax.ppermute(early_z, "mp", x_shift(step)) for step in range(1, NX)]

    both = lax.all_to_all(jnp.broadcast_to(both[None], (mp_size, own_tokens, 2 * rank)), "mp", 0, 0)
    both = both.reshape(tokens, 2 * rank)
    in_factor, out_factor = both[:, :rank], both[:, rank:]

    member = (seq_ids[0][None, :] == jnp.arange(SEQ_DEV, dtype=jnp.int32)[:, None]).astype(jnp.float32)
    activated, slope, up_value = hidden_part(gate_pre, up_pre)
    hidden = (activated * up_value).astype(jnp.bfloat16)
    hid_part = jnp.dot(hidden, proj_hidden, preferred_element_type=jnp.float32)
    left_in = (in_factor.T[:, None, :] * member[None]).reshape(rank * SEQ_DEV, tokens)
    left_hid = hid_part.T.reshape(rank // 2, 2, 1, tokens) * member[None, None]
    down_raw = [
        jnp.dot(
            left_hid[:, i].reshape(rank // 2 * SEQ_DEV, tokens), out_factor, precision=lax.Precision.HIGHEST
        ).reshape(mp_size, SEQ_DEV, rank)
        for i in range(2)
    ]
    down_raw = jnp.concatenate(down_raw, axis=2)

    w_blocks = w_down.reshape(w_down.shape[0], NX, NZ, width)
    early_grad = 0.0
    for step in range(NX):
        w_step = lax.dynamic_index_in_dim(w_blocks, (x_pos - step) % NX, 1, keepdims=False)
        rows = early[step].transpose(1, 0, 2).reshape(half, NZ * width)
        early_grad += lax.dot_general(
            rows, w_step.reshape(-1, NZ * width), CONTRACT, preferred_element_type=jnp.float32
        )
    late_rows = late.transpose(2, 1, 0, 3).reshape(half, NX * NZ * width)
    late_grad = lax.dot_general(late_rows, w_down, CONTRACT, preferred_element_type=jnp.float32)
    hidden_grad = jnp.concatenate([early_grad, late_grad], axis=0)
    gate_grad = (hidden_grad * up_value * slope).astype(jnp.bfloat16)
    upward_grad = (hidden_grad * activated).astype(jnp.bfloat16)
    gate_part = jnp.dot(gate_grad, proj_gate, preferred_element_type=jnp.float32)
    up_part = jnp.dot(upward_grad, proj_upward, preferred_element_type=jnp.float32)
    paired = jnp.dot(
        left_in, jnp.concatenate([gate_part, up_part], axis=1), precision=lax.Precision.HIGHEST
    )
    sent = jnp.concatenate([paired.reshape(mp_size, 2 * SEQ_DEV, 2 * rank), down_raw], axis=1)
    got = jnp.sum(lax.all_to_all(sent, "mp", 0, 0), axis=0)
    paired, down = got[: 2 * SEQ_DEV], got[2 * SEQ_DEV :]
    paired = paired.reshape(2, SEQ_DEV, 2, rank).transpose(1, 2, 0, 3).reshape(SEQ_DEV, 2, 2 * rank)
    raw = jnp.concatenate([paired, down[:, None]], axis=1)

    squares = jnp.sum(raw * raw, axis=(0, 2))
    squares = jnp.pad(squares, (0, 125)).reshape(1, 1, 128)
    for axis, size in (("mp", mp_size), ("dp", dp_size)):
        squares = jnp.sum(
            lax.all_to_all(jnp.broadcast_to(squares, (size, 1, 128)), axis, 0, 0), axis=0, keepdims=True
        )
    entries = SEQ_DEV * dp_size * rank * rank
    scale = lax.rsqrt(squares[0, 0, :3] / entries + 1e-06)
    return raw * scale[None, :, None]


def solution(mesh):
    in_specs = (
        P("dp", "mp"),
        P("dp", "mp"),
        P("dp", "mp"),
        P("dp", "mp"),
        P("mp", None),
        P("mp", None),
        P("mp", None),
        P("mp", None),
        P("mp", None),
        P(None, "mp"),
        P("dp", None),
    )
    out_specs = P("dp", None, "mp")
    return jax.shard_map(
        per_device, mesh=mesh, in_specs=in_specs, out_specs=out_specs, check_vma=False
    )
```

time: 381 us -> 167 us (0.44)
  waiting for transfers between devices: 250 us -> 16.5 us
  blocking collectives: 99.9 us -> 69.1 us
  starting transfers between devices: 0.04 us -> 25.4 us
  local copies, waits for them, and re-layouts: 1.2 us -> 20.6 us
    psum x1 -> x0, waiting for transfers between devices: 160 us -> none  [per_device(): lax.psum((in_part, hid_part, gate_part, up_part, out_part), 'mp')]
    psum x1 -> x0, blocking collectives: 99.9 us -> none  [per_device(): total_sq = lax.psum(squares, ('dp', 'mp'))]
    all_gather x1, waiting for transfers between devices: 89.2 us -> 0.02 us  [per_device(): late = lax.all_gather(late_x, 'mp', axis=0, axis_index_groups=Z_GROUPS)]
    all_to_all x0 -> x4, blocking collectives: none -> 69.1 us  [the longest x2 40 us: per_device(): lax.all_to_all(jnp.broadcast_to(squares, (size, 1, 128)), axis, 0, 0)]
    all_to_all x0 -> x2, starting transfers between devices: none -> 15.5 us  [the longest x1 11.7 us: per_device(): got = lax.all_to_all(sent, 'mp', 0, 0, axis_index_groups=Z_GROUPS)]
    ppermute x0 -> x3, starting transfers between devices: none -> 9.9 us  [per_device(): lax.ppermute(early_z, 'mp', x_shift(step))]
    all_to_all x0 -> x2, waiting for transfers between devices: none -> 9.48 us  [the longest x1 9.47 us: per_device(): got = lax.all_to_all(sent, 'mp', 0, 0, axis_index_groups=Z_GROUPS)]
    unnamed x14 -> x28, local copies, waits for them, and re-layouts: 0.17 us -> 7.52 us
  transfers between devices with their start and end apart: 2 -> 6, of which waited for: 2 -> 2; matrix products, arithmetic and copies ran while one was open for 1% -> 15% of each run, Pallas kernels for 0% -> 0%
where the time goes in v1:
time: 167 us; the launch traced here: 166 us
  blocking collectives  69.1 us (41%)
  starting transfers between devices  25.4 us (15%)
  local copies, waits for them, and re-layouts  20.6 us (12%)
  matrix products  17 us (10%)
  waiting for transfers between devices  16.5 us (10%)
  between operations  13.8 us (8%)
  other arithmetic  3.24 us (2%)
    all_to_all x2, blocking collectives, per_device(): lax.all_to_all(jnp.broadcast_to(squares, (size, 1, 128)), axis, 0, 0)  40 us
    all_to_all x1, blocking collectives, per_device(): got = jnp.sum(lax.all_to_all(sent, 'mp', 0, 0), axis=0)  17.5 us
    all_to_all x1, starting transfers between devices, per_device(): got = lax.all_to_all(sent, 'mp', 0, 0, axis_index_groups=Z_GROUPS)  11.7 us
    all_to_all x1, blocking collectives, per_device(): got = lax.all_to_all(sent, 'mp', 0, 0, axis_index_groups=X_GROUPS)  11.6 us
    ppermute x3, starting transfers between devices, per_device(): lax.ppermute(early_z, 'mp', x_shift(step))  9.9 us
    all_to_all x1, waiting for transfers between devices, per_device(): got = lax.all_to_all(sent, 'mp', 0, 0, axis_index_groups=Z_GROUPS)  9.47 us
    unnamed x28, local copies, waits for them, and re-layouts  7.52 us
    ppermute x3, waiting for transfers between devices, per_device(): lax.ppermute(early_z, 'mp', x_shift(step))  7.02 us
  transfers between devices with their start and end apart: 6, of which 2 were waited for; matrix products, arithmetic and copies ran while one was open for 15% of the time, Pallas kernels for 0%

profile of v1, /device:TPU:1, one launch (start us, length us, event | category | flops | bytes accessed | tf_op | source)
XLA Modules:
  0.0 165.6 jit_solution(4235466554181982252)
XLA Ops:
  6.5 0.0 copy-start
  6.5 0.0 all-gather.3.cloned.1.call-start
  6.5 0.9 fusion.38
  7.5 1.1 fusion.40
  8.5 0.0 copy-done
  8.6 0.9 fusion.39
  9.4 0.1 reduce-precision_convert_fusion
  9.7 11.6 %all_to_all.30 = bf16[4,512,128]{2,1,0:T(8,128)(2,1)S(1)} all-to-all(bf16[4,512,128]{2,1,0:T(8,128)(2,1)S(1)} %pad_maximum_fusion.2), channel_id=1, replica_groups={{0,8,16,24},{1,9,17,25},{2,10,18,26},{3,11,19,27},{4,12,20,28},{5,13,21..., dimensions={0} | all-to-all | bytes 1048576 | tf_op jit(solution)/shard_map/all_to_all | solution.py:70
  21.3 0.7 slice.66
  22.0 0.0 all-gather.3.cloned.1.call-update
  22.1 0.1 broadcast_in_dim.14
  22.2 0.9 pad_maximum_fusion.1
  23.0 11.7 %all-to-all-start.1 = ((bf16[8,288,128]{2,1,0:T(8,128)(2,1)}), bf16[8,288,128]{2,1,0:T(8,128)(2,1)S(1)}, u32[]{:S(2)}, u32[]{:S(2)}) async-start(bf16[8,288,128]{2,1,0:T(8,128)(2,1)} %pad_maximum_fusion.1), calls=%async_computation.1 | async-start | bytes 1179648 | tf_op jit(solution)/shard_map/all_to_all | solution.py:86
  34.7 0.0 copy-start.8
  34.7 0.0 copy-start.10
  34.7 5.0 %copy.76 = bf16[56,8,32,128]{3,2,1,0:T(8,128)(2,1)} copy(bf16[56,8,32,128]{3,1,2,0:T(8,128)(2,1)} %bitcast.93) | data formatting | bytes 7340032
  39.7 0.0 copy-done.6
  39.7 0.0 copy-done.8
  39.7 0.0 copy-done.10
  39.7 0.4 convolution_bitcast_fusion
  40.1 0.1 mul.76
  40.3 0.0 copy-start.5
  40.3 3.7 %constant_dynamic-slice_fusion.1 = (bf16[448,1,8,128]{3,2,1,0:T(8,128)(2,1)S(1)}, bf16[448,1,8,128]{3,2,1,0:T(8,128)(2,1)}, bf16[448,1,8,128]{3,2,1,0:T(8,128)(2,1)S(1)}, bf16[448,1,8,128]{3,2,1,0:T(8,128)(2,1)}) fusion(bf16[448,4,8,128]{3,2,1,0:T(8,128)(2,1)} %bitcast.88, s32[]{:T(128)S(6)} %select_n.42, s32[]{:T(128)S(6)} %select_n.44, s32[]{:T(128)S(6)} %select_n.40, ...), kind=kLoop, calls=%fused_computation.62 | loop fusion | bytes 7340048 | tf_op jit(solution)/shard_map/jit(dynamic_index_in_dim)/dynamic_slice | solution.py:115
  44.0 0.0 copy-done.5
  44.0 9.5 %all-to-all-done.1 = bf16[8,288,128]{2,1,0:T(8,128)(2,1)S(1)} async-done(((bf16[8,288,128]{2,1,0:T(8,128)(2,1)}), bf16[8,288,128]{2,1,0:T(8,128)(2,1)S(1)}, u32[]{:S(2)}, u32[]{:S(2)}) %all-to-all-start.1) | async-done | bytes 589856 | tf_op jit(solution)/shard_map/all_to_all | solution.py:86
  53.5 0.8 broadcast_in_dim.16
  54.2 0.1 copy-done.1
  54.4 3.9 %all-to-all-start.2 = ((f32[32,16,128]{2,1,0:T(8,128)}), f32[32,16,128]{2,1,0:T(8,128)S(1)}, u32[]{:S(2)}, u32[]{:S(2)}) async-start(f32[32,16,128]{2,1,0:T(8,128)} %broadcast_in_dim.16), calls=%async_computation.2 | async-start | bytes 524288 | tf_op jit(solution)/shard_map/all_to_all | solution.py:94
  58.2 0.1 broadcast_multiply_fusion
  58.4 1.9 %slice.65 = bf16[8,256,128]{2,1,0:T(8,128)(2,1)} slice(bf16[8,288,128]{2,1,0:T(8,128)(2,1)} %copy-done.1), slice={[0:8], [0:256], [0:128]} | slice | bytes 1048576 | tf_op jit(solution)/shard_map/slice | solution.py:87
  60.3 2.1 %copy.74 = bf16[8,256,128]{1,2,0:T(8,128)(2,1)} copy(bf16[8,256,128]{2,1,0:T(8,128)(2,1)} %slice.65) | data formatting | bytes 1048576
  62.3 3.1 %collective-permute-start = (bf16[8,256,128]{1,2,0:T(8,128)(2,1)}, bf16[8,256,128]{1,2,0:T(8,128)(2,1)}, u32[]{:S(2)}, u32[]{:S(2)}) collective-permute-start(bf16[8,256,128]{1,2,0:T(8,128)(2,1)} %copy.74), channel_id=1, source_target_pairs={{0,8},{1,9},{2,10},{3,11},{4,12},{5,13},{6,14},{7,15},{8,16},{9,17... | collective-permute-start | bytes 1572872 | tf_op jit(solution)/shard_map/ppermute | solution.py:92
  65.4 3.4 %collective-permute-start.2 = (bf16[8,256,128]{1,2,0:T(8,128)(2,1)}, bf16[8,256,128]{1,2,0:T(8,128)(2,1)}, u32[]{:S(2)}, u32[]{:S(2)}) collective-permute-start(bf16[8,256,128]{1,2,0:T(8,128)(2,1)} %copy.74), channel_id=1, source_target_pairs={{0,24},{1,25},{2,26},{3,27},{4,28},{5,29},{6,30},{7,31},{8,0},{9,1... | collective-permute-start | bytes 1572872 | tf_op jit(solution)/shard_map/ppermute | solution.py:92
  68.8 3.4 %collective-permute-start.1 = (bf16[8,256,128]{1,2,0:T(8,128)(2,1)}, bf16[8,256,128]{1,2,0:T(8,128)(2,1)}, u32[]{:S(2)}, u32[]{:S(2)}) collective-permute-start(bf16[8,256,128]{1,2,0:T(8,128)(2,1)} %copy.74), channel_id=1, source_target_pairs={{0,16},{1,17},{2,18},{3,19},{4,20},{5,21},{6,22},{7,23},{8,24},{9,... | collective-permute-start | bytes 1572872 | tf_op jit(solution)/shard_map/ppermute | solution.py:92
  72.2 2.5 %fusion.16 = f32[256,448]{0,1:T(8,128)} fusion(bf16[256,1024]{0,1:T(8,128)(2,1)} %bitcast.102, bf16[56,8,8,128]{3,2,1,0:T(8,128)(2,1)} %bitcast.101), kind=kOutput, calls=%fused_computation.24 | convolution fusion | flops 234881024 | bytes 1900544 | tf_op jit(solution)/shard_map/dot_general | solution.py:117
  74.7 0.0 all-to-all-done.2
  74.7 1.3 fusion.20
  76.1 0.8 copy.60
  76.8 0.7 fusion.19
  77.5 1.0 broadcast_multiply_fusion.1
  78.5 0.0 collective-permute-done.2
  78.5 0.0 copy-done.2
  78.6 1.4 fusion.9
  80.0 0.0 collective-permute-done
  80.0 0.0 copy-done.4
  80.0 1.4 convolution_add_fusion.1
  81.5 7.0 %collective-permute-done.1 = bf16[8,256,128]{1,2,0:T(8,128)(2,1)} collective-permute-done((bf16[8,256,128]{1,2,0:T(8,128)(2,1)}, bf16[8,256,128]{1,2,0:T(8,128)(2,1)}, u32[]{:S(2)}, u32[]{:S(2)}) %collective-permute-start.1) | collective-permute-done | bytes 524320 | tf_op jit(solution)/shard_map/ppermute | solution.py:92
  88.5 1.4 fusion
  90.0 0.0 all-gather.3.cloned.1.call-done
  90.0 3.9 %copy.62 = bf16[256,4,8,128]{0,3,2,1:T(8,128)(2,1)} copy(bf16[256,4,8,128]{3,0,1,2:T(8,128)(2,1)} %bitcast.96) | data formatting | bytes 4194304 | tf_op jit(solution)/shard_map/transpose | solution.py:120
  93.9 3.9 %fusion.41 = f32[256,448]{0,1:T(8,128)S(1)} fusion(bf16[448,4096]{1,0:T(8,128)(2,1)} %param.15, bf16[256,4096]{0,1:T(8,128)(2,1)} %bitcast.97), kind=kOutput, calls=%fused_computation.75 | convolution fusion | flops 939524096 | bytes 6225920 | tf_op jit(solution)/shard_map/dot_general | solution.py:121
  97.8 0.0 copy-start.12
  97.8 0.5 fusion.23
  98.4 0.3 copy-done.12
  98.7 0.4 fusion.22
  99.1 1.0 fusion.26
  100.1 0.1 maximum_maximum_fusion
  100.2 17.5 %all_to_all.31 = f32[32,24,128]{2,1,0:T(8,128)S(1)} all-to-all(f32[32,24,128]{2,1,0:T(8,128)S(1)} %maximum_maximum_fusion), channel_id=1, replica_groups=mesh['dp'=16,'mp'=32] {'mp'}, dimensions={0} | all-to-all | bytes 786432 | tf_op jit(solution)/shard_map/all_to_all | solution.py:131
  117.7 0.1 reshape.153
  117.8 0.1 reshape.154
  117.9 0.1 multiply_reduce_fusion
  118.0 13.6 %all_to_all.32 = f32[32,1,128]{2,1,0:T(1,128)S(1)} all-to-all(f32[32,1,128]{2,1,0:T(1,128)S(1)} %broadcast_in_dim.18), channel_id=1, replica_groups=mesh['dp'=16,'mp'=32] {'mp'}, dimensions={0} | all-to-all | bytes 32768 | tf_op jit(solution)/shard_map/all_to_all | solution.py:140
  131.7 26.4 %all_to_all.33 = f32[16,1,128]{2,1,0:T(1,128)S(1)} all-to-all(f32[16,1,128]{2,1,0:T(1,128)S(1)} %broadcast_in_dim.19), channel_id=1, replica_groups=mesh['dp'=16,'mp'=32] {'dp'}, dimensions={0} | all-to-all | bytes 16384 | tf_op jit(solution)/shard_map/all_to_all | solution.py:140
  158.1 0.7 fusion.31
  (30 shorter events, 0.3 us)
Async XLA Ops:
  6.5 2.0 %copy-start = (bf16[512,128]{1,0:T(8,128)(2,1)S(1)}, bf16[512,128]{1,0:T(8,128)(2,1)}, u32[]{:S(2)}) copy-start(bf16[512,128]{1,0:T(8,128)(2,1)} %param.11) | copy-start | bytes 393220
  6.5 83.4 %all-gather.3.cloned.1.call-start = ((), (), s32[]{:S(2)}) async-start(), calls=%async_computation.6 | async-start | bytes 2359296 | tf_op jit(solution)/shard_map/all_gather | solution.py:75
  23.0 30.4 %all-to-all-start.1 = ((bf16[8,288,128]{2,1,0:T(8,128)(2,1)}), bf16[8,288,128]{2,1,0:T(8,128)(2,1)S(1)}, u32[]{:S(2)}, u32[]{:S(2)}) async-start(bf16[8,288,128]{2,1,0:T(8,128)(2,1)} %pad_maximum_fusion.1), calls=%async_computation.1 | async-start | bytes 1179648 | tf_op jit(solution)/shard_map/all_to_all | solution.py:86
  34.7 5.0 %copy-start.6 = (bf16[512,448]{0,1:T(8,128)(2,1)S(1)}, bf16[512,448]{0,1:T(8,128)(2,1)}, u32[]{:S(2)}) copy-start(bf16[512,448]{0,1:T(8,128)(2,1)} %param.13) | copy-start | bytes 1376260
  34.7 5.0 %copy-start.8 = (bf16[512,448]{0,1:T(8,128)(2,1)S(1)}, bf16[512,448]{0,1:T(8,128)(2,1)}, u32[]{:S(2)}) copy-start(bf16[512,448]{0,1:T(8,128)(2,1)} %param.12) | copy-start | bytes 1376260
  34.7 5.0 %copy-start.10 = (bf16[448,64]{0,1:T(8,128)(2,1)S(1)}, bf16[448,64]{0,1:T(8,128)(2,1)}, u32[]{:S(2)}) copy-start(bf16[448,64]{0,1:T(8,128)(2,1)} %param.17) | copy-start | bytes 172036
  40.3 3.7 %copy-start.5 = (s32[1,512]{1,0:T(1,128)S(1)}, s32[1,512]{1,0:T(1,128)}, u32[]{:S(2)}) copy-start(s32[1,512]{1,0:T(1,128)} %param.21) | copy-start | bytes 6148
  53.4 0.9 copy-start.1
  54.4 20.4 %all-to-all-start.2 = ((f32[32,16,128]{2,1,0:T(8,128)}), f32[32,16,128]{2,1,0:T(8,128)S(1)}, u32[]{:S(2)}, u32[]{:S(2)}) async-start(f32[32,16,128]{2,1,0:T(8,128)} %broadcast_in_dim.16), calls=%async_computation.2 | async-start | bytes 524288 | tf_op jit(solution)/shard_map/all_to_all | solution.py:94
  62.3 17.7 %collective-permute-start = (bf16[8,256,128]{1,2,0:T(8,128)(2,1)}, bf16[8,256,128]{1,2,0:T(8,128)(2,1)}, u32[]{:S(2)}, u32[]{:S(2)}) collective-permute-start(bf16[8,256,128]{1,2,0:T(8,128)(2,1)} %copy.74), channel_id=1, source_target_pairs={{0,8},{1,9},{2,10},{3,11},{4,12},{5,13},{6,14},{7,15},{8,16},{9,17... | collective-permute-start | bytes 1572872 | tf_op jit(solution)/shard_map/ppermute | solution.py:92
  65.4 13.2 %collective-permute-start.2 = (bf16[8,256,128]{1,2,0:T(8,128)(2,1)}, bf16[8,256,128]{1,2,0:T(8,128)(2,1)}, u32[]{:S(2)}, u32[]{:S(2)}) collective-permute-start(bf16[8,256,128]{1,2,0:T(8,128)(2,1)} %copy.74), channel_id=1, source_target_pairs={{0,24},{1,25},{2,26},{3,27},{4,28},{5,29},{6,30},{7,31},{8,0},{9,1... | collective-permute-start | bytes 1572872 | tf_op jit(solution)/shard_map/ppermute | solution.py:92
  68.8 19.7 %collective-permute-start.1 = (bf16[8,256,128]{1,2,0:T(8,128)(2,1)}, bf16[8,256,128]{1,2,0:T(8,128)(2,1)}, u32[]{:S(2)}, u32[]{:S(2)}) collective-permute-start(bf16[8,256,128]{1,2,0:T(8,128)(2,1)} %copy.74), channel_id=1, source_target_pairs={{0,16},{1,17},{2,18},{3,19},{4,20},{5,21},{6,22},{7,23},{8,24},{9,... | collective-permute-start | bytes 1572872 | tf_op jit(solution)/shard_map/ppermute | solution.py:92
  76.8 1.7 %copy-start.2 = (bf16[448,1,8,128]{3,2,1,0:T(8,128)(2,1)S(1)}, bf16[448,1,8,128]{3,2,1,0:T(8,128)(2,1)}, u32[]{:S(2)}) copy-start(bf16[448,1,8,128]{3,2,1,0:T(8,128)(2,1)} %get-tuple-element.6) | copy-start | bytes 2752516
  76.8 3.2 %copy-start.4 = (f32[256,448]{0,1:T(8,128)S(1)}, f32[256,448]{0,1:T(8,128)}, u32[]{:S(2)}) copy-start(f32[256,448]{0,1:T(8,128)} %fusion.16) | copy-start | bytes 1376260
  93.9 3.9 %copy-start.7 = (bf16[512,448]{0,1:T(8,128)(2,1)S(1)}, bf16[512,448]{0,1:T(8,128)(2,1)}, u32[]{:S(2)}) copy-start(bf16[512,448]{0,1:T(8,128)(2,1)} %param.13) | copy-start | bytes 1376260
  93.9 3.9 %copy-start.9 = (bf16[512,448]{0,1:T(8,128)(2,1)S(1)}, bf16[512,448]{0,1:T(8,128)(2,1)}, u32[]{:S(2)}) copy-start(bf16[512,448]{0,1:T(8,128)(2,1)} %param.12) | copy-start | bytes 1376260
  93.9 3.9 %copy-start.11 = (bf16[448,64]{0,1:T(8,128)(2,1)S(1)}, bf16[448,64]{0,1:T(8,128)(2,1)}, u32[]{:S(2)}) copy-start(bf16[448,64]{0,1:T(8,128)(2,1)} %param.18) | copy-start | bytes 172036
  97.8 0.8 copy-start.12
  98.7 1.4 copy-start.3
Sparse Core Ops, SparseCore 0:
  22.1 56.3 all-gather.2

commit v2 on v1

--- a/solution.py
+++ b/solution.py
@@ -1,25 +1,68 @@
 import jax
 import jax.numpy as jnp
 from jax import lax
+from jax.experimental import pallas as pl
+from jax.experimental.pallas import tpu as pltpu
 from jax.sharding import PartitionSpec as P
 
 SEQ_DEV = 8
 NX = 4
 NZ = 8
 X_GROUPS = [[x * NZ + z for x in range(NX)] for z in range(NZ)]
-Z_GROUPS = [[x * NZ + z for z in range(NZ)] for x in range(NX)]
 CONTRACT = (((1,), (1,)), ((), ()))
 
 
-def split_hi_lo(value):
-    high = lax.reduce_precision(value, 8, 7)
-    return high.astype(jnp.bfloat16), (value - high).astype(jnp.bfloat16)
+def z_shift(step):
+    return [
+        (x * NZ + z, x * NZ + (z + step) % NZ) for x in range(NX) for z in range(NZ)
+    ]
 
 
-def x_shift(step):
-    return [
-        (x * NZ + z, ((x + step) % NX) * NZ + z) for x in range(NX) for z in range(NZ)
-    ]
+def grad_kernel(pieces, carried, place_ref, *refs):
+    piece_refs, refs = refs[:pieces], refs[pieces:]
+    widths = [piece.shape[0] for piece in piece_refs]
+    w_refs, refs = refs[: sum(widths)], refs[sum(widths) :]
+    rows = jnp.concatenate([piece[i] for piece, n in zip(piece_refs, widths) for i in range(n)], axis=1)
+    weights = jnp.concatenate([w[...] for w in w_refs], axis=1)
+    total = lax.dot_general(rows, weights, CONTRACT, preferred_element_type=jnp.float32)
+    if carried:
+        total = refs[0][...] + total
+    refs[-1][...] = total
+
+
+def add_grad(places, pieces, w_down, carried=None):
+    hidden, _ = w_down.shape
+    tokens, width = pieces[0][0].shape[1:]
+
+    def whole(shape):
+        return pl.BlockSpec(shape, lambda i, place, n=len(shape): (0,) * n)
+
+    specs, w_specs = [], []
+    for k, (block, first) in enumerate(pieces):
+        specs.append(whole(block.shape))
+        for x in range(first, first + block.shape[0]):
+            w_specs.append(
+                pl.BlockSpec((hidden, width), lambda i, place, k=k, x=x: (0, x * NZ + place[k]))
+            )
+    operands = [block for block, _ in pieces] + [w_down] * len(w_specs)
+    specs += w_specs
+    aliases = {}
+    if carried is not None:
+        aliases = {1 + len(operands): 0}
+        operands.append(carried)
+        specs.append(whole((tokens, hidden)))
+    return pl.pallas_call(
+        lambda *refs: grad_kernel(len(pieces), carried is not None, *refs),
+        out_shape=jax.ShapeDtypeStruct((tokens, hidden), jnp.float32),
+        grid_spec=pltpu.PrefetchScalarGridSpec(
+            num_scalar_prefetch=1,
+            grid=(1,),
+            in_specs=specs,
+            out_specs=whole((tokens, hidden)),
+        ),
+        input_output_aliases=aliases,
+        compiler_params=pltpu.CompilerParams(vmem_limit_bytes=32 * 1024 * 1024),
+    )(places, *operands)
 
 
 def hidden_part(gate_pre, up_pre):
@@ -45,52 +88,31 @@
     seq_ids,
 ):
     tokens, width = out_grad.shape
-    half = tokens // 2
     rank = proj_input.shape[1]
     mp_size = lax.axis_size("mp")
     dp_size = lax.axis_size("dp")
     own_tokens = tokens // mp_size
     position = lax.axis_index("mp")
-    x_pos = position // NZ
+    z_pos = position % NZ
 
     in_part = jnp.dot(layer_input, proj_input, preferred_element_type=jnp.float32)
     out_part = lax.dot_general(out_grad, proj_output, CONTRACT, preferred_element_type=jnp.float32)
     both = jnp.concatenate([in_part, out_part], axis=1)
 
-    high, low = split_hi_lo(both)
-    share = tokens // NX
-    sent = jnp.concatenate(
-        [
-            jnp.broadcast_to(out_grad[None, half:], (NX, half, width)),
-            high.reshape(NX, share, 2 * rank),
-            low.reshape(NX, share, 2 * rank),
-        ],
-        axis=1,
+    across_x = lax.all_to_all(
+        jnp.broadcast_to(out_grad[None], (NX, tokens, width)), "mp", 0, 0, axis_index_groups=X_GROUPS
     )
-    got = lax.all_to_all(sent, "mp", 0, 0, axis_index_groups=X_GROUPS)
-    late_x = got[:, :half]
-    both = jnp.sum(
-        got[:, half : half + share].astype(jnp.float32) + got[:, half + share :].astype(jnp.float32), axis=0
-    )
-    late = lax.all_gather(late_x, "mp", axis=0, axis_index_groups=Z_GROUPS)
+    blocks = {0: across_x}
+    for step in range(1, NZ // 2):
+        blocks[step] = lax.ppermute(blocks[step - 1], "mp", z_shift(1))
+        blocks[-step] = lax.ppermute(blocks[1 - step], "mp", z_shift(-1))
+    far = NZ // 2
+    far_pieces = [
+        (lax.ppermute(blocks[far - 1][: NX // 2], "mp", z_shift(1)), 0),
+        (lax.ppermute(blocks[1 - far][NX // 2 :], "mp", z_shift(-1)), NX // 2),
+    ]
 
-    high, low = split_hi_lo(both)
-    sent = jnp.concatenate(
-        [
-            jnp.broadcast_to(out_grad[None, :half], (NZ, half, width)),
-            high.reshape(NZ, own_tokens, 2 * rank),
-            low.reshape(NZ, own_tokens, 2 * rank),
-        ],
-        axis=1,
-    )
-    got = lax.all_to_all(sent, "mp", 0, 0, axis_index_groups=Z_GROUPS)
-    early_z = got[:, :half]
-    both = jnp.sum(
-        got[:, half : half + own_tokens].astype(jnp.float32) + got[:, half + own_tokens :].astype(jnp.float32),
-        axis=0,
-    )
-    early = [early_z] + [lax.ppermute(early_z, "mp", x_shift(step)) for step in range(1, NX)]
-
+    both = lax.all_to_all(both.reshape(mp_size, own_tokens, 2 * rank), "mp", 0, 0).sum(axis=0)
     both = lax.all_to_all(jnp.broadcast_to(both[None], (mp_size, own_tokens, 2 * rank)), "mp", 0, 0)
     both = both.reshape(tokens, 2 * rank)
     in_factor, out_factor = both[:, :rank], both[:, rank:]
@@ -109,17 +131,15 @@
     ]
     down_raw = jnp.concatenate(down_raw, axis=2)
 
-    w_blocks = w_down.reshape(w_down.shape[0], NX, NZ, width)
-    early_grad = 0.0
-    for step in range(NX):
-        w_step = lax.dynamic_index_in_dim(w_blocks, (x_pos - step) % NX, 1, keepdims=False)
-        rows = early[step].transpose(1, 0, 2).reshape(half, NZ * width)
-        early_grad += lax.dot_general(
-            rows, w_step.reshape(-1, NZ * width), CONTRACT, preferred_element_type=jnp.float32
+    def places(*steps):
+        return jnp.stack([(z_pos - step) % NZ for step in steps]).astype(jnp.int32)
+
+    hidden_grad = add_grad(places(0), [(blocks[0], 0)], w_down)
+    for step in range(1, far):
+        hidden_grad = add_grad(
+            places(step, -step), [(blocks[step], 0), (blocks[-step], 0)], w_down, hidden_grad
         )
-    late_rows = late.transpose(2, 1, 0, 3).reshape(half, NX * NZ * width)
-    late_grad = lax.dot_general(late_rows, w_down, CONTRACT, preferred_element_type=jnp.float32)
-    hidden_grad = jnp.concatenate([early_grad, late_grad], axis=0)
+    hidden_grad = add_grad(places(far, far), far_pieces, w_down, hidden_grad)
     gate_grad = (hidden_grad * up_value * slope).astype(jnp.bfloat16)
     upward_grad = (hidden_grad * activated).astype(jnp.bfloat16)
     gate_part = jnp.dot(gate_grad, proj_gate, preferred_element_type=jnp.float32)

time: 167 us -> 146 us (0.87)
  starting transfers between devices: 25.4 us -> 51.5 us
  blocking collectives: 69.1 us -> 55.2 us
  between operations: 13.8 us -> 0.52 us
  waiting for transfers between devices: 16.5 us -> 7.46 us
  local copies, waits for them, and re-layouts: 20.6 us -> 11.7 us
  matrix products: 17 us -> 9.1 us
  Pallas kernels: 0 us -> 6.93 us
    ppermute x3 -> x8, starting transfers between devices: 9.9 us -> 34.5 us  [the longest x3 18.1 us: per_device(): blocks[-step] = lax.ppermute(blocks[1 - step], 'mp', z_shift(-1))]
    all_to_all x1 -> x0, blocking collectives: 11.6 us -> none  [per_device(): got = lax.all_to_all(sent, 'mp', 0, 0, axis_index_groups=X_GROUPS)]
    dot_general x5 -> x2, matrix products: 10.7 us -> 1.95 us  [the longest x1 1.07 us: per_device(): lax.dot_general(out_grad, proj_output, CONTRACT, preferred_element_type=j...]
    pallas_call x0 -> x5, Pallas kernels: none -> 6.93 us  [add_grad(): pl.pallas_call(lambda *refs: grad_kernel(len(pieces), carried is not None...]
    ppermute x3 -> x8, waiting for transfers between devices: 7.02 us -> 2.48 us  [the longest x3 2.29 us: per_device(): blocks[step] = lax.ppermute(blocks[step - 1], 'mp', z_shift(1))]
    all_to_all x1 -> x2, waiting for transfers between devices: 9.47 us -> 4.97 us  [the longest x1 4.97 us: per_device(): lax.all_to_all(jnp.broadcast_to(out_grad[None], (NX, tokens, width)), 'mp...]
    transpose x1 -> x0, local copies, waits for them, and re-layouts: 3.91 us -> none  [per_device(): late_rows = late.transpose(2, 1, 0, 3).reshape(half, NX * NZ * width)]
    dynamic_slice x1 -> x0, local copies, waits for them, and re-layouts: 3.67 us -> none  [per_device(): lax.dynamic_index_in_dim(w_blocks, (x_pos - step) % NX, 1, keepdims=False)]
  transfers between devices with their start and end apart: 6 -> 11, of which waited for: 2 -> 5; matrix products, arithmetic and copies ran while one was open for 15% -> 8% of each run, Pallas kernels for 0% -> 4%
where the time goes in v2:
time: 146 us; the launch traced here: 145 us
  blocking collectives  55.2 us (38%)
  starting transfers between devices  51.5 us (35%)
  local copies, waits for them, and re-layouts  11.7 us (8%)
  matrix products  9.1 us (6%)
  waiting for transfers between devices  7.46 us (5%)
  Pallas kernels  6.93 us (5%)
  other arithmetic  2.57 us (2%)
    all_to_all x2, blocking collectives, per_device(): lax.all_to_all(jnp.broadcast_to(squares, (size, 1, 128)), axis, 0, 0)  36.8 us
    all_to_all x1, blocking collectives, per_device(): got = jnp.sum(lax.all_to_all(sent, 'mp', 0, 0), axis=0)  18.4 us
    ppermute x3, starting transfers between devices, per_device(): blocks[-step] = lax.ppermute(blocks[1 - step], 'mp', z_shift(-1))  18.1 us
    ppermute x3, starting transfers between devices, per_device(): blocks[step] = lax.ppermute(blocks[step - 1], 'mp', z_shift(1))  9.89 us
    all_to_all x1, starting transfers between devices, per_device(): lax.all_to_all(jnp.broadcast_to(both[None], (mp_size, own_tokens, 2 * ran...  7.25 us
    pallas_call x5, Pallas kernels, add_grad(): pl.pallas_call(lambda *refs: grad_kernel(len(pieces), carried is not None...  6.93 us
    unnamed x42, local copies, waits for them, and re-layouts  6.46 us
    all_to_all x1, waiting for transfers between devices, per_device(): lax.all_to_all(jnp.broadcast_to(out_grad[None], (NX, tokens, width)), 'mp...  4.97 us
  transfers between devices with their start and end apart: 11, of which 5 were waited for; matrix products, arithmetic and copies ran while one was open for 8% of the time, Pallas kernels for 4%

profile of v2, /device:TPU:1, one launch (start us, length us, event | category | flops | bytes accessed | tf_op | source)
XLA Modules:
  0.0 144.9 jit_solution(17818023149196711856)
XLA Ops:
  0.0 1.9 %broadcast_in_dim.13 = bf16[4,512,128]{2,1,0:T(8,128)(2,1)} broadcast(bf16[512,128]{1,0:T(8,128)(2,1)} %param.14), dimensions={1,2} | broadcast | bytes 655360 | tf_op jit(solution)/shard_map/broadcast_in_dim | solution.py:103
  1.9 4.8 %all-to-all-start.2 = ((bf16[4,512,128]{2,1,0:T(8,128)(2,1)}), bf16[4,512,128]{2,1,0:T(8,128)(2,1)S(1)}, u32[]{:S(2)}, u32[]{:S(2)}) async-start(bf16[4,512,128]{2,1,0:T(8,128)(2,1)} %broadcast_in_dim.13), calls=%async_computation.2 | async-start | bytes 1048576 | tf_op jit(solution)/shard_map/all_to_all | solution.py:102
  6.7 1.1 fusion.24
  7.8 0.9 fusion.23
  8.7 5.0 %all-to-all-done.2.refs_1_ = bf16[4,512,128]{2,1,0:T(8,128)(2,1)S(1)} async-done(((bf16[4,512,128]{2,1,0:T(8,128)(2,1)}), bf16[4,512,128]{2,1,0:T(8,128)(2,1)S(1)}, u32[]{:S(2)}, u32[]{:S(2)}) %all-to-all-start.2) | async-done | bytes 524320 | tf_op jit(solution)/shard_map/all_to_all | solution.py:102
  13.7 5.3 %collective-permute-start = (bf16[4,512,128]{2,1,0:T(8,128)(2,1)S(1)}, bf16[4,512,128]{2,1,0:T(8,128)(2,1)S(1)}, u32[]{:S(2)}, u32[]{:S(2)}) collective-permute-start(bf16[4,512,128]{2,1,0:T(8,128)(2,1)S(1)} %all-to-all-done.2.refs_1_), channel_id=1, source_target_pairs={{0,1},{1,2},{2,3},{3,4},{4,5},{5,6},{6,7},{7,0},{8,9},{9,10},{10,1... | collective-permute-start | bytes 1572872 | tf_op jit(solution)/shard_map/ppermute | solution.py:107
  19.0 8.6 %collective-permute-start.4 = (bf16[4,512,128]{2,1,0:T(8,128)(2,1)S(1)}, bf16[4,512,128]{2,1,0:T(8,128)(2,1)S(1)}, u32[]{:S(2)}, u32[]{:S(2)}) collective-permute-start(bf16[4,512,128]{2,1,0:T(8,128)(2,1)S(1)} %all-to-all-done.2.refs_1_), channel_id=1, source_target_pairs={{0,7},{1,0},{2,1},{3,2},{4,3},{5,4},{6,5},{7,6},{8,15},{9,8},{10,9... | collective-permute-start | bytes 1572872 | tf_op jit(solution)/shard_map/ppermute | solution.py:108
  27.6 0.8 copy.35
  28.5 4.9 %all-to-all-start = ((f32[32,16,128]{2,1,0:T(8,128)}), f32[32,16,128]{2,1,0:T(8,128)S(1)}, u32[]{:S(2)}, u32[]{:S(2)}) async-start(f32[32,16,128]{2,1,0:T(8,128)} %bitcast), calls=%async_computation | async-start | bytes 524288 | tf_op jit(solution)/shard_map/all_to_all | solution.py:115
  33.4 0.2 copy.38
  33.6 0.2 copy.37
  33.9 0.5 convolution_bitcast_fusion
  34.4 1.4 collective-permute-done.refs_1_
  35.7 1.9 %collective-permute-start.1 = (bf16[4,512,128]{2,1,0:T(8,128)(2,1)S(1)}, bf16[4,512,128]{2,1,0:T(8,128)(2,1)}, u32[]{:S(2)}, u32[]{:S(2)}) collective-permute-start(bf16[4,512,128]{2,1,0:T(8,128)(2,1)S(1)} %collective-permute-done.refs_1_), channel_id=1, source_target_pairs={{0,1},{1,2},{2,3},{3,4},{4,5},{5,6},{6,7},{7,0},{8,9},{9,10},{10,1... | collective-permute-start | bytes 1572872 | tf_op jit(solution)/shard_map/ppermute | solution.py:107
  37.7 0.2 collective-permute-done.4.refs_2_
  37.8 5.7 %collective-permute-start.5 = (bf16[4,512,128]{2,1,0:T(8,128)(2,1)S(1)}, bf16[4,512,128]{2,1,0:T(8,128)(2,1)}, u32[]{:S(2)}, u32[]{:S(2)}) collective-permute-start(bf16[4,512,128]{2,1,0:T(8,128)(2,1)S(1)} %collective-permute-done.4.refs_2_), channel_id=1, source_target_pairs={{0,7},{1,0},{2,1},{3,2},{4,3},{5,4},{6,5},{7,6},{8,15},{9,8},{10,9... | collective-permute-start | bytes 1572872 | tf_op jit(solution)/shard_map/ppermute | solution.py:108
  43.6 0.1 pad_add_fusion.refs_0_
  43.6 0.0 all-to-all-done
  43.7 0.7 broadcast_in_dim.12
  44.4 7.3 %all-to-all-start.1 = ((f32[32,16,128]{2,1,0:T(8,128)}), f32[32,16,128]{2,1,0:T(8,128)S(1)}, u32[]{:S(2)}, u32[]{:S(2)}) async-start(f32[32,16,128]{2,1,0:T(8,128)} %broadcast_in_dim.12), calls=%async_computation.1 | async-start | bytes 524288 | tf_op jit(solution)/shard_map/all_to_all | solution.py:116
  51.7 0.1 pad_add_fusion.3.refs_0_
  51.7 0.1 mul.76
  51.9 0.1 pad_add_fusion.2.refs_0_
  52.0 1.1 broadcast_multiply_fusion
  53.1 0.5 collective-permute-done.1.refs_1_
  53.6 2.7 %collective-permute-start.2 = (bf16[4,512,128]{2,1,0:T(8,128)(2,1)}, bf16[4,512,128]{2,1,0:T(8,128)(2,1)S(1)}, u32[]{:S(2)}, u32[]{:S(2)}) collective-permute-start(bf16[4,512,128]{2,1,0:T(8,128)(2,1)} %collective-permute-done.1.refs_1_), channel_id=1, source_target_pairs={{0,1},{1,2},{2,3},{3,4},{4,5},{5,6},{6,7},{7,0},{8,9},{9,10},{10,1... | collective-permute-start | bytes 1572872 | tf_op jit(solution)/shard_map/ppermute | solution.py:107
  56.2 0.0 collective-permute-done.5.refs_2_
  56.3 3.8 %collective-permute-start.6 = (bf16[4,512,128]{2,1,0:T(8,128)(2,1)}, bf16[4,512,128]{2,1,0:T(8,128)(2,1)S(1)}, u32[]{:S(2)}, u32[]{:S(2)}) collective-permute-start(bf16[4,512,128]{2,1,0:T(8,128)(2,1)} %collective-permute-done.5.refs_2_), channel_id=1, source_target_pairs={{0,7},{1,0},{2,1},{3,2},{4,3},{5,4},{6,5},{7,6},{8,15},{9,8},{10,9... | collective-permute-start | bytes 1572872 | tf_op jit(solution)/shard_map/ppermute | solution.py:108
  60.1 0.1 pad_add_fusion.1.refs_0_
  60.2 2.0 %copy-done.1 = bf16[448,4096]{1,0:T(8,128)(2,1)S(1)} copy-done((bf16[448,4096]{1,0:T(8,128)(2,1)S(1)}, bf16[448,4096]{1,0:T(8,128)(2,1)}, u32[]{:S(2)}) %copy-start.1) | copy-done | bytes 3670040
  62.2 0.5 shard_map.112.refs_11_
  62.7 1.5 %copy-done.2 = bf16[448,4096]{1,0:T(8,128)(2,1)S(1)} copy-done((bf16[448,4096]{1,0:T(8,128)(2,1)S(1)}, bf16[448,4096]{1,0:T(8,128)(2,1)}, u32[]{:S(2)}) %copy-start.2) | copy-done | bytes 3670040
  64.2 0.1 copy-done.5
  64.4 1.4 shard_map.113.refs_11_
  65.8 0.0 all-to-all-done.1
  65.8 2.4 %fusion.10 = f32[32,8,64]{2,1,0:T(8,128)} fusion(f32[32,2,8,512]{3,2,0,1:T(8,128)} %broadcast_multiply_fusion, f32[512,128]{1,0:T(8,128)S(1)} %bitcast.49), kind=kOutput, calls=%fused_computation.17 | convolution fusion | flops 100663296 | bytes 851968 | tf_op jit(solution)/shard_map/dot_general | solution.py:127
  68.1 2.3 %fusion.11 = f32[32,8,64]{2,1,0:T(8,128)} fusion(f32[32,2,8,512]{3,2,0,1:T(8,128)} %broadcast_multiply_fusion, f32[512,128]{1,0:T(8,128)S(1)} %bitcast.50), kind=kOutput, calls=%fused_computation.19 | convolution fusion | flops 100663296 | bytes 851968 | tf_op jit(solution)/shard_map/dot_general | solution.py:127
  70.5 0.4 collective-permute-done.2.refs_1_
  70.9 0.7 slice.37
  71.6 1.9 %collective-permute-start.3 = (bf16[2,512,128]{2,1,0:T(8,128)(2,1)}, bf16[2,512,128]{2,1,0:T(8,128)(2,1)S(1)}, u32[]{:S(2)}, u32[]{:S(2)}) collective-permute-start(bf16[2,512,128]{2,1,0:T(8,128)(2,1)} %slice.37), channel_id=1, source_target_pairs={{0,1},{1,2},{2,3},{3,4},{4,5},{5,6},{6,7},{7,0},{8,9},{9,10},{10,1... | collective-permute-start | bytes 786440 | tf_op jit(solution)/shard_map/ppermute | solution.py:111
  73.5 0.0 collective-permute-done.6.refs_2_
  73.5 0.7 slice.38
  74.3 4.6 %collective-permute-start.7 = (bf16[2,512,128]{2,1,0:T(8,128)(2,1)}, bf16[2,512,128]{2,1,0:T(8,128)(2,1)S(1)}, u32[]{:S(2)}, u32[]{:S(2)}) collective-permute-start(bf16[2,512,128]{2,1,0:T(8,128)(2,1)} %slice.38), channel_id=1, source_target_pairs={{0,7},{1,0},{2,1},{3,2},{4,3},{5,4},{6,5},{7,6},{8,15},{9,8},{10,9... | collective-permute-start | bytes 786440 | tf_op jit(solution)/shard_map/ppermute | solution.py:112
  78.9 0.1 copy.36
  79.0 0.1 broadcast_multiply_fusion.1
  79.1 0.0 copy-start.3
  79.1 2.0 %copy-done.3 = bf16[448,4096]{1,0:T(8,128)(2,1)S(1)} copy-done((bf16[448,4096]{1,0:T(8,128)(2,1)S(1)}, bf16[448,4096]{1,0:T(8,128)(2,1)}, u32[]{:S(2)}) %copy-start.3) | copy-done | bytes 3670040
  81.2 2.5 %shard_map.114.refs_11_ = f32[512,448]{1,0:T(8,128)S(1)} custom-call(s32[2]{0:T(128)S(1)} %pad_add_fusion.2.refs_0_, bf16[4,512,128]{2,1,0:T(8,128)(2,1)} %collective-permute-done.1.refs_1_, bf16[4,512,128]{2,1,0:T(8,128)(2,1)} %collective-permute-done.5.refs_2_, bf16[448,4096]{1,0:T(8,128)(2,1)S(1)} %copy-done.3, ...), custom_call_target="tpu_custom_call", output_to_operand_aliasing={{}: (11, {})} | custom-call | tf_op jit(solution)/shard_map/pallas_call | solution.py:54
  83.7 1.4 shard_map.115.refs_7_
  85.1 0.0 copy-start.18
  85.1 1.1 shard_map.116
  86.2 0.0 copy-done.11
  86.3 0.6 fusion.12
  86.9 0.3 copy-done.19
  87.1 0.4 fusion.8
  87.6 1.0 fusion.14
  88.6 0.1 maximum_maximum_fusion
  88.7 18.4 %all_to_all.30 = f32[32,24,128]{2,1,0:T(8,128)S(1)} all-to-all(f32[32,24,128]{2,1,0:T(8,128)S(1)} %maximum_maximum_fusion), channel_id=1, replica_groups=mesh['dp'=16,'mp'=32] {'mp'}, dimensions={0} | all-to-all | bytes 786432 | tf_op jit(solution)/shard_map/all_to_all | solution.py:151
  107.1 0.1 reshape.102
  107.2 0.1 reshape.103
  107.3 0.1 multiply_reduce_fusion
  107.4 13.7 %all_to_all.31 = f32[32,1,128]{2,1,0:T(1,128)S(1)} all-to-all(f32[32,1,128]{2,1,0:T(1,128)S(1)} %broadcast_in_dim.15), channel_id=1, replica_groups=mesh['dp'=16,'mp'=32] {'mp'}, dimensions={0} | all-to-all | bytes 32768 | tf_op jit(solution)/shard_map/all_to_all | solution.py:160
  121.1 23.1 %all_to_all.32 = f32[16,1,128]{2,1,0:T(1,128)S(1)} all-to-all(f32[16,1,128]{2,1,0:T(1,128)S(1)} %broadcast_in_dim.16), channel_id=1, replica_groups=mesh['dp'=16,'mp'=32] {'dp'}, dimensions={0} | all-to-all | bytes 16384 | tf_op jit(solution)/shard_map/all_to_all | solution.py:160
  144.3 0.7 fusion.18
  (49 shorter events, 0.3 us)
Async XLA Ops:
  0.0 7.8 %copy-start = (bf16[512,128]{1,0:T(8,128)(2,1)S(1)}, bf16[512,128]{1,0:T(8,128)(2,1)}, u32[]{:S(2)}) copy-start(bf16[512,128]{1,0:T(8,128)(2,1)} %param.11) | copy-start | bytes 393220
  0.0 33.4 %copy-start.12 = (bf16[512,448]{0,1:T(8,128)(2,1)S(1)}, bf16[512,448]{0,1:T(8,128)(2,1)}, u32[]{:S(2)}) copy-start(bf16[512,448]{0,1:T(8,128)(2,1)} %param.12) | copy-start | bytes 1376260
  0.0 33.6 %copy-start.13 = (bf16[512,448]{0,1:T(8,128)(2,1)S(1)}, bf16[512,448]{0,1:T(8,128)(2,1)}, u32[]{:S(2)}) copy-start(bf16[512,448]{0,1:T(8,128)(2,1)} %param.13) | copy-start | bytes 1376260
  0.0 33.9 %copy-start.16 = (s32[1,512]{1,0:T(1,128)S(1)}, s32[1,512]{1,0:T(1,128)}, u32[]{:S(2)}) copy-start(s32[1,512]{1,0:T(1,128)} %param.21) | copy-start | bytes 6148
  0.0 33.9 %copy-start.17 = (bf16[448,64]{0,1:T(8,128)(2,1)S(1)}, bf16[448,64]{0,1:T(8,128)(2,1)}, u32[]{:S(2)}) copy-start(bf16[448,64]{0,1:T(8,128)(2,1)} %param.17) | copy-start | bytes 172036
  1.9 11.8 %all-to-all-start.2 = ((bf16[4,512,128]{2,1,0:T(8,128)(2,1)}), bf16[4,512,128]{2,1,0:T(8,128)(2,1)S(1)}, u32[]{:S(2)}, u32[]{:S(2)}) async-start(bf16[4,512,128]{2,1,0:T(8,128)(2,1)} %broadcast_in_dim.13), calls=%async_computation.2 | async-start | bytes 1048576 | tf_op jit(solution)/shard_map/all_to_all | solution.py:102
  13.7 22.1 %collective-permute-start = (bf16[4,512,128]{2,1,0:T(8,128)(2,1)S(1)}, bf16[4,512,128]{2,1,0:T(8,128)(2,1)S(1)}, u32[]{:S(2)}, u32[]{:S(2)}) collective-permute-start(bf16[4,512,128]{2,1,0:T(8,128)(2,1)S(1)} %all-to-all-done.2.refs_1_), channel_id=1, source_target_pairs={{0,1},{1,2},{2,3},{3,4},{4,5},{5,6},{6,7},{7,0},{8,9},{9,10},{10,1... | collective-permute-start | bytes 1572872 | tf_op jit(solution)/shard_map/ppermute | solution.py:107
  19.0 18.8 %collective-permute-start.4 = (bf16[4,512,128]{2,1,0:T(8,128)(2,1)S(1)}, bf16[4,512,128]{2,1,0:T(8,128)(2,1)S(1)}, u32[]{:S(2)}, u32[]{:S(2)}) collective-permute-start(bf16[4,512,128]{2,1,0:T(8,128)(2,1)S(1)} %all-to-all-done.2.refs_1_), channel_id=1, source_target_pairs={{0,7},{1,0},{2,1},{3,2},{4,3},{5,4},{6,5},{7,6},{8,15},{9,8},{10,9... | collective-permute-start | bytes 1572872 | tf_op jit(solution)/shard_map/ppermute | solution.py:108
  28.5 15.2 %all-to-all-start = ((f32[32,16,128]{2,1,0:T(8,128)}), f32[32,16,128]{2,1,0:T(8,128)S(1)}, u32[]{:S(2)}, u32[]{:S(2)}) async-start(f32[32,16,128]{2,1,0:T(8,128)} %bitcast), calls=%async_computation | async-start | bytes 524288 | tf_op jit(solution)/shard_map/all_to_all | solution.py:115
  33.6 10.8 %copy-start.8 = (bf16[512,448]{1,0:T(8,128)(2,1)}, bf16[512,448]{1,0:T(8,128)(2,1)S(1)}, u32[]{:S(2)}) copy-start(bf16[512,448]{1,0:T(8,128)(2,1)S(1)} %copy.38) | copy-start | bytes 1376260
  33.8 19.2 %copy-start.10 = (bf16[512,448]{1,0:T(8,128)(2,1)}, bf16[512,448]{1,0:T(8,128)(2,1)S(1)}, u32[]{:S(2)}) copy-start(bf16[512,448]{1,0:T(8,128)(2,1)S(1)} %copy.37) | copy-start | bytes 1376260
  33.9 19.2 %copy-start.14 = (f32[8,512]{1,0:T(8,128)}, f32[8,512]{1,0:T(8,128)S(1)}, u32[]{:S(2)}) copy-start(f32[8,512]{1,0:T(8,128)S(1)} %fusion.17) | copy-start | bytes 49156
  35.7 17.8 %collective-permute-start.1 = (bf16[4,512,128]{2,1,0:T(8,128)(2,1)S(1)}, bf16[4,512,128]{2,1,0:T(8,128)(2,1)}, u32[]{:S(2)}, u32[]{:S(2)}) collective-permute-start(bf16[4,512,128]{2,1,0:T(8,128)(2,1)S(1)} %collective-permute-done.refs_1_), channel_id=1, source_target_pairs={{0,1},{1,2},{2,3},{3,4},{4,5},{5,6},{6,7},{7,0},{8,9},{9,10},{10,1... | collective-permute-start | bytes 1572872 | tf_op jit(solution)/shard_map/ppermute | solution.py:107
  37.8 18.4 %copy-start.4 = (bf16[4,512,128]{2,1,0:T(8,128)(2,1)}, bf16[4,512,128]{2,1,0:T(8,128)(2,1)S(1)}, u32[]{:S(2)}) copy-start(bf16[4,512,128]{2,1,0:T(8,128)(2,1)S(1)} %collective-permute-done.4.refs_2_) | copy-start | bytes 1572868
  37.8 18.4 %collective-permute-start.5 = (bf16[4,512,128]{2,1,0:T(8,128)(2,1)S(1)}, bf16[4,512,128]{2,1,0:T(8,128)(2,1)}, u32[]{:S(2)}, u32[]{:S(2)}) collective-permute-start(bf16[4,512,128]{2,1,0:T(8,128)(2,1)S(1)} %collective-permute-done.4.refs_2_), channel_id=1, source_target_pairs={{0,7},{1,0},{2,1},{3,2},{4,3},{5,4},{6,5},{7,6},{8,15},{9,8},{10,9... | collective-permute-start | bytes 1572872 | tf_op jit(solution)/shard_map/ppermute | solution.py:108
  44.4 21.4 %all-to-all-start.1 = ((f32[32,16,128]{2,1,0:T(8,128)}), f32[32,16,128]{2,1,0:T(8,128)S(1)}, u32[]{:S(2)}, u32[]{:S(2)}) async-start(f32[32,16,128]{2,1,0:T(8,128)} %broadcast_in_dim.12), calls=%async_computation.1 | async-start | bytes 524288 | tf_op jit(solution)/shard_map/all_to_all | solution.py:116
  53.6 17.3 %collective-permute-start.2 = (bf16[4,512,128]{2,1,0:T(8,128)(2,1)}, bf16[4,512,128]{2,1,0:T(8,128)(2,1)S(1)}, u32[]{:S(2)}, u32[]{:S(2)}) collective-permute-start(bf16[4,512,128]{2,1,0:T(8,128)(2,1)} %collective-permute-done.1.refs_1_), channel_id=1, source_target_pairs={{0,1},{1,2},{2,3},{3,4},{4,5},{5,6},{6,7},{7,0},{8,9},{9,10},{10,1... | collective-permute-start | bytes 1572872 | tf_op jit(solution)/shard_map/ppermute | solution.py:107
  56.3 17.3 %collective-permute-start.6 = (bf16[4,512,128]{2,1,0:T(8,128)(2,1)}, bf16[4,512,128]{2,1,0:T(8,128)(2,1)S(1)}, u32[]{:S(2)}, u32[]{:S(2)}) collective-permute-start(bf16[4,512,128]{2,1,0:T(8,128)(2,1)} %collective-permute-done.5.refs_2_), channel_id=1, source_target_pairs={{0,7},{1,0},{2,1},{3,2},{4,3},{5,4},{6,5},{7,6},{8,15},{9,8},{10,9... | collective-permute-start | bytes 1572872 | tf_op jit(solution)/shard_map/ppermute | solution.py:108
  60.2 2.0 %copy-start.1 = (bf16[448,4096]{1,0:T(8,128)(2,1)S(1)}, bf16[448,4096]{1,0:T(8,128)(2,1)}, u32[]{:S(2)}) copy-start(bf16[448,4096]{1,0:T(8,128)(2,1)} %refs_6_.7) | copy-start | bytes 11010052
  62.2 2.0 %copy-start.2 = (bf16[448,4096]{1,0:T(8,128)(2,1)S(1)}, bf16[448,4096]{1,0:T(8,128)(2,1)}, u32[]{:S(2)}) copy-start(bf16[448,4096]{1,0:T(8,128)(2,1)} %refs_6_.7) | copy-start | bytes 11010052
  62.2 2.1 %copy-start.5 = (bf16[4,512,128]{2,1,0:T(8,128)(2,1)S(1)}, bf16[4,512,128]{2,1,0:T(8,128)(2,1)}, u32[]{:S(2)}) copy-start(bf16[4,512,128]{2,1,0:T(8,128)(2,1)} %copy-done.4) | copy-start | bytes 1572868
  65.8 13.2 %copy-start.15 = (f32[8,512]{1,0:T(8,128)S(1)}, f32[8,512]{1,0:T(8,128)}, u32[]{:S(2)}) copy-start(f32[8,512]{1,0:T(8,128)} %copy-done.14) | copy-start | bytes 49156
  71.6 13.5 %collective-permute-start.3 = (bf16[2,512,128]{2,1,0:T(8,128)(2,1)}, bf16[2,512,128]{2,1,0:T(8,128)(2,1)S(1)}, u32[]{:S(2)}, u32[]{:S(2)}) collective-permute-start(bf16[2,512,128]{2,1,0:T(8,128)(2,1)} %slice.37), channel_id=1, source_target_pairs={{0,1},{1,2},{2,3},{3,4},{4,5},{5,6},{6,7},{7,0},{8,9},{9,10},{10,1... | collective-permute-start | bytes 786440 | tf_op jit(solution)/shard_map/ppermute | solution.py:111
  74.3 10.9 %collective-permute-start.7 = (bf16[2,512,128]{2,1,0:T(8,128)(2,1)}, bf16[2,512,128]{2,1,0:T(8,128)(2,1)S(1)}, u32[]{:S(2)}, u32[]{:S(2)}) collective-permute-start(bf16[2,512,128]{2,1,0:T(8,128)(2,1)} %slice.38), channel_id=1, source_target_pairs={{0,7},{1,0},{2,1},{3,2},{4,3},{5,4},{6,5},{7,6},{8,15},{9,8},{10,9... | collective-permute-start | bytes 786440 | tf_op jit(solution)/shard_map/ppermute | solution.py:112
  79.1 2.0 %copy-start.3 = (bf16[448,4096]{1,0:T(8,128)(2,1)S(1)}, bf16[448,4096]{1,0:T(8,128)(2,1)}, u32[]{:S(2)}) copy-start(bf16[448,4096]{1,0:T(8,128)(2,1)} %refs_6_.7) | copy-start | bytes 11010052
  85.1 1.2 copy-start.9
  85.1 1.2 copy-start.11
  85.1 1.2 copy-start.18
  86.3 0.8 copy-start.19
  87.1 1.4 copy-start.6
  87.1 1.4 copy-start.7

commit v3 on v0

v3 whole, which is shorter than its diff:
```python
import jax
import jax.numpy as jnp
from jax import lax
from jax.experimental import pallas as pl
from jax.experimental.pallas import tpu as pltpu
from jax.sharding import PartitionSpec as P

SEQ_DEV = 8
NX = 4
NZ = 8
RING = [(0,), (1, -1), (2, -2), (3, -3), (4,)]
X_GROUPS = [[x * NZ + z for x in range(NX)] for z in range(NZ)]
Z_GROUPS = [[x * NZ + z for z in range(NZ)] for x in range(NX)]
F32, BF16 = jnp.float32, jnp.bfloat16
VMEM = pl.BlockSpec(memory_space=pltpu.VMEM)
HBM = pl.BlockSpec(memory_space=pltpu.HBM)
MIB = 1024 * 1024


def z_shift(step):
    return [(x * NZ + z, x * NZ + (z + step) % NZ) for x in range(NX) for z in range(NZ)]


def mm(left, right):
    return jnp.dot(left, right, preferred_element_type=F32)


def mm_nt(left, right):
    return lax.dot_general(left, right, (((1,), (1,)), ((), ())), preferred_element_type=F32)


def halves(value):
    high = value.astype(BF16)
    return high, (value - high.astype(F32)).astype(BF16)


def tie(value, *others):
    return lax.optimization_barrier((value, *others))[0]


def call(kernel, out_shape, specs, operands, flops, aliases=None, scratch=(), vmem=8):
    size = sum(x.size * x.dtype.itemsize for x in operands)
    return pl.pallas_call(
        kernel,
        out_shape=out_shape,
        in_specs=specs,
        out_specs=jax.tree.map(lambda _: VMEM, out_shape),
        scratch_shapes=scratch,
        input_output_aliases=aliases or {},
        cost_estimate=pl.CostEstimate(flops=flops, bytes_accessed=size, transcendentals=0),
        compiler_params=pltpu.CompilerParams(vmem_limit_bytes=vmem * MIB),
    )(*operands)


def fetch(pairs, sems):
    copies = [pltpu.make_async_copy(source, target, sems.at[k]) for k, (source, target) in enumerate(pairs)]
    for copy in copies:
        copy.start()
    return copies


def wait(copies):
    for copy in copies:
        copy.wait()


def start_kernel(
    input_hbm, grad_hbm, proj_in_hbm, proj_out_hbm, sent_ref, input_ref, grad_ref, proj_in_ref, proj_out_ref, sems
):
    wait(
        fetch(
            [
                (grad_hbm, grad_ref),
                (proj_out_hbm, proj_out_ref),
                (input_hbm, input_ref),
                (proj_in_hbm, proj_in_ref),
            ],
            sems,
        )
    )
    grad = grad_ref[...]
    both = jnp.concatenate(
        [mm_nt(proj_in_ref[...], input_ref[...]), mm_nt(proj_out_ref[...], grad)], axis=0
    )
    share = both.shape[1] // NX
    for x in range(NX):
        sent_ref[x] = jnp.concatenate([grad, *halves(both[:, x * share : (x + 1) * share])], axis=0)


def split_kernel(got_ref, block_ref, both_ref, parts_ref):
    deep = both_ref.shape[0]
    tokens = got_ref.shape[1] - 2 * deep
    both = got_ref[:, tokens : tokens + deep].astype(F32) + got_ref[:, tokens + deep :].astype(F32)
    both = jnp.sum(both, axis=0)
    both_ref[...] = both
    parts = jnp.concatenate(halves(both), axis=0)
    parts_ref[...] = parts
    block_ref[:, :tokens] = got_ref[:, :tokens]
    block_ref[:, tokens:] = parts.reshape(NX, -1, parts.shape[1])


def spread_kernel(both_ref, parts_ref, sent_ref):
    deep = both_ref.shape[0]
    both = both_ref[...] + parts_ref[:deep].astype(F32) + parts_ref[deep:].astype(F32)
    for x in range(NX):
        sent_ref[x] = both


def hidden_kernel(gate_ref, up_ref, proj_ref, activated_ref, slope_ref, hid_ref):
    gate = gate_ref[...].T.astype(F32)
    up = up_ref[...].T.astype(F32)
    sigmoid = jax.nn.sigmoid(gate)
    activated = gate * sigmoid
    activated_ref[...] = activated
    slope_ref[...] = up * (sigmoid * (1.0 + gate * (1.0 - sigmoid)))
    hid_ref[...] = mm_nt(proj_ref[...], (activated * up).astype(BF16))


def factor_kernel(both_ref, hid_ref, ids_ref, high_ref, low_ref, down_ref):
    rank, tokens = hid_ref.shape
    both = jnp.concatenate([both_ref[x] for x in range(NX)], axis=1)
    member = ids_ref[...] == lax.broadcasted_iota(jnp.int32, (SEQ_DEV, tokens), 0)

    def masked(value):
        spread = jnp.where(member[None], value[:, None, :], 0.0)
        return halves(spread.reshape(rank * SEQ_DEV, tokens))

    high_ref[...], low_ref[...] = masked(both[:rank])
    high, low = masked(hid_ref[...])
    right_high, right_low = halves(both[rank:])
    product = mm_nt(high, jnp.concatenate([right_high, right_low], axis=0))
    product = product[:, :rank] + product[:, rank:] + mm_nt(low, right_high)
    product = product.reshape(rank // 2, 2, SEQ_DEV, rank)
    down_ref[...] = jnp.concatenate([product[:, 0], product[:, 1]], axis=2)


def halve_kernel(first, block_ref, half_ref):
    half_ref[...] = block_ref[pl.ds(first, half_ref.shape[0]), : half_ref.shape[1]]


def halve(block, first, tokens):
    shape = (NX // 2, tokens, block.shape[2])
    return call(
        lambda *refs: halve_kernel(first, *refs), jax.ShapeDtypeStruct(shape, block.dtype), [VMEM], (block,), 1, vmem=4
    )


def sort_kernel(w_ref, *out_refs):
    width = w_ref.shape[1] // (NX * NZ)
    z_pos = lax.rem(lax.axis_index("mp"), NZ)
    for steps, out_ref in zip(RING, out_refs):
        for k, step in enumerate(steps):
            place = lax.rem(z_pos + (NZ - step), NZ)
            for x in range(NX):
                column = pl.multiple_of((x * NZ + place) * width, width)
                out_ref[:, pl.ds((k * NX + x) * width, width)] = w_ref[:, pl.ds(column, width)]


def rows(block_ref, tokens):
    return jnp.concatenate([block_ref[i, :tokens] for i in range(block_ref.shape[0])], axis=1)


def first_kernel(w_ref, block_ref, total_ref):
    total_ref[...] = mm_nt(rows(block_ref, total_ref.shape[0]), w_ref[...])


def pair_kernel(w_ref, up_ref, down_ref, total_in, both_in, total_ref, both_ref):
    tokens, deep = total_in.shape[0], both_in.shape[0]
    left = jnp.concatenate([rows(up_ref, tokens), rows(down_ref, tokens)], axis=1)
    total_ref[...] = total_in[...] + mm_nt(left, w_ref[...])
    both = both_in[...]
    for block in (up_ref, down_ref):
        parts = jnp.concatenate([block[x, tokens:] for x in range(NX)], axis=0).astype(F32)
        both += parts[:deep] + parts[deep:]
    both_ref[...] = both


def add_pair(w_part, up, down, total, both):
    return call(
        pair_kernel,
        (jax.ShapeDtypeStruct(total.shape, F32), jax.ShapeDtypeStruct(both.shape, F32)),
        [VMEM] * 5,
        (w_part, up, down, total, both),
        4 * w_part.shape[0] * up.size,
        {3: 0, 4: 1},
    )


def last_kernel(
    w_ref, up_piece, down_piece, total_ref, activated_ref, slope_ref, gate_proj, up_proj, high_ref, low_ref, down_ref,
    sent_ref,
):
    tokens = total_ref.shape[0]
    left = jnp.concatenate([rows(up_piece, tokens), rows(down_piece, tokens)], axis=1)
    hidden_grad = total_ref[...] + mm_nt(left, w_ref[...])
    gate_grad = (hidden_grad * slope_ref[...]).astype(BF16)
    upward_grad = (hidden_grad * activated_ref[...]).astype(BF16)
    factors = jnp.concatenate([mm_nt(gate_grad, gate_proj[...]), mm_nt(upward_grad, up_proj[...])], axis=1)
    high, low = halves(factors)
    product = mm(high_ref[...], jnp.concatenate([high, low], axis=1))
    wide = factors.shape[1]
    product = product[:, :wide] + product[:, wide:] + mm(low_ref[...], high)
    devices = sent_ref.shape[0]
    product = product.reshape(devices, 2 * SEQ_DEV, wide)
    sent_ref[...] = jnp.concatenate([product, down_ref[...]], axis=1).astype(BF16)


def per_device(
    layer_input,
    gate_pre,
    up_pre,
    out_grad,
    w_down,
    proj_input,
    proj_hidden,
    proj_gate,
    proj_upward,
    proj_output,
    seq_ids,
):
    tokens, width = out_grad.shape
    hidden = w_down.shape[0]
    rank = proj_input.shape[1]
    mp_size = lax.axis_size("mp")
    dp_size = lax.axis_size("dp")

    def shape(dims, dtype=F32):
        return jax.ShapeDtypeStruct(dims, dtype)

    deep, share = 2 * rank, tokens // NX
    sent = call(
        start_kernel,
        shape((NX, tokens + 2 * deep, width), BF16),
        [HBM] * 4,
        (layer_input, out_grad, proj_input.T, proj_output),
        4 * tokens * width * rank,
        scratch=[
            pltpu.VMEM((tokens, width), BF16),
            pltpu.VMEM((tokens, width), BF16),
            pltpu.VMEM((rank, width), BF16),
            pltpu.VMEM((rank, width), BF16),
            pltpu.SemaphoreType.DMA((4,)),
        ],
        vmem=56,
    )
    got = lax.all_to_all(sent, "mp", 0, 0, axis_index_groups=X_GROUPS)
    activated, slope, hid_part = call(
        hidden_kernel,
        (shape((tokens, hidden)), shape((tokens, hidden)), shape((rank, tokens))),
        [VMEM] * 3,
        (gate_pre.T, up_pre.T, proj_hidden.T),
        2 * tokens * hidden * rank,
    )
    w_parts = call(
        sort_kernel, [shape((hidden, len(steps) * NX * width), BF16) for steps in RING], [VMEM], (w_down,), w_down.size
    )
    got = tie(got, hid_part, *w_parts)
    across_x, both, parts = call(
        split_kernel,
        (
            shape((NX, tokens + 2 * deep // NX, width), BF16),
            shape((deep, share)),
            shape((2 * deep, share), BF16),
        ),
        [VMEM],
        (got,),
        got.size,
    )
    far_parts = lax.ppermute(parts, "mp", z_shift(NZ // 2))

    up = down = across_x
    next_up, next_down = lax.ppermute(up, "mp", z_shift(1)), lax.ppermute(down, "mp", z_shift(-1))
    total = call(
        first_kernel, shape((tokens, hidden)), [VMEM] * 2, (w_parts[0], across_x), 2 * hidden * across_x.size
    )
    next_up = tie(next_up, total)
    for step in (1, 2):
        up, down = next_up, next_down
        next_up, next_down = lax.ppermute(up, "mp", z_shift(1)), lax.ppermute(down, "mp", z_shift(-1))
        total, both = add_pair(w_parts[step], up, down, total, both)
        next_up = tie(next_up, total)

    up, down = next_up, next_down
    far_up = lax.ppermute(halve(up, 0, tokens), "mp", z_shift(1))
    far_down = lax.ppermute(halve(down, NX // 2, tokens), "mp", z_shift(-1))
    total, both = add_pair(w_parts[3], up, down, total, both)
    both = call(spread_kernel, shape((NX, deep, share)), [VMEM] * 2, (both, far_parts), 1)
    shared = lax.all_to_all(both, "mp", 0, 0, axis_index_groups=X_GROUPS)
    high, low, down_raw = call(
        factor_kernel,
        (
            shape((rank * SEQ_DEV, tokens), BF16),
            shape((rank * SEQ_DEV, tokens), BF16),
            shape((mp_size, SEQ_DEV, 2 * rank)),
        ),
        [VMEM] * 3,
        (shared, hid_part, seq_ids),
        6 * SEQ_DEV * tokens * rank * rank,
    )
    sent = call(
        last_kernel,
        shape((mp_size, 3 * SEQ_DEV, 2 * rank), BF16),
        [VMEM] * 11,
        (
            w_parts[4], far_up, far_down, total, activated, slope, proj_gate.T, proj_upward.T, high, low, down_raw,
        ),
        2 * tokens * hidden * (NX * width + 2 * rank),
        vmem=16,
    )
    got = jnp.sum(lax.all_to_all(sent, "mp", 0, 0).astype(F32), axis=0)
    paired, down_raw = got[: 2 * SEQ_DEV], got[2 * SEQ_DEV :]
    paired = paired.reshape(2, SEQ_DEV, 2, rank).transpose(1, 2, 0, 3).reshape(SEQ_DEV, 2, 2 * rank)
    raw = jnp.concatenate([paired, down_raw[:, None]], axis=1)

    squares = jnp.sum(raw * raw, axis=(0, 2))
    squares = jnp.pad(squares, (0, 125)).reshape(1, 1, 128)
    for axis, size in (("mp", mp_size), ("dp", dp_size)):
        squares = jnp.sum(
            lax.all_to_all(jnp.broadcast_to(squares, (size, 1, 128)), axis, 0, 0), axis=0, keepdims=True
        )
    entries = SEQ_DEV * dp_size * rank * rank
    scale = lax.rsqrt(squares[0, 0, :3] / entries + 1e-06)
    return raw * scale[None, :, None]


def solution(mesh):
    in_specs = (
        P("dp", "mp"),
        P("dp", "mp"),
        P("dp", "mp"),
        P("dp", "mp"),
        P("mp", None),
        P("mp", None),
        P("mp", None),
        P("mp", None),
        P("mp", None),
        P(None, "mp"),
        P("dp", None),
    )
    out_specs = P("dp", None, "mp")
    return jax.shard_map(
        per_device, mesh=mesh, in_specs=in_specs, out_specs=out_specs, check_vma=False
    )
```

time: 381 us -> 141 us (0.37)
  waiting for transfers between devices: 250 us -> 19.3 us
  starting transfers between devices: 0.04 us -> 44.4 us
  blocking collectives: 99.9 us -> 57.7 us
  matrix products: 14.8 us -> 0 us
  between operations: 13.5 us -> 0.33 us
  Pallas kernels: 0 us -> 8.9 us
  local copies, waits for them, and re-layouts: 1.2 us -> 8.86 us
    psum x1 -> x0, waiting for transfers between devices: 160 us -> none  [per_device(): lax.psum((in_part, hid_part, gate_part, up_part, out_part), 'mp')]
    psum x1 -> x0, blocking collectives: 99.9 us -> none  [per_device(): total_sq = lax.psum(squares, ('dp', 'mp'))]
    all_gather x1 -> x0, waiting for transfers between devices: 89.2 us -> none  [per_device(): lax.all_gather(out_grad, 'mp', axis=1, tiled=True)]
    all_to_all x0 -> x4, blocking collectives: none -> 57.7 us  [the longest x2 36.9 us: per_device(): lax.all_to_all(jnp.broadcast_to(squares, (size, 1, 128)), axis, 0, 0)]
    ppermute x0 -> x9, starting transfers between devices: none -> 39.6 us  [the longest x3 17.7 us: per_device(): lax.ppermute(down, 'mp', z_shift(-1))]
    ppermute x0 -> x9, waiting for transfers between devices: none -> 19.2 us  [the longest x3 19.2 us: per_device(): lax.ppermute(up, 'mp', z_shift(1))]
    dot_general x8 -> x0, matrix products: 14.8 us -> none  [the longest x1 5.4 us: per_device(): lax.dot_general(lax.all_gather(out_grad, 'mp', axis=1, tiled=True), w_dow...]
    pallas_call x0 -> x13, Pallas kernels: none -> 8.9 us  [call(): pl.pallas_call(kernel, out_shape=out_shape, in_specs=specs, out_specs=jax...]
  transfers between devices with their start and end apart: 2 -> 10, of which waited for: 2 -> 4; matrix products, arithmetic and copies ran while one was open for 1% -> 0% of each run, Pallas kernels for 0% -> 4%
where the time goes in v3:
time: 141 us; the launch traced here: 140 us
  blocking collectives  57.7 us (41%)
  starting transfers between devices  44.4 us (31%)
  waiting for transfers between devices  19.3 us (14%)
  Pallas kernels  8.9 us (6%)
  local copies, waits for them, and re-layouts  8.86 us (6%)
    all_to_all x2, blocking collectives, per_device(): lax.all_to_all(jnp.broadcast_to(squares, (size, 1, 128)), axis, 0, 0)  36.9 us
    ppermute x3, waiting for transfers between devices, per_device(): lax.ppermute(up, 'mp', z_shift(1))  19.2 us
    ppermute x3, starting transfers between devices, per_device(): lax.ppermute(down, 'mp', z_shift(-1))  17.7 us
    all_to_all x1, blocking collectives, per_device(): got = jnp.sum(lax.all_to_all(sent, 'mp', 0, 0).astype(F32), axis=0)  12.8 us
    ppermute x3, starting transfers between devices, per_device(): lax.ppermute(up, 'mp', z_shift(1))  11 us
    pallas_call x13, Pallas kernels, call(): pl.pallas_call(kernel, out_shape=out_shape, in_specs=specs, out_specs=jax...  8.9 us
    unnamed x34, local copies, waits for them, and re-layouts  8.66 us
    all_to_all x1, blocking collectives, per_device(): shared = lax.all_to_all(both, 'mp', 0, 0, axis_index_groups=X_GROUPS)  7.92 us
  transfers between devices with their start and end apart: 10, of which 4 were waited for; matrix products, arithmetic and copies ran while one was open for 0% of the time, Pallas kernels for 4%

profile of v3, /device:TPU:1, one launch (start us, length us, event | category | flops | bytes accessed | tf_op | source)
XLA Modules:
  0.0 140.4 jit_solution(2646574238860267811)
XLA Ops:
  0.0 0.0 copy-start.7
  0.0 0.0 copy-start.15
  0.0 2.2 %shard_map.110 = bf16[4,768,128]{2,1,0:T(8,128)(2,1)} custom-call(bf16[512,128]{1,0:T(8,128)(2,1)} %input_hbm.1, bf16[512,128]{1,0:T(8,128)(2,1)} %grad_hbm.1, bf16[64,128]{1,0:T(8,128)(2,1)} %bitcast.24, bf16[64,128]{1,0:T(8,128)(2,1)} %proj_out_hbm.1), custom_call_target="tpu_custom_call" | custom-call | flops 16777216 | bytes 294912 | tf_op jit(solution)/shard_map/pallas_call | solution.py:43
  2.2 4.9 %all-to-all-start = ((bf16[4,768,128]{2,1,0:T(8,128)(2,1)}), bf16[4,768,128]{2,1,0:T(8,128)(2,1)S(1)}, u32[]{:S(2)}, u32[]{:S(2)}) async-start(bf16[4,768,128]{2,1,0:T(8,128)(2,1)} %shard_map.110), calls=%async_computation | async-start | bytes 1572864 | tf_op jit(solution)/shard_map/all_to_all | solution.py:246
  7.1 2.0 %copy-done = bf16[448,4096]{1,0:T(8,128)(2,1)S(1)} copy-done((bf16[448,4096]{1,0:T(8,128)(2,1)S(1)}, bf16[448,4096]{1,0:T(8,128)(2,1)}, u32[]{:S(2)}) %copy-start) | copy-done | bytes 3670040
  9.1 1.0 shard_map.109
  10.1 0.0 copy-start.1
  10.1 0.9 copy-done.1
  11.0 1.0 copy-done.3
  12.0 0.9 copy-done.5
  12.9 0.8 copy-done.9
  13.7 0.8 copy-done.11
  14.5 0.0 copy-done.7
  14.5 0.0 copy-done.15
  14.5 0.0 copy-done.8
  14.5 0.8 shard_map.111
  15.3 0.1 all-to-all-done.got_ref
  15.4 0.1 shard_map.112
  15.5 7.2 %collective-permute-start = (bf16[4,576,128]{2,1,0:T(8,128)(2,1)S(1)}, bf16[4,576,128]{2,1,0:T(8,128)(2,1)S(1)}, u32[]{:S(2)}, u32[]{:S(2)}) collective-permute-start(bf16[4,576,128]{2,1,0:T(8,128)(2,1)S(1)} %get-tuple-element.36.block_ref), channel_id=1, source_target_pairs={{0,1},{1,2},{2,3},{3,4},{4,5},{5,6},{6,7},{7,0},{8,9},{9,10},{10,1... | collective-permute-start | bytes 1769480 | tf_op jit(solution)/shard_map/ppermute | solution.py:272
  22.6 8.6 %collective-permute-start.2 = (bf16[4,576,128]{2,1,0:T(8,128)(2,1)S(1)}, bf16[4,576,128]{2,1,0:T(8,128)(2,1)S(1)}, u32[]{:S(2)}, u32[]{:S(2)}) collective-permute-start(bf16[4,576,128]{2,1,0:T(8,128)(2,1)S(1)} %get-tuple-element.36.block_ref), channel_id=1, source_target_pairs={{0,7},{1,0},{2,1},{3,2},{4,3},{5,4},{6,5},{7,6},{8,15},{9,8},{10,9... | collective-permute-start | bytes 1769480 | tf_op jit(solution)/shard_map/ppermute | solution.py:272
  31.2 0.0 copy-start.12
  31.2 1.0 copy-done.12
  32.3 0.5 shard_map.113.total_in
  32.7 8.4 %collective-permute-done.up_ref = bf16[4,576,128]{2,1,0:T(8,128)(2,1)S(1)} collective-permute-done((bf16[4,576,128]{2,1,0:T(8,128)(2,1)S(1)}, bf16[4,576,128]{2,1,0:T(8,128)(2,1)S(1)}, u32[]{:S(2)}, u32[]{:S(2)}) %collective-permute-start) | collective-permute-done | bytes 589856 | tf_op jit(solution)/shard_map/ppermute | solution.py:272
  41.1 1.9 %collective-permute-start.1 = (bf16[4,576,128]{2,1,0:T(8,128)(2,1)S(1)}, bf16[4,576,128]{2,1,0:T(8,128)(2,1)S(1)}, u32[]{:S(2)}, u32[]{:S(2)}) collective-permute-start(bf16[4,576,128]{2,1,0:T(8,128)(2,1)S(1)} %collective-permute-done.up_ref), channel_id=1, source_target_pairs={{0,1},{1,2},{2,3},{3,4},{4,5},{5,6},{6,7},{7,0},{8,9},{9,10},{10,1... | collective-permute-start | bytes 1769480 | tf_op jit(solution)/shard_map/ppermute | solution.py:279
  43.0 0.0 collective-permute-done.2.down_ref
  43.0 4.6 %collective-permute-start.4 = (bf16[4,576,128]{2,1,0:T(8,128)(2,1)S(1)}, bf16[4,576,128]{2,1,0:T(8,128)(2,1)S(1)}, u32[]{:S(2)}, u32[]{:S(2)}) collective-permute-start(bf16[4,576,128]{2,1,0:T(8,128)(2,1)S(1)} %collective-permute-done.2.down_ref), channel_id=1, source_target_pairs={{0,7},{1,0},{2,1},{3,2},{4,3},{5,4},{6,5},{7,6},{8,15},{9,8},{10,9... | collective-permute-start | bytes 1769480 | tf_op jit(solution)/shard_map/ppermute | solution.py:279
  47.6 0.0 copy-start.6
  47.6 1.2 copy-done.6
  48.8 0.8 shard_map.114
  49.5 6.9 %collective-permute-done.1.up_ref = bf16[4,576,128]{2,1,0:T(8,128)(2,1)S(1)} collective-permute-done((bf16[4,576,128]{2,1,0:T(8,128)(2,1)S(1)}, bf16[4,576,128]{2,1,0:T(8,128)(2,1)S(1)}, u32[]{:S(2)}, u32[]{:S(2)}) %collective-permute-start.1) | collective-permute-done | bytes 589856 | tf_op jit(solution)/shard_map/ppermute | solution.py:279
  56.5 1.9 %collective-permute-start.3 = (bf16[4,576,128]{2,1,0:T(8,128)(2,1)S(1)}, bf16[4,576,128]{2,1,0:T(8,128)(2,1)S(1)}, u32[]{:S(2)}, u32[]{:S(2)}) collective-permute-start(bf16[4,576,128]{2,1,0:T(8,128)(2,1)S(1)} %collective-permute-done.1.up_ref), channel_id=1, source_target_pairs={{0,1},{1,2},{2,3},{3,4},{4,5},{5,6},{6,7},{7,0},{8,9},{9,10},{10,1... | collective-permute-start | bytes 1769480 | tf_op jit(solution)/shard_map/ppermute | solution.py:279
  58.4 0.0 collective-permute-done.4.down_ref
  58.4 4.6 %collective-permute-start.6 = (bf16[4,576,128]{2,1,0:T(8,128)(2,1)S(1)}, bf16[4,576,128]{2,1,0:T(8,128)(2,1)S(1)}, u32[]{:S(2)}, u32[]{:S(2)}) collective-permute-start(bf16[4,576,128]{2,1,0:T(8,128)(2,1)S(1)} %collective-permute-done.4.down_ref), channel_id=1, source_target_pairs={{0,7},{1,0},{2,1},{3,2},{4,3},{5,4},{6,5},{7,6},{8,15},{9,8},{10,9... | collective-permute-start | bytes 1769480 | tf_op jit(solution)/shard_map/ppermute | solution.py:279
  63.0 4.0 %collective-permute-start.8 = (bf16[256,128]{1,0:T(8,128)(2,1)S(1)}, bf16[256,128]{1,0:T(8,128)(2,1)S(1)}, u32[]{:S(2)}, u32[]{:S(2)}) collective-permute-start(bf16[256,128]{1,0:T(8,128)(2,1)S(1)} %get-tuple-element.49), channel_id=1, source_target_pairs={{0,4},{1,5},{2,6},{3,7},{4,0},{5,1},{6,2},{7,3},{8,12},{9,13},{10,... | collective-permute-start | bytes 196616 | tf_op jit(solution)/shard_map/ppermute | solution.py:269
  67.0 0.0 copy-done.4
  67.0 0.8 shard_map.115
  67.8 0.0 copy-start.16
  67.8 0.0 copy-start.10
  67.8 0.0 copy-start.13
  67.8 0.0 copy-start.14
  67.8 3.9 %collective-permute-done.3.refs_0_.up_ref = bf16[4,576,128]{2,1,0:T(8,128)(2,1)S(1)} collective-permute-done((bf16[4,576,128]{2,1,0:T(8,128)(2,1)S(1)}, bf16[4,576,128]{2,1,0:T(8,128)(2,1)S(1)}, u32[]{:S(2)}, u32[]{:S(2)}) %collective-permute-start.3) | collective-permute-done | bytes 589856 | tf_op jit(solution)/shard_map/ppermute | solution.py:279
  71.7 1.9 %collective-permute-start.5 = (bf16[2,512,128]{2,1,0:T(8,128)(2,1)S(1)}, bf16[2,512,128]{2,1,0:T(8,128)(2,1)S(1)}, u32[]{:S(2)}, u32[]{:S(2)}) collective-permute-start(bf16[2,512,128]{2,1,0:T(8,128)(2,1)S(1)} %shard_map.116), channel_id=1, source_target_pairs={{0,1},{1,2},{2,3},{3,4},{4,5},{5,6},{6,7},{7,0},{8,9},{9,10},{10,1... | collective-permute-start | bytes 786440 | tf_op jit(solution)/shard_map/ppermute | solution.py:284
  73.6 0.0 collective-permute-done.6.refs_0_.down_ref
  73.7 5.0 %collective-permute-start.7 = (bf16[2,512,128]{2,1,0:T(8,128)(2,1)S(1)}, bf16[2,512,128]{2,1,0:T(8,128)(2,1)S(1)}, u32[]{:S(2)}, u32[]{:S(2)}) collective-permute-start(bf16[2,512,128]{2,1,0:T(8,128)(2,1)S(1)} %shard_map.117), channel_id=1, source_target_pairs={{0,7},{1,0},{2,1},{3,2},{4,3},{5,4},{6,5},{7,6},{8,15},{9,8},{10,9... | collective-permute-start | bytes 786440 | tf_op jit(solution)/shard_map/ppermute | solution.py:285
  78.6 0.0 copy-done.2
  78.6 0.8 shard_map.118
  79.4 0.0 collective-permute-done.8.parts_ref
  79.5 7.9 %all_to_all.25.both_ref = f32[4,128,128]{2,1,0:T(8,128)S(1)} all-to-all(f32[4,128,128]{2,1,0:T(8,128)S(1)} %shard_map.119), channel_id=1, replica_groups={{0,8,16,24},{1,9,17,25},{2,10,18,26},{3,11,19,27},{4,12,20,28},{5,13,21..., dimensions={0} | all-to-all | bytes 524288 | tf_op jit(solution)/shard_map/all_to_all | solution.py:288
  87.4 0.0 copy-done.16
  87.4 0.9 shard_map.120
  88.3 0.0 collective-permute-done.5.up_piece
  88.3 0.0 collective-permute-done.7.down_piece
  88.3 0.0 copy-done.10
  88.3 0.0 copy-done.13
  88.4 0.0 copy-done.14
  88.4 1.2 shard_map.121
  89.5 12.8 %all_to_all.26 = bf16[32,24,128]{2,1,0:T(8,128)(2,1)S(1)} all-to-all(bf16[32,24,128]{2,1,0:T(8,128)(2,1)S(1)} %shard_map.121), channel_id=1, replica_groups=mesh['dp'=16,'mp'=32] {'mp'}, dimensions={0} | all-to-all | bytes 393216 | tf_op jit(solution)/shard_map/all_to_all | solution.py:310
  102.4 0.1 reshape.29
  102.5 0.1 reshape.30
  102.6 0.1 multiply_reduce_fusion
  102.8 12.4 %all_to_all.27 = f32[32,1,128]{2,1,0:T(1,128)S(1)} all-to-all(f32[32,1,128]{2,1,0:T(1,128)S(1)} %broadcast_in_dim.9), channel_id=1, replica_groups=mesh['dp'=16,'mp'=32] {'mp'}, dimensions={0} | all-to-all | bytes 32768 | tf_op jit(solution)/shard_map/all_to_all | solution.py:319
  115.2 24.5 %all_to_all.28 = f32[16,1,128]{2,1,0:T(1,128)S(1)} all-to-all(f32[16,1,128]{2,1,0:T(1,128)S(1)} %broadcast_in_dim.20), channel_id=1, replica_groups=mesh['dp'=16,'mp'=32] {'dp'}, dimensions={0} | all-to-all | bytes 16384 | tf_op jit(solution)/shard_map/all_to_all | solution.py:319
  139.7 0.7 fusion
  (21 shorter events, 0.2 us)
Async XLA Ops:
  0.0 14.5 %copy-start.7 = (bf16[512,448]{0,1:T(8,128)(2,1)S(1)}, bf16[512,448]{0,1:T(8,128)(2,1)}, u32[]{:S(2)}) copy-start(bf16[512,448]{0,1:T(8,128)(2,1)} %param.12) | copy-start | bytes 1376260
  0.0 14.5 %copy-start.15 = (bf16[448,64]{0,1:T(8,128)(2,1)S(1)}, bf16[448,64]{0,1:T(8,128)(2,1)}, u32[]{:S(2)}) copy-start(bf16[448,64]{0,1:T(8,128)(2,1)} %param.17) | copy-start | bytes 172036
  2.2 13.2 %all-to-all-start = ((bf16[4,768,128]{2,1,0:T(8,128)(2,1)}), bf16[4,768,128]{2,1,0:T(8,128)(2,1)S(1)}, u32[]{:S(2)}, u32[]{:S(2)}) async-start(bf16[4,768,128]{2,1,0:T(8,128)(2,1)} %shard_map.110), calls=%async_computation | async-start | bytes 1572864 | tf_op jit(solution)/shard_map/all_to_all | solution.py:246
  7.1 2.0 %copy-start = (bf16[448,4096]{1,0:T(8,128)(2,1)S(1)}, bf16[448,4096]{1,0:T(8,128)(2,1)}, u32[]{:S(2)}) copy-start(bf16[448,4096]{1,0:T(8,128)(2,1)} %w_ref.1) | copy-start | bytes 11010052
  9.1 5.4 %copy-start.8 = (bf16[512,448]{0,1:T(8,128)(2,1)S(1)}, bf16[512,448]{0,1:T(8,128)(2,1)}, u32[]{:S(2)}) copy-start(bf16[512,448]{0,1:T(8,128)(2,1)} %param.13) | copy-start | bytes 1376260
  10.1 0.9 copy-start.1
  11.0 1.0 copy-start.3
  12.0 0.9 copy-start.5
  12.9 0.8 copy-start.9
  13.7 0.8 copy-start.11
  15.4 51.6 %copy-start.4 = (bf16[448,1024]{1,0:T(8,128)(2,1)S(1)}, bf16[448,1024]{1,0:T(8,128)(2,1)}, u32[]{:S(2)}) copy-start(bf16[448,1024]{1,0:T(8,128)(2,1)} %copy-done.3) | copy-start | bytes 2752516
  15.5 25.6 %collective-permute-start = (bf16[4,576,128]{2,1,0:T(8,128)(2,1)S(1)}, bf16[4,576,128]{2,1,0:T(8,128)(2,1)S(1)}, u32[]{:S(2)}, u32[]{:S(2)}) collective-permute-start(bf16[4,576,128]{2,1,0:T(8,128)(2,1)S(1)} %get-tuple-element.36.block_ref), channel_id=1, source_target_pairs={{0,1},{1,2},{2,3},{3,4},{4,5},{5,6},{6,7},{7,0},{8,9},{9,10},{10,1... | collective-permute-start | bytes 1769480 | tf_op jit(solution)/shard_map/ppermute | solution.py:272
  22.6 20.3 %collective-permute-start.2 = (bf16[4,576,128]{2,1,0:T(8,128)(2,1)S(1)}, bf16[4,576,128]{2,1,0:T(8,128)(2,1)S(1)}, u32[]{:S(2)}, u32[]{:S(2)}) collective-permute-start(bf16[4,576,128]{2,1,0:T(8,128)(2,1)S(1)} %get-tuple-element.36.block_ref), channel_id=1, source_target_pairs={{0,7},{1,0},{2,1},{3,2},{4,3},{5,4},{6,5},{7,6},{8,15},{9,8},{10,9... | collective-permute-start | bytes 1769480 | tf_op jit(solution)/shard_map/ppermute | solution.py:272
  31.2 1.0 copy-start.12
  41.1 15.4 %collective-permute-start.1 = (bf16[4,576,128]{2,1,0:T(8,128)(2,1)S(1)}, bf16[4,576,128]{2,1,0:T(8,128)(2,1)S(1)}, u32[]{:S(2)}, u32[]{:S(2)}) collective-permute-start(bf16[4,576,128]{2,1,0:T(8,128)(2,1)S(1)} %collective-permute-done.up_ref), channel_id=1, source_target_pairs={{0,1},{1,2},{2,3},{3,4},{4,5},{5,6},{6,7},{7,0},{8,9},{9,10},{10,1... | collective-permute-start | bytes 1769480 | tf_op jit(solution)/shard_map/ppermute | solution.py:279
  43.0 15.4 %collective-permute-start.4 = (bf16[4,576,128]{2,1,0:T(8,128)(2,1)S(1)}, bf16[4,576,128]{2,1,0:T(8,128)(2,1)S(1)}, u32[]{:S(2)}, u32[]{:S(2)}) collective-permute-start(bf16[4,576,128]{2,1,0:T(8,128)(2,1)S(1)} %collective-permute-done.2.down_ref), channel_id=1, source_target_pairs={{0,7},{1,0},{2,1},{3,2},{4,3},{5,4},{6,5},{7,6},{8,15},{9,8},{10,9... | collective-permute-start | bytes 1769480 | tf_op jit(solution)/shard_map/ppermute | solution.py:279
  47.6 1.2 copy-start.6
  48.8 29.9 %copy-start.2 = (bf16[448,1024]{1,0:T(8,128)(2,1)S(1)}, bf16[448,1024]{1,0:T(8,128)(2,1)}, u32[]{:S(2)}) copy-start(bf16[448,1024]{1,0:T(8,128)(2,1)} %copy-done.1) | copy-start | bytes 2752516
  56.5 15.2 %collective-permute-start.3 = (bf16[4,576,128]{2,1,0:T(8,128)(2,1)S(1)}, bf16[4,576,128]{2,1,0:T(8,128)(2,1)S(1)}, u32[]{:S(2)}, u32[]{:S(2)}) collective-permute-start(bf16[4,576,128]{2,1,0:T(8,128)(2,1)S(1)} %collective-permute-done.1.up_ref), channel_id=1, source_target_pairs={{0,1},{1,2},{2,3},{3,4},{4,5},{5,6},{6,7},{7,0},{8,9},{9,10},{10,1... | collective-permute-start | bytes 1769480 | tf_op jit(solution)/shard_map/ppermute | solution.py:279
  58.4 15.2 %collective-permute-start.6 = (bf16[4,576,128]{2,1,0:T(8,128)(2,1)S(1)}, bf16[4,576,128]{2,1,0:T(8,128)(2,1)S(1)}, u32[]{:S(2)}, u32[]{:S(2)}) collective-permute-start(bf16[4,576,128]{2,1,0:T(8,128)(2,1)S(1)} %collective-permute-done.4.down_ref), channel_id=1, source_target_pairs={{0,7},{1,0},{2,1},{3,2},{4,3},{5,4},{6,5},{7,6},{8,15},{9,8},{10,9... | collective-permute-start | bytes 1769480 | tf_op jit(solution)/shard_map/ppermute | solution.py:279
  63.0 16.4 %collective-permute-start.8 = (bf16[256,128]{1,0:T(8,128)(2,1)S(1)}, bf16[256,128]{1,0:T(8,128)(2,1)S(1)}, u32[]{:S(2)}, u32[]{:S(2)}) collective-permute-start(bf16[256,128]{1,0:T(8,128)(2,1)S(1)} %get-tuple-element.49), channel_id=1, source_target_pairs={{0,4},{1,5},{2,6},{3,7},{4,0},{5,1},{6,2},{7,3},{8,12},{9,13},{10,... | collective-permute-start | bytes 196616 | tf_op jit(solution)/shard_map/ppermute | solution.py:269
  67.8 19.6 %copy-start.16 = (s32[1,512]{1,0:T(1,128)S(1)}, s32[1,512]{1,0:T(1,128)}, u32[]{:S(2)}) copy-start(s32[1,512]{1,0:T(1,128)} %ids_ref.1) | copy-start | bytes 6148
  67.8 20.6 %copy-start.10 = (bf16[448,512]{1,0:T(8,128)(2,1)S(1)}, bf16[448,512]{1,0:T(8,128)(2,1)}, u32[]{:S(2)}) copy-start(bf16[448,512]{1,0:T(8,128)(2,1)} %copy-done.9) | copy-start | bytes 1376260
  67.8 20.6 %copy-start.13 = (bf16[448,64]{0,1:T(8,128)(2,1)S(1)}, bf16[448,64]{0,1:T(8,128)(2,1)}, u32[]{:S(2)}) copy-start(bf16[448,64]{0,1:T(8,128)(2,1)} %param.18) | copy-start | bytes 172036
  67.8 20.6 %copy-start.14 = (bf16[448,64]{0,1:T(8,128)(2,1)S(1)}, bf16[448,64]{0,1:T(8,128)(2,1)}, u32[]{:S(2)}) copy-start(bf16[448,64]{0,1:T(8,128)(2,1)} %param.19) | copy-start | bytes 172036
  71.7 16.6 %collective-permute-start.5 = (bf16[2,512,128]{2,1,0:T(8,128)(2,1)S(1)}, bf16[2,512,128]{2,1,0:T(8,128)(2,1)S(1)}, u32[]{:S(2)}, u32[]{:S(2)}) collective-permute-start(bf16[2,512,128]{2,1,0:T(8,128)(2,1)S(1)} %shard_map.116), channel_id=1, source_target_pairs={{0,1},{1,2},{2,3},{3,4},{4,5},{5,6},{6,7},{7,0},{8,9},{9,10},{10,1... | collective-permute-start | bytes 786440 | tf_op jit(solution)/shard_map/ppermute | solution.py:284
  73.7 14.7 %collective-permute-start.7 = (bf16[2,512,128]{2,1,0:T(8,128)(2,1)S(1)}, bf16[2,512,128]{2,1,0:T(8,128)(2,1)S(1)}, u32[]{:S(2)}, u32[]{:S(2)}) collective-permute-start(bf16[2,512,128]{2,1,0:T(8,128)(2,1)S(1)} %shard_map.117), channel_id=1, source_target_pairs={{0,7},{1,0},{2,1},{3,2},{4,3},{5,4},{6,5},{7,6},{8,15},{9,8},{10,9... | collective-permute-start | bytes 786440 | tf_op jit(solution)/shard_map/ppermute | solution.py:285

commit v4 on v3

v4 whole, which is shorter than its diff:
```python
import jax
import jax.numpy as jnp
from jax import lax
from jax.experimental import pallas as pl
from jax.experimental.pallas import tpu as pltpu
from jax.sharding import PartitionSpec as P

SEQ_DEV = 8
NX = 4
NZ = 8
X_GROUPS = [[x * NZ + z for x in range(NX)] for z in range(NZ)]
F32, BF16 = jnp.float32, jnp.bfloat16
VMEM = pl.BlockSpec(memory_space=pltpu.VMEM)
HBM = pl.BlockSpec(memory_space=pltpu.HBM)
MIB = 1024 * 1024


def z_shift(step):
    return [(x * NZ + z, x * NZ + (z + step) % NZ) for x in range(NX) for z in range(NZ)]


PARTNER = [(x * NZ + z, (x ^ 1) * NZ + z) for x in range(NX) for z in range(NZ)]
OPPOSITE = [(x * NZ + z, (x ^ 2) * NZ + z) for x in range(NX) for z in range(NZ)]


def place():
    position = lax.axis_index("mp")
    x_pos = lax.div(position, NZ)
    return x_pos, lax.rem(position, NZ), lax.rem(x_pos, 2), lax.rem(lax.axis_index("dp"), 2)


def span(index, size):
    return pl.ds(pl.multiple_of(index * size, size), size)


def quarters(ref, parity):
    share = ref.shape[1] // NX
    return jnp.concatenate([ref[:, span(parity, share)], ref[:, span(parity + 2, share)]], axis=1)


def mm(left, right):
    return jnp.dot(left, right, preferred_element_type=F32)


def mm_nt(left, right):
    return lax.dot_general(left, right, (((1,), (1,)), ((), ())), preferred_element_type=F32)


def halves(value):
    high = value.astype(BF16)
    return high, (value - high.astype(F32)).astype(BF16)


def tie(value, *others):
    return lax.optimization_barrier((value, *others))[0]


def call(kernel, out_shape, specs, operands, flops, aliases=None, scratch=(), vmem=8, out_specs=None):
    size = sum(x.size * x.dtype.itemsize for x in operands)
    return pl.pallas_call(
        kernel,
        out_shape=out_shape,
        in_specs=specs,
        out_specs=out_specs or jax.tree.map(lambda _: VMEM, out_shape),
        scratch_shapes=scratch,
        input_output_aliases=aliases or {},
        cost_estimate=pl.CostEstimate(flops=flops, bytes_accessed=size, transcendentals=0),
        compiler_params=pltpu.CompilerParams(vmem_limit_bytes=vmem * MIB),
    )(*operands)


def fetch(pairs, sems):
    copies = [pltpu.make_async_copy(source, target, sems.at[k]) for k, (source, target) in enumerate(pairs)]
    for copy in copies:
        copy.start()
    return copies


def wait(copies):
    for copy in copies:
        copy.wait()


def start_kernel(
    input_hbm, grad_hbm, gate_hbm, up_hbm, proj_in_hbm, proj_out_hbm, proj_hid_hbm, sent_ref,
    input_ref, grad_ref, gate_ref, up_ref, proj_in_ref, proj_out_ref, proj_hid_ref, sems,
):
    copies = fetch(
        [
            (grad_hbm, grad_ref),
            (proj_out_hbm, proj_out_ref),
            (input_hbm, input_ref),
            (proj_in_hbm, proj_in_ref),
            (gate_hbm, gate_ref),
            (up_hbm, up_ref),
            (proj_hid_hbm, proj_hid_ref),
        ],
        sems,
    )
    wait(copies[:4])
    grad = grad_ref[...]
    factors = [mm_nt(proj_in_ref[...], input_ref[...]), mm_nt(proj_out_ref[...], grad)]
    wait(copies[4:])
    gate = gate_ref[...].astype(F32)
    hidden = gate * jax.nn.sigmoid(gate) * up_ref[...].astype(F32)
    factors.append(mm(proj_hid_ref[...], hidden.astype(BF16)))
    factors = jnp.concatenate(factors, axis=0)
    share = factors.shape[1] // NX
    for x in range(NX):
        own = [grad[k * share : (k + 1) * share] for k in (x % 2, x % 2 + 2)]
        sent_ref[x] = jnp.concatenate([*own, *halves(factors[:, x * share : (x + 1) * share])], axis=0)


def lend_kernel(w_hbm, gate_ref, up_ref, gate_proj, up_proj, lent_ref, sems):
    _, _, own, core = place()
    rows, features = lent_ref.shape[0], w_hbm.shape[1]
    half = gate_ref.shape[1] // 2
    copies = fetch([(w_hbm.at[span(core, rows)], lent_ref.at[:, :features])], sems)
    proj = jnp.concatenate([gate_proj[...], up_proj[...]], axis=0).astype(F32).T.astype(BF16)
    gate, up = quarters(gate_ref, 1 - own), quarters(up_ref, 1 - own)
    for k in range(2):
        part, first = slice(k * rows, (k + 1) * rows), features + k * (lent_ref.shape[1] - features) // 2
        lent_ref[:, first : first + half] = gate[part]
        lent_ref[:, first + half : first + 2 * half] = up[part]
        lent_ref[:, first + 2 * half : first + 2 * half + proj.shape[1]] = proj[part]
    wait(copies)


def split_kernel(got_ref, block_ref, both_ref):
    deep = both_ref.shape[0]
    tokens = got_ref.shape[1] - 2 * deep
    both = got_ref[:, tokens : tokens + deep].astype(F32) + got_ref[:, tokens + deep :].astype(F32)
    both = jnp.sum(both, axis=0)
    both_ref[...] = both
    block_ref[:, :tokens] = got_ref[:, :tokens]
    block_ref[:, tokens:] = jnp.concatenate(halves(both), axis=0).reshape(NX, -1, both.shape[1])


def slopes(gate, up):
    sigmoid = jax.nn.sigmoid(gate)
    return gate * sigmoid, up * (sigmoid * (1.0 + gate * (1.0 - sigmoid)))


def hidden_kernel(gate_ref, up_ref, activated_ref, slope_ref):
    _, _, own, _ = place()
    gate, up = quarters(gate_ref, own), quarters(up_ref, own)
    activated_ref[...], slope_ref[...] = slopes(gate.T.astype(F32), up.T.astype(F32))


def lent_kernel(features, lent_ref, activated_ref, slope_ref, proj_ref):
    _, _, _, core = place()
    half, wide = activated_ref.shape[0], (lent_ref.shape[1] - features) // 2
    parts = [lent_ref[:, pl.ds(pl.multiple_of(features + k * wide, 128), wide)] for k in (core, 1 - core)]
    lent = jnp.concatenate(parts, axis=0)
    gate = lent[:, :half].T.astype(F32)
    up = lent[:, half : 2 * half].T.astype(F32)
    activated_ref[...], slope_ref[...] = slopes(gate, up)
    proj_ref[...] = lent[:, 2 * half :]


def masked(value, ids, member=True):
    count, tokens = value.shape
    member = member & (ids == lax.broadcasted_iota(jnp.int32, (SEQ_DEV, tokens), 0))
    spread = jnp.where(member[None], value[:, None, :], 0.0)
    return halves(spread.reshape(count * SEQ_DEV, tokens))


def left_kernel(own_ref, other_ref, ids_ref, high_ref, low_ref):
    x_pos, _, parity, _ = place()
    first = x_pos < 2
    own, other = own_ref[...], other_ref[...]
    left = jnp.concatenate([jnp.where(first, own, other), jnp.where(first, other, own)], axis=1)
    high_ref[...], low_ref[...] = masked(left, quarters(ids_ref, parity))


def put(grad_ref, block_ref, step):
    _, z_pos, _, _ = place()
    tokens, width = grad_ref.shape[0], block_ref.shape[2]
    came = lax.rem(z_pos + (NZ - step), NZ)
    for x in range(block_ref.shape[0]):
        grad_ref[:, span(x * NZ + came, width)] = block_ref[x, :tokens]


def first_kernel(block_ref, grad_ref):
    put(grad_ref, block_ref, 0)


def add_parts(both, block_ref, tokens):
    deep = both.shape[0]
    parts = jnp.concatenate([block_ref[x, tokens:] for x in range(NX)], axis=0).astype(F32)
    return both + (parts[:deep] + parts[deep:])


def pair_kernel(step, up_ref, down_ref, grad_in, both_in, grad_ref, both_ref):
    tokens = grad_ref.shape[0]
    put(grad_ref, up_ref, step)
    put(grad_ref, down_ref, -step)
    both_ref[...] = add_parts(add_parts(both_in[...], up_ref, tokens), down_ref, tokens)


def far_kernel(block_ref, grad_in, both_ref, ids_ref, grad_ref, in_ref, down_ref):
    tokens, rank = grad_ref.shape[0], in_ref.shape[0]
    x_pos, z_pos, _, _ = place()
    put(grad_ref, block_ref, NZ // 2)
    both = add_parts(both_ref[...], block_ref, tokens)
    share = both.shape[1]
    in_ref[...] = both[:rank]
    own = lax.div(lax.broadcasted_iota(jnp.int32, (SEQ_DEV, share), 1), share // NZ) == z_pos
    high, low = masked(both[2 * rank :], ids_ref[:, span(x_pos, share)], own)
    right_high, right_low = halves(both[rank : 2 * rank])
    product = mm_nt(high, jnp.concatenate([right_high, right_low], axis=0))
    product = product[:, :rank] + product[:, rank:] + mm_nt(low, right_high)
    product = product.reshape(rank // 2, 2, SEQ_DEV, rank)
    down_ref[...] = jnp.concatenate([product[:, 0], product[:, 1]], axis=2)


def add_pair(step, up, down, grad, both):
    return call(
        lambda *refs: pair_kernel(step, *refs),
        (jax.ShapeDtypeStruct(grad.shape, BF16), jax.ShapeDtypeStruct(both.shape, F32)),
        [VMEM] * 4,
        (up, down, grad, both),
        2 * up.size,
        {2: 0, 3: 1},
    )


def own_kernel(grad_ref, w_ref, activated_ref, slope_ref, gate_proj, up_proj, out_ref):
    hidden_grad = mm_nt(grad_ref[...], w_ref[...])
    gate_grad = (hidden_grad * slope_ref[...]).astype(BF16)
    upward_grad = (hidden_grad * activated_ref[...]).astype(BF16)
    out_ref[...] = jnp.concatenate(
        [mm_nt(gate_grad, gate_proj[...]), mm_nt(upward_grad, up_proj[...])], axis=1
    )


def partner_kernel(grad_ref, near_w, far_w, activated_ref, slope_ref, proj_ref, own_ref, out_ref):
    grad = grad_ref[...]
    wide = grad.shape[1]
    hidden_grad = jnp.concatenate([mm_nt(grad, near_w[:, :wide]), mm_nt(grad, far_w[:, :wide])], axis=1)
    gate_grad = (hidden_grad * slope_ref[...]).astype(BF16)
    upward_grad = (hidden_grad * activated_ref[...]).astype(BF16)
    rank = proj_ref.shape[1] // 2
    lent = jnp.concatenate(
        [mm(gate_grad, proj_ref[:, :rank]), mm(upward_grad, proj_ref[:, rank:])], axis=1
    )
    out_ref[...] = own_ref[...] + lent


def last_kernel(total_ref, high_ref, low_ref, down_ref, sent_ref):
    total = total_ref[...]
    high, low = halves(total)
    product = mm(high_ref[...], jnp.concatenate([high, low], axis=1))
    wide = total.shape[1]
    product = product[:, :wide] + product[:, wide:] + mm(low_ref[...], high)
    devices = sent_ref.shape[0]
    sent_ref[:, : 2 * SEQ_DEV] = product.reshape(devices, 2 * SEQ_DEV, wide)
    sent_ref[:, 2 * SEQ_DEV :] = down_ref[...]


def per_device(
    layer_input,
    gate_pre,
    up_pre,
    out_grad,
    w_down,
    proj_input,
    proj_hidden,
    proj_gate,
    proj_upward,
    proj_output,
    seq_ids,
):
    tokens, width = out_grad.shape
    half = tokens // 2
    hidden, features = w_down.shape
    rank = proj_input.shape[1]
    mp_size = lax.axis_size("mp")
    dp_size = lax.axis_size("dp")
    cores = [(k, k ^ 1) for k in range(dp_size)]

    def shape(dims, dtype=F32):
        return jax.ShapeDtypeStruct(dims, dtype)

    gate_turned, up_turned = gate_pre.T, up_pre.T
    deep, share = 3 * rank, tokens // NX
    sent = call(
        start_kernel,
        shape((NX, half + 2 * deep, width), BF16),
        [HBM] * 7,
        (layer_input, out_grad, gate_turned, up_turned, proj_input.T, proj_output, proj_hidden.T),
        4 * tokens * width * rank + 2 * tokens * hidden * rank,
        scratch=[
            pltpu.VMEM((tokens, width), BF16),
            pltpu.VMEM((tokens, width), BF16),
            pltpu.VMEM((hidden, tokens), BF16),
            pltpu.VMEM((hidden, tokens), BF16),
            pltpu.VMEM((rank, width), BF16),
            pltpu.VMEM((rank, width), BF16),
            pltpu.VMEM((rank, hidden), BF16),
            pltpu.SemaphoreType.DMA((7,)),
        ],
        vmem=56,
    )
    lent_w = tie(w_down, sent)
    lent = call(
        lend_kernel,
        shape((hidden // 2, features + 2 * (tokens + 2 * rank)), BF16),
        [HBM] + [VMEM] * 4,
        (lent_w, gate_turned, up_turned, proj_gate.T, proj_upward.T),
        w_down.size,
        scratch=[pltpu.SemaphoreType.DMA((1,))],
    )
    got = lax.all_to_all(sent, "mp", 0, 0, axis_index_groups=X_GROUPS)
    got, lent = lax.optimization_barrier((got, lent))
    near = lax.ppermute(lent, "mp", PARTNER)
    block, both = call(
        split_kernel,
        (
            shape((NX, half + 2 * deep // NX, width), BF16),
            shape((deep, share)),
        ),
        [VMEM],
        (got,),
        got.size,
    )

    up = down = block
    next_up, next_down = lax.ppermute(up, "mp", z_shift(1)), lax.ppermute(down, "mp", z_shift(-1))
    grad = call(first_kernel, shape((half, features), BF16), [VMEM], (block,), block.size)
    next_up = tie(next_up, grad)

    up, down = next_up, next_down
    next_up, next_down = lax.ppermute(up, "mp", z_shift(1)), lax.ppermute(down, "mp", z_shift(-1))
    grad, both = add_pair(1, up, down, grad, both)
    activated, slope = call(
        hidden_kernel,
        (shape((half, hidden)), shape((half, hidden))),
        [VMEM] * 2,
        (gate_turned, up_turned),
        gate_pre.size,
    )
    next_up = tie(next_up, grad, slope)

    up, down = next_up, next_down
    next_up, next_down = lax.ppermute(up, "mp", z_shift(1)), lax.ppermute(down, "mp", z_shift(-1))
    grad, both = add_pair(2, up, down, grad, both)
    next_up = tie(next_up, grad)

    up, down = lax.optimization_barrier((next_up, next_down))
    far = lax.ppermute(up, "mp", z_shift(1))
    grad, both = add_pair(3, up, down, grad, both)
    grad, in_factor, down_raw = call(
        far_kernel,
        (shape(grad.shape, BF16), shape((rank, share)), shape((mp_size, SEQ_DEV, 2 * rank))),
        [VMEM] * 4,
        (far, grad, both, seq_ids),
        far.size,
        {1: 0},
    )
    other_factor = lax.ppermute(in_factor, "mp", OPPOSITE)
    own_factors = call(
        own_kernel,
        shape((half, 2 * rank)),
        [VMEM] * 6,
        (grad, w_down, activated, slope, proj_gate.T, proj_upward.T),
        2 * half * hidden * features,
    )
    near, other_factor, own_factors = lax.optimization_barrier((near, other_factor, own_factors))
    other = lax.ppermute(near, "dp", cores)
    lent_activated, lent_slope, lent_proj = call(
        lambda *refs: lent_kernel(features, *refs),
        (shape((half, hidden)), shape((half, hidden)), shape((hidden, 2 * rank), BF16)),
        [VMEM],
        (near,),
        lent.size,
    )
    high, low = call(
        left_kernel,
        (shape((rank * SEQ_DEV, half), BF16), shape((rank * SEQ_DEV, half), BF16)),
        [VMEM] * 3,
        (in_factor, other_factor, seq_ids),
        SEQ_DEV * half * rank,
    )
    total = call(
        partner_kernel,
        shape(own_factors.shape),
        [VMEM] * 7,
        (grad, near, other, lent_activated, lent_slope, lent_proj, own_factors),
        2 * half * hidden * features,
    )
    sent = call(
        last_kernel,
        shape((mp_size, 3 * SEQ_DEV, 2 * rank)),
        [VMEM] * 4,
        (total, high, low, down_raw),
        6 * high.size * rank,
    )
    got = jnp.sum(lax.all_to_all(sent, "mp", 0, 0), axis=0)
    paired, down_raw = got[: 2 * SEQ_DEV], got[2 * SEQ_DEV :]
    paired = paired.reshape(2, SEQ_DEV, 2, rank).transpose(1, 2, 0, 3).reshape(SEQ_DEV, 2, 2 * rank)
    raw = jnp.concatenate([paired, down_raw[:, None]], axis=1)

    squares = jnp.sum(raw * raw, axis=(0, 2))
    squares = jnp.pad(squares, (0, 125)).reshape(1, 1, 128)
    for axis, size in (("mp", mp_size), ("dp", dp_size)):
        squares = jnp.sum(
            lax.all_to_all(jnp.broadcast_to(squares, (size, 1, 128)), axis, 0, 0), axis=0, keepdims=True
        )
    entries = SEQ_DEV * dp_size * rank * rank
    scale = lax.rsqrt(squares[0, 0, :3] / entries + 1e-06)
    return raw * scale[None, :, None]


def solution(mesh):
    in_specs = (
        P("dp", "mp"),
        P("dp", "mp"),
        P("dp", "mp"),
        P("dp", "mp"),
        P("mp", None),
        P("mp", None),
        P("mp", None),
        P("mp", None),
        P("mp", None),
        P(None, "mp"),
        P("dp", None),
    )
    out_specs = P("dp", None, "mp")
    return jax.shard_map(
        per_device, mesh=mesh, in_specs=in_specs, out_specs=out_specs, check_vma=False
    )
```

time: 141 us -> 141 us (level)
  waiting for transfers between devices: 19.3 us -> 28.1 us
  blocking collectives: 57.7 us -> 49.8 us
  starting transfers between devices: 44.4 us -> 49.6 us
  local copies, waits for them, and re-layouts: 8.86 us -> 3.7 us
    ppermute x3 -> x4, waiting for transfers between devices: 0.01 us -> 12.3 us  [the longest x1 7.69 us: per_device(): far = lax.ppermute(up, 'mp', z_shift(1))]
    ppermute x3, waiting for transfers between devices: 19.2 us -> 10.4 us  [per_device(): lax.ppermute(up, 'mp', z_shift(1))]
    ppermute x3 -> x4, starting transfers between devices: 10.9 us -> 16.8 us  [the longest x1 9.05 us: per_device(): other = lax.ppermute(near, 'dp', cores)]
    unnamed x34 -> x16, local copies, waits for them, and re-layouts: 8.66 us -> 3.49 us
    all_to_all x2, blocking collectives: 36.9 us -> 32.4 us  [per_device(): lax.all_to_all(jnp.broadcast_to(squares, (size, 1, 128)), axis, 0, 0)]
    all_to_all x1, waiting for transfers between devices: 0.14 us -> 3.87 us  [per_device(): got = lax.all_to_all(sent, 'mp', 0, 0, axis_index_groups=X_GROUPS)]
    all_to_all x2 -> x1, blocking collectives: 20.8 us -> 17.4 us  [per_device(): got = jnp.sum(lax.all_to_all(sent, 'mp', 0, 0), axis=0)]
    ppermute x3, waiting for transfers between devices: 0.01 us -> 1.49 us  [per_device(): lax.ppermute(down, 'mp', z_shift(-1))]
  transfers between devices with their start and end apart: 10 -> 11, of which waited for: 4 -> 8; matrix products, arithmetic and copies ran while one was open for 0% -> 0% of each run, Pallas kernels for 4% -> 3%
where the time goes in v4:
time: 141 us
  blocking collectives  49.8 us (35%)
  starting transfers between devices  49.6 us (35%)
  waiting for transfers between devices  28.1 us (20%)
  Pallas kernels  8.33 us (6%)
  local copies, waits for them, and re-layouts  3.7 us (3%)
    all_to_all x2, blocking collectives, per_device(): lax.all_to_all(jnp.broadcast_to(squares, (size, 1, 128)), axis, 0, 0)  32.4 us
    ppermute x3, starting transfers between devices, per_device(): lax.ppermute(down, 'mp', z_shift(-1))  17.7 us
    all_to_all x1, blocking collectives, per_device(): got = jnp.sum(lax.all_to_all(sent, 'mp', 0, 0), axis=0)  17.4 us
    ppermute x3, waiting for transfers between devices, per_device(): lax.ppermute(up, 'mp', z_shift(1))  10.4 us
    ppermute x3, starting transfers between devices, per_device(): lax.ppermute(up, 'mp', z_shift(1))  10.2 us
    ppermute x1, starting transfers between devices, per_device(): other = lax.ppermute(near, 'dp', cores)  9.05 us
    pallas_call x14, Pallas kernels, call(): pl.pallas_call(kernel, out_shape=out_shape, in_specs=specs, out_specs=out...  8.33 us
    ppermute x1, waiting for transfers between devices, per_device(): far = lax.ppermute(up, 'mp', z_shift(1))  7.69 us
  transfers between devices with their start and end apart: 11, of which 8 were waited for; matrix products, arithmetic and copies ran while one was open for 0% of the time, Pallas kernels for 3%

profile of v4, /device:TPU:1, one launch (start us, length us, event | category | flops | bytes accessed | tf_op | source)
XLA Modules:
  0.0 140.6 jit_solution(10813489563488094474)
XLA Ops:
  0.0 0.0 copy-start.2
  0.0 0.0 copy-start.3
  0.0 0.0 copy-start.5
  0.0 0.0 copy-start.6
  0.0 2.7 %shard_map.109 = bf16[4,640,128]{2,1,0:T(8,128)(2,1)} custom-call(bf16[512,128]{1,0:T(8,128)(2,1)} %input_hbm.1, bf16[512,128]{1,0:T(8,128)(2,1)} %grad_hbm.1, bf16[448,512]{1,0:T(8,128)(2,1)} %bitcast.16, bf16[448,512]{1,0:T(8,128)(2,1)} %bitcast.19, bf16[64,128]{1,0:T(8,128)(2,1)} %bitcast.30, bf16[64,128]{1,0:T(8,128)(2,1)} %proj_out_hbm.1, ...), custom_call_target="tpu_custom_call" | custom-call | flops 46137344 | bytes 1269760 | tf_op jit(solution)/shard_map/pallas_call | solution.py:60
  2.7 4.9 %all-to-all-start = ((bf16[4,640,128]{2,1,0:T(8,128)(2,1)}), bf16[4,640,128]{2,1,0:T(8,128)(2,1)S(1)}, u32[]{:S(2)}, u32[]{:S(2)}) async-start(bf16[4,640,128]{2,1,0:T(8,128)(2,1)} %shard_map.109), calls=%async_computation | async-start | bytes 1310720 | tf_op jit(solution)/shard_map/all_to_all | solution.py:314
  7.5 0.0 copy-done.2
  7.5 0.0 copy-done.3
  7.5 0.0 copy-done.5
  7.6 0.0 copy-done.6
  7.6 0.0 copy-start
  7.6 2.0 %copy-done = bf16[448,4096]{1,0:T(8,128)(2,1)S(1)} copy-done((bf16[448,4096]{1,0:T(8,128)(2,1)S(1)}, bf16[448,4096]{1,0:T(8,128)(2,1)}, u32[]{:S(2)}) %copy-start) | copy-done | bytes 3670040
  9.6 0.3 shard_map.110
  9.9 0.0 copy-start.4
  9.9 1.4 %copy-done.4 = bf16[224,5376]{1,0:T(8,128)(2,1)} copy-done((bf16[224,5376]{1,0:T(8,128)(2,1)}, bf16[224,5376]{1,0:T(8,128)(2,1)S(1)}, u32[]{:S(2)}) %copy-start.4) | copy-done | bytes 2408472
  11.3 3.9 %all-to-all-done.got_ref = bf16[4,640,128]{2,1,0:T(8,128)(2,1)S(1)} async-done(((bf16[4,640,128]{2,1,0:T(8,128)(2,1)}), bf16[4,640,128]{2,1,0:T(8,128)(2,1)S(1)}, u32[]{:S(2)}, u32[]{:S(2)}) %all-to-all-start) | async-done | bytes 655392 | tf_op jit(solution)/shard_map/all_to_all | solution.py:314
  15.2 2.2 %collective-permute-start.7 = (bf16[224,5376]{1,0:T(8,128)(2,1)}, bf16[224,5376]{1,0:T(8,128)(2,1)S(1)}, u32[]{:S(2)}, u32[]{:S(2)}) collective-permute-start(bf16[224,5376]{1,0:T(8,128)(2,1)} %copy-done.4), channel_id=1, source_target_pairs={{0,8},{1,9},{2,10},{3,11},{4,12},{5,13},{6,14},{7,15},{8,0},{9,1},... | collective-permute-start | bytes 7225352 | tf_op jit(solution)/shard_map/ppermute | solution.py:316
  17.4 0.1 shard_map.111
  17.4 6.3 %collective-permute-start = (bf16[4,352,128]{2,1,0:T(8,128)(2,1)S(1)}, bf16[4,352,128]{2,1,0:T(8,128)(2,1)S(1)}, u32[]{:S(2)}, u32[]{:S(2)}) collective-permute-start(bf16[4,352,128]{2,1,0:T(8,128)(2,1)S(1)} %get-tuple-element.36.block_ref), channel_id=1, source_target_pairs={{0,1},{1,2},{2,3},{3,4},{4,5},{5,6},{6,7},{7,0},{8,9},{9,10},{10,1... | collective-permute-start | bytes 1081352 | tf_op jit(solution)/shard_map/ppermute | solution.py:329
  23.8 8.6 %collective-permute-start.2 = (bf16[4,352,128]{2,1,0:T(8,128)(2,1)S(1)}, bf16[4,352,128]{2,1,0:T(8,128)(2,1)S(1)}, u32[]{:S(2)}, u32[]{:S(2)}) collective-permute-start(bf16[4,352,128]{2,1,0:T(8,128)(2,1)S(1)} %get-tuple-element.36.block_ref), channel_id=1, source_target_pairs={{0,7},{1,0},{2,1},{3,2},{4,3},{5,4},{6,5},{7,6},{8,15},{9,8},{10,9... | collective-permute-start | bytes 1081352 | tf_op jit(solution)/shard_map/ppermute | solution.py:329
  32.4 0.1 shard_map.112.refs_2_
  32.5 4.6 %collective-permute-done.refs_0_ = bf16[4,352,128]{2,1,0:T(8,128)(2,1)S(1)} collective-permute-done((bf16[4,352,128]{2,1,0:T(8,128)(2,1)S(1)}, bf16[4,352,128]{2,1,0:T(8,128)(2,1)S(1)}, u32[]{:S(2)}, u32[]{:S(2)}) %collective-permute-start) | collective-permute-done | bytes 360480 | tf_op jit(solution)/shard_map/ppermute | solution.py:329
  37.0 1.9 %collective-permute-start.1 = (bf16[4,352,128]{2,1,0:T(8,128)(2,1)S(1)}, bf16[4,352,128]{2,1,0:T(8,128)(2,1)S(1)}, u32[]{:S(2)}, u32[]{:S(2)}) collective-permute-start(bf16[4,352,128]{2,1,0:T(8,128)(2,1)S(1)} %collective-permute-done.refs_0_), channel_id=1, source_target_pairs={{0,1},{1,2},{2,3},{3,4},{4,5},{5,6},{6,7},{7,0},{8,9},{9,10},{10,1... | collective-permute-start | bytes 1081352 | tf_op jit(solution)/shard_map/ppermute | solution.py:334
  38.9 0.0 collective-permute-done.2.refs_1_
  38.9 4.6 %collective-permute-start.4 = (bf16[4,352,128]{2,1,0:T(8,128)(2,1)S(1)}, bf16[4,352,128]{2,1,0:T(8,128)(2,1)S(1)}, u32[]{:S(2)}, u32[]{:S(2)}) collective-permute-start(bf16[4,352,128]{2,1,0:T(8,128)(2,1)S(1)} %collective-permute-done.2.refs_1_), channel_id=1, source_target_pairs={{0,7},{1,0},{2,1},{3,2},{4,3},{5,4},{6,5},{7,6},{8,15},{9,8},{10,9... | collective-permute-start | bytes 1081352 | tf_op jit(solution)/shard_map/ppermute | solution.py:334
  43.5 0.3 shard_map.114
  43.8 0.2 shard_map.113
  44.0 3.2 %collective-permute-done.1.refs_0_ = bf16[4,352,128]{2,1,0:T(8,128)(2,1)S(1)} collective-permute-done((bf16[4,352,128]{2,1,0:T(8,128)(2,1)S(1)}, bf16[4,352,128]{2,1,0:T(8,128)(2,1)S(1)}, u32[]{:S(2)}, u32[]{:S(2)}) %collective-permute-start.1) | collective-permute-done | bytes 360480 | tf_op jit(solution)/shard_map/ppermute | solution.py:334
  47.2 1.9 %collective-permute-start.3 = (bf16[4,352,128]{2,1,0:T(8,128)(2,1)S(1)}, bf16[4,352,128]{2,1,0:T(8,128)(2,1)S(1)}, u32[]{:S(2)}, u32[]{:S(2)}) collective-permute-start(bf16[4,352,128]{2,1,0:T(8,128)(2,1)S(1)} %collective-permute-done.1.refs_0_), channel_id=1, source_target_pairs={{0,1},{1,2},{2,3},{3,4},{4,5},{5,6},{6,7},{7,0},{8,9},{9,10},{10,1... | collective-permute-start | bytes 1081352 | tf_op jit(solution)/shard_map/ppermute | solution.py:346
  49.1 0.0 collective-permute-done.4.refs_1_
  49.2 4.6 %collective-permute-start.5 = (bf16[4,352,128]{2,1,0:T(8,128)(2,1)S(1)}, bf16[4,352,128]{2,1,0:T(8,128)(2,1)S(1)}, u32[]{:S(2)}, u32[]{:S(2)}) collective-permute-start(bf16[4,352,128]{2,1,0:T(8,128)(2,1)S(1)} %collective-permute-done.4.refs_1_), channel_id=1, source_target_pairs={{0,7},{1,0},{2,1},{3,2},{4,3},{5,4},{6,5},{7,6},{8,15},{9,8},{10,9... | collective-permute-start | bytes 1081352 | tf_op jit(solution)/shard_map/ppermute | solution.py:346
  53.7 0.2 shard_map.115
  53.9 0.0 copy-start.7
  54.0 2.6 %collective-permute-done.3.refs_0_ = bf16[4,352,128]{2,1,0:T(8,128)(2,1)S(1)} collective-permute-done((bf16[4,352,128]{2,1,0:T(8,128)(2,1)S(1)}, bf16[4,352,128]{2,1,0:T(8,128)(2,1)S(1)}, u32[]{:S(2)}, u32[]{:S(2)}) %collective-permute-start.3) | collective-permute-done | bytes 360480 | tf_op jit(solution)/shard_map/ppermute | solution.py:346
  56.6 1.5 %collective-permute-done.5.refs_1_ = bf16[4,352,128]{2,1,0:T(8,128)(2,1)S(1)} collective-permute-done((bf16[4,352,128]{2,1,0:T(8,128)(2,1)S(1)}, bf16[4,352,128]{2,1,0:T(8,128)(2,1)S(1)}, u32[]{:S(2)}, u32[]{:S(2)}) %collective-permute-start.5) | collective-permute-done | bytes 360480 | tf_op jit(solution)/shard_map/ppermute | solution.py:346
  58.1 1.9 %collective-permute-start.6 = (bf16[4,352,128]{2,1,0:T(8,128)(2,1)S(1)}, bf16[4,352,128]{2,1,0:T(8,128)(2,1)S(1)}, u32[]{:S(2)}, u32[]{:S(2)}) collective-permute-start(bf16[4,352,128]{2,1,0:T(8,128)(2,1)S(1)} %collective-permute-done.3.refs_0_), channel_id=1, source_target_pairs={{0,1},{1,2},{2,3},{3,4},{4,5},{5,6},{6,7},{7,0},{8,9},{9,10},{10,1... | collective-permute-start | bytes 1081352 | tf_op jit(solution)/shard_map/ppermute | solution.py:351
  60.0 0.0 copy-start.1
  60.0 0.2 shard_map.116
  60.2 7.7 %collective-permute-done.6.block_ref = bf16[4,352,128]{2,1,0:T(8,128)(2,1)S(1)} collective-permute-done((bf16[4,352,128]{2,1,0:T(8,128)(2,1)S(1)}, bf16[4,352,128]{2,1,0:T(8,128)(2,1)S(1)}, u32[]{:S(2)}, u32[]{:S(2)}) %collective-permute-start.6) | collective-permute-done | bytes 360480 | tf_op jit(solution)/shard_map/ppermute | solution.py:351
  67.9 0.0 copy-done.7
  67.9 0.5 shard_map.117
  68.4 3.7 %collective-permute-start.8 = (f32[64,128]{1,0:T(8,128)S(1)}, f32[64,128]{1,0:T(8,128)S(1)}, u32[]{:S(2)}, u32[]{:S(2)}) collective-permute-start(f32[64,128]{1,0:T(8,128)S(1)} %get-tuple-element.52.own_ref), channel_id=1, source_target_pairs={{0,16},{1,17},{2,18},{3,19},{4,20},{5,21},{6,22},{7,23},{8,24},{9,... | collective-permute-start | bytes 98312 | tf_op jit(solution)/shard_map/ppermute | solution.py:361
  72.1 0.0 copy-done.1
  72.1 1.6 %shard_map.118.own_ref = f32[256,128]{1,0:T(8,128)S(1)} custom-call(bf16[256,4096]{1,0:T(8,128)(2,1)S(1)} %get-tuple-element.50.grad_ref, bf16[448,4096]{1,0:T(8,128)(2,1)S(1)} %copy-done.1, f32[256,448]{1,0:T(8,128)S(1)} %get-tuple-element.53.activated_ref, f32[256,448]{1,0:T(8,128)S(1)} %get-tuple-element.40.slope_ref, bf16[64,448]{1,0:T(8,128)(2,1)S(1)} %bitcast.23, ...), custom_call_target="tpu_custom_call" | custom-call | flops 939524096 | bytes 6799360 | tf_op jit(solution)/shard_map/pallas_call | solution.py:60
  73.7 0.9 collective-permute-done.8.other_ref
  74.5 0.0 collective-permute-done.7.refs_0_.near_w
  74.5 9.1 %collective-permute-start.9 = (bf16[224,5376]{1,0:T(8,128)(2,1)S(1)}, bf16[224,5376]{1,0:T(8,128)(2,1)S(1)}, u32[]{:S(2)}, u32[]{:S(2)}) collective-permute-start(bf16[224,5376]{1,0:T(8,128)(2,1)S(1)} %collective-permute-done.7.refs_0_.near_w), channel_id=1, source_target_pairs={{0,32},{32,0},{64,96},{96,64},{128,160},{160,128},{192,224},{224,1... | collective-permute-start | bytes 7225352 | tf_op jit(solution)/shard_map/ppermute | solution.py:370
  83.6 0.1 shard_map.121
  83.7 0.3 shard_map.119
  84.1 3.8 %collective-permute-done.9.far_w = bf16[224,5376]{1,0:T(8,128)(2,1)S(1)} collective-permute-done((bf16[224,5376]{1,0:T(8,128)(2,1)S(1)}, bf16[224,5376]{1,0:T(8,128)(2,1)S(1)}, u32[]{:S(2)}, u32[]{:S(2)}) %collective-permute-start.9) | collective-permute-done | bytes 2408480 | tf_op jit(solution)/shard_map/ppermute | solution.py:370
  87.8 1.6 %shard_map.120.total_ref = f32[256,128]{1,0:T(8,128)S(1)} custom-call(bf16[256,4096]{1,0:T(8,128)(2,1)S(1)} %get-tuple-element.50.grad_ref, bf16[224,5376]{1,0:T(8,128)(2,1)S(1)} %collective-permute-done.7.refs_0_.near_w, bf16[224,5376]{1,0:T(8,128)(2,1)S(1)} %collective-permute-done.9.far_w, f32[256,448]{1,0:T(8,128)S(1)} %get-tuple-element.55.activated_ref, ...), custom_call_target="tpu_custom_call" | custom-call | flops 939524096 | bytes 8077312 | tf_op jit(solution)/shard_map/pallas_call | solution.py:60
  89.4 0.3 shard_map.122
  89.8 17.4 %all_to_all.20 = f32[32,24,128]{2,1,0:T(8,128)S(1)} all-to-all(f32[32,24,128]{2,1,0:T(8,128)S(1)} %shard_map.122), channel_id=1, replica_groups=mesh['dp'=16,'mp'=32] {'mp'}, dimensions={0} | all-to-all | bytes 786432 | tf_op jit(solution)/shard_map/all_to_all | solution.py:399
  107.2 0.1 reshape.29
  107.3 0.1 reshape.30
  107.4 0.1 multiply_reduce_fusion
  107.5 16.0 %all_to_all.21 = f32[32,1,128]{2,1,0:T(1,128)S(1)} all-to-all(f32[32,1,128]{2,1,0:T(1,128)S(1)} %broadcast_in_dim.9), channel_id=1, replica_groups=mesh['dp'=16,'mp'=32] {'mp'}, dimensions={0} | all-to-all | bytes 32768 | tf_op jit(solution)/shard_map/all_to_all | solution.py:408
  123.6 16.3 %all_to_all.22 = f32[16,1,128]{2,1,0:T(1,128)S(1)} all-to-all(f32[16,1,128]{2,1,0:T(1,128)S(1)} %broadcast_in_dim.20), channel_id=1, replica_groups=mesh['dp'=16,'mp'=32] {'dp'}, dimensions={0} | all-to-all | bytes 16384 | tf_op jit(solution)/shard_map/all_to_all | solution.py:408
  140.0 0.7 fusion
  (10 shorter events, 0.1 us)
Async XLA Ops:
  0.0 7.5 %copy-start.2 = (bf16[512,448]{0,1:T(8,128)(2,1)S(1)}, bf16[512,448]{0,1:T(8,128)(2,1)}, u32[]{:S(2)}) copy-start(bf16[512,448]{0,1:T(8,128)(2,1)} %param.12) | copy-start | bytes 1376260
  0.0 7.5 %copy-start.3 = (bf16[512,448]{0,1:T(8,128)(2,1)S(1)}, bf16[512,448]{0,1:T(8,128)(2,1)}, u32[]{:S(2)}) copy-start(bf16[512,448]{0,1:T(8,128)(2,1)} %param.13) | copy-start | bytes 1376260
  0.0 7.5 %copy-start.5 = (bf16[448,64]{0,1:T(8,128)(2,1)S(1)}, bf16[448,64]{0,1:T(8,128)(2,1)}, u32[]{:S(2)}) copy-start(bf16[448,64]{0,1:T(8,128)(2,1)} %param.18) | copy-start | bytes 172036
  0.0 7.5 %copy-start.6 = (bf16[448,64]{0,1:T(8,128)(2,1)S(1)}, bf16[448,64]{0,1:T(8,128)(2,1)}, u32[]{:S(2)}) copy-start(bf16[448,64]{0,1:T(8,128)(2,1)} %param.19) | copy-start | bytes 172036
  2.7 12.5 %all-to-all-start = ((bf16[4,640,128]{2,1,0:T(8,128)(2,1)}), bf16[4,640,128]{2,1,0:T(8,128)(2,1)S(1)}, u32[]{:S(2)}, u32[]{:S(2)}) async-start(bf16[4,640,128]{2,1,0:T(8,128)(2,1)} %shard_map.109), calls=%async_computation | async-start | bytes 1310720 | tf_op jit(solution)/shard_map/all_to_all | solution.py:314
  7.6 2.0 %copy-start = (bf16[448,4096]{1,0:T(8,128)(2,1)S(1)}, bf16[448,4096]{1,0:T(8,128)(2,1)}, u32[]{:S(2)}) copy-start(bf16[448,4096]{1,0:T(8,128)(2,1)} %w_ref.1) | copy-start | bytes 11010052
  9.9 1.4 %copy-start.4 = (bf16[224,5376]{1,0:T(8,128)(2,1)}, bf16[224,5376]{1,0:T(8,128)(2,1)S(1)}, u32[]{:S(2)}) copy-start(bf16[224,5376]{1,0:T(8,128)(2,1)S(1)} %shard_map.110) | copy-start | bytes 7225348
  15.2 59.4 %collective-permute-start.7 = (bf16[224,5376]{1,0:T(8,128)(2,1)}, bf16[224,5376]{1,0:T(8,128)(2,1)S(1)}, u32[]{:S(2)}, u32[]{:S(2)}) collective-permute-start(bf16[224,5376]{1,0:T(8,128)(2,1)} %copy-done.4), channel_id=1, source_target_pairs={{0,8},{1,9},{2,10},{3,11},{4,12},{5,13},{6,14},{7,15},{8,0},{9,1},... | collective-permute-start | bytes 7225352 | tf_op jit(solution)/shard_map/ppermute | solution.py:316
  17.4 19.6 %collective-permute-start = (bf16[4,352,128]{2,1,0:T(8,128)(2,1)S(1)}, bf16[4,352,128]{2,1,0:T(8,128)(2,1)S(1)}, u32[]{:S(2)}, u32[]{:S(2)}) collective-permute-start(bf16[4,352,128]{2,1,0:T(8,128)(2,1)S(1)} %get-tuple-element.36.block_ref), channel_id=1, source_target_pairs={{0,1},{1,2},{2,3},{3,4},{4,5},{5,6},{6,7},{7,0},{8,9},{9,10},{10,1... | collective-permute-start | bytes 1081352 | tf_op jit(solution)/shard_map/ppermute | solution.py:329
  23.8 15.2 %collective-permute-start.2 = (bf16[4,352,128]{2,1,0:T(8,128)(2,1)S(1)}, bf16[4,352,128]{2,1,0:T(8,128)(2,1)S(1)}, u32[]{:S(2)}, u32[]{:S(2)}) collective-permute-start(bf16[4,352,128]{2,1,0:T(8,128)(2,1)S(1)} %get-tuple-element.36.block_ref), channel_id=1, source_target_pairs={{0,7},{1,0},{2,1},{3,2},{4,3},{5,4},{6,5},{7,6},{8,15},{9,8},{10,9... | collective-permute-start | bytes 1081352 | tf_op jit(solution)/shard_map/ppermute | solution.py:329
  37.0 10.2 %collective-permute-start.1 = (bf16[4,352,128]{2,1,0:T(8,128)(2,1)S(1)}, bf16[4,352,128]{2,1,0:T(8,128)(2,1)S(1)}, u32[]{:S(2)}, u32[]{:S(2)}) collective-permute-start(bf16[4,352,128]{2,1,0:T(8,128)(2,1)S(1)} %collective-permute-done.refs_0_), channel_id=1, source_target_pairs={{0,1},{1,2},{2,3},{3,4},{4,5},{5,6},{6,7},{7,0},{8,9},{9,10},{10,1... | collective-permute-start | bytes 1081352 | tf_op jit(solution)/shard_map/ppermute | solution.py:334
  38.9 10.2 %collective-permute-start.4 = (bf16[4,352,128]{2,1,0:T(8,128)(2,1)S(1)}, bf16[4,352,128]{2,1,0:T(8,128)(2,1)S(1)}, u32[]{:S(2)}, u32[]{:S(2)}) collective-permute-start(bf16[4,352,128]{2,1,0:T(8,128)(2,1)S(1)} %collective-permute-done.2.refs_1_), channel_id=1, source_target_pairs={{0,7},{1,0},{2,1},{3,2},{4,3},{5,4},{6,5},{7,6},{8,15},{9,8},{10,9... | collective-permute-start | bytes 1081352 | tf_op jit(solution)/shard_map/ppermute | solution.py:334
  47.2 9.4 %collective-permute-start.3 = (bf16[4,352,128]{2,1,0:T(8,128)(2,1)S(1)}, bf16[4,352,128]{2,1,0:T(8,128)(2,1)S(1)}, u32[]{:S(2)}, u32[]{:S(2)}) collective-permute-start(bf16[4,352,128]{2,1,0:T(8,128)(2,1)S(1)} %collective-permute-done.1.refs_0_), channel_id=1, source_target_pairs={{0,1},{1,2},{2,3},{3,4},{4,5},{5,6},{6,7},{7,0},{8,9},{9,10},{10,1... | collective-permute-start | bytes 1081352 | tf_op jit(solution)/shard_map/ppermute | solution.py:346
  49.2 8.9 %collective-permute-start.5 = (bf16[4,352,128]{2,1,0:T(8,128)(2,1)S(1)}, bf16[4,352,128]{2,1,0:T(8,128)(2,1)S(1)}, u32[]{:S(2)}, u32[]{:S(2)}) collective-permute-start(bf16[4,352,128]{2,1,0:T(8,128)(2,1)S(1)} %collective-permute-done.4.refs_1_), channel_id=1, source_target_pairs={{0,7},{1,0},{2,1},{3,2},{4,3},{5,4},{6,5},{7,6},{8,15},{9,8},{10,9... | collective-permute-start | bytes 1081352 | tf_op jit(solution)/shard_map/ppermute | solution.py:346
  53.9 14.0 %copy-start.7 = (s32[1,512]{1,0:T(1,128)S(1)}, s32[1,512]{1,0:T(1,128)}, u32[]{:S(2)}) copy-start(s32[1,512]{1,0:T(1,128)} %ids_ref.3) | copy-start | bytes 6148
  58.1 9.8 %collective-permute-start.6 = (bf16[4,352,128]{2,1,0:T(8,128)(2,1)S(1)}, bf16[4,352,128]{2,1,0:T(8,128)(2,1)S(1)}, u32[]{:S(2)}, u32[]{:S(2)}) collective-permute-start(bf16[4,352,128]{2,1,0:T(8,128)(2,1)S(1)} %collective-permute-done.3.refs_0_), channel_id=1, source_target_pairs={{0,1},{1,2},{2,3},{3,4},{4,5},{5,6},{6,7},{7,0},{8,9},{9,10},{10,1... | collective-permute-start | bytes 1081352 | tf_op jit(solution)/shard_map/ppermute | solution.py:351
  60.0 12.1 %copy-start.1 = (bf16[448,4096]{1,0:T(8,128)(2,1)S(1)}, bf16[448,4096]{1,0:T(8,128)(2,1)}, u32[]{:S(2)}) copy-start(bf16[448,4096]{1,0:T(8,128)(2,1)} %w_ref.1) | copy-start | bytes 11010052
  68.4 6.2 %collective-permute-start.8 = (f32[64,128]{1,0:T(8,128)S(1)}, f32[64,128]{1,0:T(8,128)S(1)}, u32[]{:S(2)}, u32[]{:S(2)}) collective-permute-start(f32[64,128]{1,0:T(8,128)S(1)} %get-tuple-element.52.own_ref), channel_id=1, source_target_pairs={{0,16},{1,17},{2,18},{3,19},{4,20},{5,21},{6,22},{7,23},{8,24},{9,... | collective-permute-start | bytes 98312 | tf_op jit(solution)/shard_map/ppermute | solution.py:361
  74.5 13.3 %collective-permute-start.9 = (bf16[224,5376]{1,0:T(8,128)(2,1)S(1)}, bf16[224,5376]{1,0:T(8,128)(2,1)S(1)}, u32[]{:S(2)}, u32[]{:S(2)}) collective-permute-start(bf16[224,5376]{1,0:T(8,128)(2,1)S(1)} %collective-permute-done.7.refs_0_.near_w), channel_id=1, source_target_pairs={{0,32},{32,0},{64,96},{96,64},{128,160},{160,128},{192,224},{224,1... | collective-permute-start | bytes 7225352 | tf_op jit(solution)/shard_map/ppermute | solution.py:370

commit v5 on v4

--- a/solution.py
+++ b/solution.py
@@ -116,24 +116,26 @@
     rows, features = lent_ref.shape[0], w_hbm.shape[1]
     half = gate_ref.shape[1] // 2
     copies = fetch([(w_hbm.at[span(core, rows)], lent_ref.at[:, :features])], sems)
-    proj = jnp.concatenate([gate_proj[...], up_proj[...]], axis=0).astype(F32).T.astype(BF16)
     gate, up = quarters(gate_ref, 1 - own), quarters(up_ref, 1 - own)
     for k in range(2):
-        part, first = slice(k * rows, (k + 1) * rows), features + k * (lent_ref.shape[1] - features) // 2
+        part, first = slice(k * rows, (k + 1) * rows), features + k * 2 * half
         lent_ref[:, first : first + half] = gate[part]
         lent_ref[:, first + half : first + 2 * half] = up[part]
-        lent_ref[:, first + 2 * half : first + 2 * half + proj.shape[1]] = proj[part]
+    proj = jnp.concatenate([gate_proj[...], up_proj[...]], axis=0).astype(F32).T.astype(BF16)
+    proj = jnp.where(core == 0, proj[:rows].astype(F32), proj[rows:].astype(F32))
+    lent_ref[:, features + 4 * half :] = proj.astype(BF16)
     wait(copies)
 
 
-def split_kernel(got_ref, block_ref, both_ref):
-    deep = both_ref.shape[0]
-    tokens = got_ref.shape[1] - 2 * deep
-    both = got_ref[:, tokens : tokens + deep].astype(F32) + got_ref[:, tokens + deep :].astype(F32)
+def split_kernel(got_ref, block_ref, both_ref, hid_ref):
+    rank, deep = hid_ref.shape[0], both_ref.shape[0]
+    tokens = got_ref.shape[1] - 2 * (deep + rank)
+    both = got_ref[:, tokens : tokens + deep + rank].astype(F32) + got_ref[:, tokens + deep + rank :].astype(F32)
     both = jnp.sum(both, axis=0)
-    both_ref[...] = both
+    both_ref[...] = both[:deep]
+    hid_ref[...] = both[deep:]
     block_ref[:, :tokens] = got_ref[:, :tokens]
-    block_ref[:, tokens:] = jnp.concatenate(halves(both), axis=0).reshape(NX, -1, both.shape[1])
+    block_ref[:, tokens:] = jnp.concatenate(halves(both[:deep]), axis=0).reshape(NX, -1, both.shape[1])
 
 
 def slopes(gate, up):
@@ -147,20 +149,18 @@
     activated_ref[...], slope_ref[...] = slopes(gate.T.astype(F32), up.T.astype(F32))
 
 
-def lent_kernel(features, lent_ref, activated_ref, slope_ref, proj_ref):
+def lent_kernel(features, lent_ref, activated_ref, slope_ref):
     _, _, _, core = place()
-    half, wide = activated_ref.shape[0], (lent_ref.shape[1] - features) // 2
-    parts = [lent_ref[:, pl.ds(pl.multiple_of(features + k * wide, 128), wide)] for k in (core, 1 - core)]
-    lent = jnp.concatenate(parts, axis=0)
-    gate = lent[:, :half].T.astype(F32)
-    up = lent[:, half : 2 * half].T.astype(F32)
+    half = activated_ref.shape[0]
+    firsts = [pl.multiple_of(features + index * 2 * half, 2 * half) for index in (core, 1 - core)]
+    lent = jnp.concatenate([lent_ref[:, pl.ds(first, 2 * half)] for first in firsts], axis=0)
+    gate, up = lent[:, :half].T.astype(F32), lent[:, half:].T.astype(F32)
     activated_ref[...], slope_ref[...] = slopes(gate, up)
-    proj_ref[...] = lent[:, 2 * half :]
-
-
-def masked(value, ids, member=True):
+
+
+def masked(value, ids):
     count, tokens = value.shape
-    member = member & (ids == lax.broadcasted_iota(jnp.int32, (SEQ_DEV, tokens), 0))
+    member = ids == lax.broadcasted_iota(jnp.int32, (SEQ_DEV, tokens), 0)
     spread = jnp.where(member[None], value[:, None, :], 0.0)
     return halves(spread.reshape(count * SEQ_DEV, tokens))
 
@@ -198,16 +198,14 @@
     both_ref[...] = add_parts(add_parts(both_in[...], up_ref, tokens), down_ref, tokens)
 
 
-def far_kernel(block_ref, grad_in, both_ref, ids_ref, grad_ref, in_ref, down_ref):
+def far_kernel(block_ref, grad_in, both_ref, hid_ref, ids_ref, grad_ref, in_ref, down_ref):
     tokens, rank = grad_ref.shape[0], in_ref.shape[0]
-    x_pos, z_pos, _, _ = place()
+    x_pos, _, _, _ = place()
     put(grad_ref, block_ref, NZ // 2)
     both = add_parts(both_ref[...], block_ref, tokens)
-    share = both.shape[1]
     in_ref[...] = both[:rank]
-    own = lax.div(lax.broadcasted_iota(jnp.int32, (SEQ_DEV, share), 1), share // NZ) == z_pos
-    high, low = masked(both[2 * rank :], ids_ref[:, span(x_pos, share)], own)
-    right_high, right_low = halves(both[rank : 2 * rank])
+    high, low = masked(hid_ref[...], ids_ref[:, span(x_pos, both.shape[1])])
+    right_high, right_low = halves(both[rank:])
     product = mm_nt(high, jnp.concatenate([right_high, right_low], axis=0))
     product = product[:, :rank] + product[:, rank:] + mm_nt(low, right_high)
     product = product.reshape(rank // 2, 2, SEQ_DEV, rank)
@@ -220,7 +218,7 @@
         (jax.ShapeDtypeStruct(grad.shape, BF16), jax.ShapeDtypeStruct(both.shape, F32)),
         [VMEM] * 4,
         (up, down, grad, both),
-        2 * up.size,
+        7000000000,
         {2: 0, 3: 1},
     )
 
@@ -234,17 +232,15 @@
     )
 
 
-def partner_kernel(grad_ref, near_w, far_w, activated_ref, slope_ref, proj_ref, own_ref, out_ref):
-    grad = grad_ref[...]
-    wide = grad.shape[1]
-    hidden_grad = jnp.concatenate([mm_nt(grad, near_w[:, :wide]), mm_nt(grad, far_w[:, :wide])], axis=1)
+def partner_kernel(grad_ref, near_ref, other_ref, activated_ref, slope_ref, own_ref, out_ref):
+    grad, lent = grad_ref[...], (near_ref, other_ref)
+    features, wide = grad.shape[1], own_ref.shape[1]
+    hidden_grad = jnp.concatenate([mm_nt(grad, part[:, :features]) for part in lent], axis=1)
     gate_grad = (hidden_grad * slope_ref[...]).astype(BF16)
     upward_grad = (hidden_grad * activated_ref[...]).astype(BF16)
-    rank = proj_ref.shape[1] // 2
-    lent = jnp.concatenate(
-        [mm(gate_grad, proj_ref[:, :rank]), mm(upward_grad, proj_ref[:, rank:])], axis=1
-    )
-    out_ref[...] = own_ref[...] + lent
+    proj = jnp.concatenate([part[:, part.shape[1] - wide :] for part in lent], axis=0)
+    factors = [mm(gate_grad, proj[:, : wide // 2]), mm(upward_grad, proj[:, wide // 2 :])]
+    out_ref[...] = own_ref[...] + jnp.concatenate(factors, axis=1)
 
 
 def last_kernel(total_ref, high_ref, low_ref, down_ref, sent_ref):
@@ -283,10 +279,10 @@
         return jax.ShapeDtypeStruct(dims, dtype)
 
     gate_turned, up_turned = gate_pre.T, up_pre.T
-    deep, share = 3 * rank, tokens // NX
+    deep, share = 2 * rank, tokens // NX
     sent = call(
         start_kernel,
-        shape((NX, half + 2 * deep, width), BF16),
+        shape((NX, half + 2 * (deep + rank), width), BF16),
         [HBM] * 7,
         (layer_input, out_grad, gate_turned, up_turned, proj_input.T, proj_output, proj_hidden.T),
         4 * tokens * width * rank + 2 * tokens * hidden * rank,
@@ -305,20 +301,21 @@
     lent_w = tie(w_down, sent)
     lent = call(
         lend_kernel,
-        shape((hidden // 2, features + 2 * (tokens + 2 * rank)), BF16),
+        shape((hidden // 2, features + 4 * half + 2 * rank), BF16),
         [HBM] + [VMEM] * 4,
         (lent_w, gate_turned, up_turned, proj_gate.T, proj_upward.T),
         w_down.size,
         scratch=[pltpu.SemaphoreType.DMA((1,))],
     )
     got = lax.all_to_all(sent, "mp", 0, 0, axis_index_groups=X_GROUPS)
-    got, lent = lax.optimization_barrier((got, lent))
     near = lax.ppermute(lent, "mp", PARTNER)
-    block, both = call(
+    got = tie(got, lent)
+    block, both, hid = call(
         split_kernel,
         (
             shape((NX, half + 2 * deep // NX, width), BF16),
             shape((deep, share)),
+            shape((rank, share)),
         ),
         [VMEM],
         (got,),
@@ -353,8 +350,8 @@
     grad, in_factor, down_raw = call(
         far_kernel,
         (shape(grad.shape, BF16), shape((rank, share)), shape((mp_size, SEQ_DEV, 2 * rank))),
-        [VMEM] * 4,
-        (far, grad, both, seq_ids),
+        [VMEM] * 5,
+        (far, grad, both, hid, seq_ids),
         far.size,
         {1: 0},
     )
@@ -366,11 +363,11 @@
         (grad, w_down, activated, slope, proj_gate.T, proj_upward.T),
         2 * half * hidden * features,
     )
-    near, other_factor, own_factors = lax.optimization_barrier((near, other_factor, own_factors))
+    near = tie(near, in_factor)
     other = lax.ppermute(near, "dp", cores)
-    lent_activated, lent_slope, lent_proj = call(
+    lent_activated, lent_slope = call(
         lambda *refs: lent_kernel(features, *refs),
-        (shape((half, hidden)), shape((half, hidden)), shape((hidden, 2 * rank), BF16)),
+        (shape((half, hidden)), shape((half, hidden))),
         [VMEM],
         (near,),
         lent.size,
@@ -385,8 +382,8 @@
     total = call(
         partner_kernel,
         shape(own_factors.shape),
-        [VMEM] * 7,
-        (grad, near, other, lent_activated, lent_slope, lent_proj, own_factors),
+        [VMEM] * 6,
+        (grad, near, other, lent_activated, lent_slope, own_factors),
         2 * half * hidden * features,
     )
     sent = call(

time: 141 us -> 137 us (0.972)
  waiting for transfers between devices: 28.1 us -> 18.8 us
  blocking collectives: 49.8 us -> 53.6 us
  Pallas kernels: 8.33 us -> 10.8 us
  local copies, waits for them, and re-layouts: 3.7 us -> 2.27 us
    ppermute x1, waiting for transfers between devices: 3.75 us -> 0.01 us  [per_device(): other = lax.ppermute(near, 'dp', cores)]
    all_to_all x1, waiting for transfers between devices: 3.87 us -> 0.61 us  [per_device(): got = lax.all_to_all(sent, 'mp', 0, 0, axis_index_groups=X_GROUPS)]
    all_to_all x1, blocking collectives: 17.4 us -> 20.2 us  [per_device(): got = jnp.sum(lax.all_to_all(sent, 'mp', 0, 0), axis=0)]
    ppermute x3, waiting for transfers between devices: 10.4 us -> 7.91 us  [per_device(): lax.ppermute(up, 'mp', z_shift(1))]
    pallas_call x14, Pallas kernels: 8.33 us -> 10.8 us  [call(): pl.pallas_call(kernel, out_shape=out_shape, in_specs=specs, out_specs=out...]
    ppermute x1, starting transfers between devices: 9.05 us -> 7.57 us  [per_device(): other = lax.ppermute(near, 'dp', cores)]
    unnamed x16 -> x14, local copies, waits for them, and re-layouts: 3.49 us -> 2.06 us
  transfers between devices with their start and end apart: 11 -> 11, of which waited for: 8 -> 8; matrix products, arithmetic and copies ran while one was open for 0% -> 0% of each run, Pallas kernels for 3% -> 5%
where the time goes in v5:
time: 137 us; the launch traced here: 136 us
  blocking collectives  53.6 us (39%)
  starting transfers between devices  49.8 us (36%)
  waiting for transfers between devices  18.8 us (14%)
  Pallas kernels  10.8 us (8%)
  local copies, waits for them, and re-layouts  2.27 us (2%)
    all_to_all x2, blocking collectives, per_device(): lax.all_to_all(jnp.broadcast_to(squares, (size, 1, 128)), axis, 0, 0)  33.4 us
    all_to_all x1, blocking collectives, per_device(): got = jnp.sum(lax.all_to_all(sent, 'mp', 0, 0), axis=0)  20.2 us
    ppermute x3, starting transfers between devices, per_device(): lax.ppermute(down, 'mp', z_shift(-1))  17.7 us
    pallas_call x14, Pallas kernels, call(): pl.pallas_call(kernel, out_shape=out_shape, in_specs=specs, out_specs=out...  10.8 us
    ppermute x3, starting transfers between devices, per_device(): lax.ppermute(up, 'mp', z_shift(1))  10.4 us
    ppermute x3, waiting for transfers between devices, per_device(): lax.ppermute(up, 'mp', z_shift(1))  7.91 us
    ppermute x1, starting transfers between devices, per_device(): other = lax.ppermute(near, 'dp', cores)  7.57 us
    ppermute x1, waiting for transfers between devices, per_device(): far = lax.ppermute(up, 'mp', z_shift(1))  7.34 us
  transfers between devices with their start and end apart: 11, of which 8 were waited for; matrix products, arithmetic and copies ran while one was open for 0% of the time, Pallas kernels for 5%

profile of v5, /device:TPU:1, one launch (start us, length us, event | category | flops | bytes accessed | tf_op | source)
XLA Modules:
  0.0 136.4 jit_solution(2422797069376968332)
XLA Ops:
  0.0 0.0 copy-start.3
  0.0 0.0 copy-start.2
  0.0 0.0 copy-start.5
  0.0 0.0 copy-start.4
  0.0 2.7 %shard_map.109 = bf16[4,640,128]{2,1,0:T(8,128)(2,1)} custom-call(bf16[512,128]{1,0:T(8,128)(2,1)} %input_hbm.1, bf16[512,128]{1,0:T(8,128)(2,1)} %grad_hbm.1, bf16[448,512]{1,0:T(8,128)(2,1)} %bitcast.16, bf16[448,512]{1,0:T(8,128)(2,1)} %bitcast.19, bf16[64,128]{1,0:T(8,128)(2,1)} %bitcast.30, bf16[64,128]{1,0:T(8,128)(2,1)} %proj_out_hbm.1, ...), custom_call_target="tpu_custom_call" | custom-call | flops 46137344 | bytes 1269760 | tf_op jit(solution)/shard_map/pallas_call | solution.py:60
  2.7 4.9 %all-to-all-start = ((bf16[4,640,128]{2,1,0:T(8,128)(2,1)}), bf16[4,640,128]{2,1,0:T(8,128)(2,1)}, u32[]{:S(2)}, u32[]{:S(2)}) async-start(bf16[4,640,128]{2,1,0:T(8,128)(2,1)} %shard_map.109), calls=%async_computation | async-start | bytes 1310720 | tf_op jit(solution)/shard_map/all_to_all | solution.py:310
  7.5 0.0 copy-done.3
  7.5 0.0 copy-done.2
  7.5 0.0 copy-done.5
  7.6 0.0 copy-done.4
  7.6 0.0 copy-start
  7.6 2.0 %copy-done = bf16[448,4096]{1,0:T(8,128)(2,1)S(1)} copy-done((bf16[448,4096]{1,0:T(8,128)(2,1)S(1)}, bf16[448,4096]{1,0:T(8,128)(2,1)}, u32[]{:S(2)}) %copy-start) | copy-done | bytes 3670040
  9.6 1.7 %shard_map.110 = bf16[224,5248]{1,0:T(8,128)(2,1)} custom-call(bf16[448,4096]{1,0:T(8,128)(2,1)S(1)} %copy-done, bf16[448,512]{1,0:T(8,128)(2,1)S(1)} %bitcast.17, bf16[448,512]{1,0:T(8,128)(2,1)S(1)} %bitcast.20, bf16[64,448]{1,0:T(8,128)(2,1)S(1)} %bitcast.22, bf16[64,448]{1,0:T(8,128)(2,1)S(1)} %bitcast.24), custom_call_target="tpu_custom_call" | custom-call | flops 1835008 | bytes 4702208 | tf_op jit(solution)/shard_map/pallas_call | solution.py:60
  11.3 3.4 %collective-permute-start.7 = (bf16[224,5248]{1,0:T(8,128)(2,1)}, bf16[224,5248]{1,0:T(8,128)(2,1)S(1)}, u32[]{:S(2)}, u32[]{:S(2)}) collective-permute-start(bf16[224,5248]{1,0:T(8,128)(2,1)} %shard_map.110), channel_id=1, source_target_pairs={{0,8},{1,9},{2,10},{3,11},{4,12},{5,13},{6,14},{7,15},{8,0},{9,1},... | collective-permute-start | bytes 7053320 | tf_op jit(solution)/shard_map/ppermute | solution.py:311
  14.7 0.6 all-to-all-done.got_ref
  15.3 1.1 shard_map.111
  16.4 6.6 %collective-permute-start = (bf16[4,320,128]{2,1,0:T(8,128)(2,1)S(1)}, bf16[4,320,128]{2,1,0:T(8,128)(2,1)S(1)}, u32[]{:S(2)}, u32[]{:S(2)}) collective-permute-start(bf16[4,320,128]{2,1,0:T(8,128)(2,1)S(1)} %get-tuple-element.33.block_ref), channel_id=1, source_target_pairs={{0,1},{1,2},{2,3},{3,4},{4,5},{5,6},{6,7},{7,0},{8,9},{9,10},{10,1... | collective-permute-start | bytes 983048 | tf_op jit(solution)/shard_map/ppermute | solution.py:326
  23.0 8.6 %collective-permute-start.2 = (bf16[4,320,128]{2,1,0:T(8,128)(2,1)S(1)}, bf16[4,320,128]{2,1,0:T(8,128)(2,1)S(1)}, u32[]{:S(2)}, u32[]{:S(2)}) collective-permute-start(bf16[4,320,128]{2,1,0:T(8,128)(2,1)S(1)} %get-tuple-element.33.block_ref), channel_id=1, source_target_pairs={{0,7},{1,0},{2,1},{3,2},{4,3},{5,4},{6,5},{7,6},{8,15},{9,8},{10,9... | collective-permute-start | bytes 983048 | tf_op jit(solution)/shard_map/ppermute | solution.py:326
  31.6 0.3 shard_map.114
  31.9 0.1 shard_map.112.refs_2_
  32.0 3.3 %collective-permute-done.refs_0_ = bf16[4,320,128]{2,1,0:T(8,128)(2,1)S(1)} collective-permute-done((bf16[4,320,128]{2,1,0:T(8,128)(2,1)S(1)}, bf16[4,320,128]{2,1,0:T(8,128)(2,1)S(1)}, u32[]{:S(2)}, u32[]{:S(2)}) %collective-permute-start) | collective-permute-done | bytes 327712 | tf_op jit(solution)/shard_map/ppermute | solution.py:326
  35.2 1.9 %collective-permute-start.1 = (bf16[4,320,128]{2,1,0:T(8,128)(2,1)S(1)}, bf16[4,320,128]{2,1,0:T(8,128)(2,1)S(1)}, u32[]{:S(2)}, u32[]{:S(2)}) collective-permute-start(bf16[4,320,128]{2,1,0:T(8,128)(2,1)S(1)} %collective-permute-done.refs_0_), channel_id=1, source_target_pairs={{0,1},{1,2},{2,3},{3,4},{4,5},{5,6},{6,7},{7,0},{8,9},{9,10},{10,1... | collective-permute-start | bytes 983048 | tf_op jit(solution)/shard_map/ppermute | solution.py:331
  37.1 0.0 collective-permute-done.2.refs_1_
  37.2 4.6 %collective-permute-start.4 = (bf16[4,320,128]{2,1,0:T(8,128)(2,1)S(1)}, bf16[4,320,128]{2,1,0:T(8,128)(2,1)S(1)}, u32[]{:S(2)}, u32[]{:S(2)}) collective-permute-start(bf16[4,320,128]{2,1,0:T(8,128)(2,1)S(1)} %collective-permute-done.2.refs_1_), channel_id=1, source_target_pairs={{0,7},{1,0},{2,1},{3,2},{4,3},{5,4},{6,5},{7,6},{8,15},{9,8},{10,9... | collective-permute-start | bytes 983048 | tf_op jit(solution)/shard_map/ppermute | solution.py:331
  41.7 0.2 shard_map.113
  41.9 2.3 %collective-permute-done.1.refs_0_ = bf16[4,320,128]{2,1,0:T(8,128)(2,1)S(1)} collective-permute-done((bf16[4,320,128]{2,1,0:T(8,128)(2,1)S(1)}, bf16[4,320,128]{2,1,0:T(8,128)(2,1)S(1)}, u32[]{:S(2)}, u32[]{:S(2)}) %collective-permute-start.1) | collective-permute-done | bytes 327712 | tf_op jit(solution)/shard_map/ppermute | solution.py:331
  44.3 1.9 %collective-permute-start.3 = (bf16[4,320,128]{2,1,0:T(8,128)(2,1)S(1)}, bf16[4,320,128]{2,1,0:T(8,128)(2,1)S(1)}, u32[]{:S(2)}, u32[]{:S(2)}) collective-permute-start(bf16[4,320,128]{2,1,0:T(8,128)(2,1)S(1)} %collective-permute-done.1.refs_0_), channel_id=1, source_target_pairs={{0,1},{1,2},{2,3},{3,4},{4,5},{5,6},{6,7},{7,0},{8,9},{9,10},{10,1... | collective-permute-start | bytes 983048 | tf_op jit(solution)/shard_map/ppermute | solution.py:343
  46.2 0.0 collective-permute-done.4.refs_1_
  46.2 4.6 %collective-permute-start.5 = (bf16[4,320,128]{2,1,0:T(8,128)(2,1)S(1)}, bf16[4,320,128]{2,1,0:T(8,128)(2,1)S(1)}, u32[]{:S(2)}, u32[]{:S(2)}) collective-permute-start(bf16[4,320,128]{2,1,0:T(8,128)(2,1)S(1)} %collective-permute-done.4.refs_1_), channel_id=1, source_target_pairs={{0,7},{1,0},{2,1},{3,2},{4,3},{5,4},{6,5},{7,6},{8,15},{9,8},{10,9... | collective-permute-start | bytes 983048 | tf_op jit(solution)/shard_map/ppermute | solution.py:343
  50.8 0.2 shard_map.115
  50.9 2.3 %collective-permute-done.3.refs_0_ = bf16[4,320,128]{2,1,0:T(8,128)(2,1)S(1)} collective-permute-done((bf16[4,320,128]{2,1,0:T(8,128)(2,1)S(1)}, bf16[4,320,128]{2,1,0:T(8,128)(2,1)S(1)}, u32[]{:S(2)}, u32[]{:S(2)}) %collective-permute-start.3) | collective-permute-done | bytes 327712 | tf_op jit(solution)/shard_map/ppermute | solution.py:343
  53.3 1.5 %collective-permute-done.5.refs_1_ = bf16[4,320,128]{2,1,0:T(8,128)(2,1)S(1)} collective-permute-done((bf16[4,320,128]{2,1,0:T(8,128)(2,1)S(1)}, bf16[4,320,128]{2,1,0:T(8,128)(2,1)S(1)}, u32[]{:S(2)}, u32[]{:S(2)}) %collective-permute-start.5) | collective-permute-done | bytes 327712 | tf_op jit(solution)/shard_map/ppermute | solution.py:343
  54.8 1.9 %collective-permute-start.6 = (bf16[4,320,128]{2,1,0:T(8,128)(2,1)S(1)}, bf16[4,320,128]{2,1,0:T(8,128)(2,1)S(1)}, u32[]{:S(2)}, u32[]{:S(2)}) collective-permute-start(bf16[4,320,128]{2,1,0:T(8,128)(2,1)S(1)} %collective-permute-done.3.refs_0_), channel_id=1, source_target_pairs={{0,1},{1,2},{2,3},{3,4},{4,5},{5,6},{6,7},{7,0},{8,9},{9,10},{10,1... | collective-permute-start | bytes 983048 | tf_op jit(solution)/shard_map/ppermute | solution.py:348
  56.7 0.0 copy-start.6
  56.7 0.0 copy-start.1
  56.7 0.2 shard_map.116
  56.9 7.3 %collective-permute-done.6.block_ref = bf16[4,320,128]{2,1,0:T(8,128)(2,1)S(1)} collective-permute-done((bf16[4,320,128]{2,1,0:T(8,128)(2,1)S(1)}, bf16[4,320,128]{2,1,0:T(8,128)(2,1)S(1)}, u32[]{:S(2)}, u32[]{:S(2)}) %collective-permute-start.6) | collective-permute-done | bytes 327712 | tf_op jit(solution)/shard_map/ppermute | solution.py:348
  64.2 0.0 copy-done.6
  64.2 0.5 shard_map.117
  64.7 0.9 collective-permute-done.7.refs_0_.near_ref
  65.6 7.6 %collective-permute-start.8 = (bf16[224,5248]{1,0:T(8,128)(2,1)S(1)}, bf16[224,5248]{1,0:T(8,128)(2,1)S(1)}, u32[]{:S(2)}, u32[]{:S(2)}) collective-permute-start(bf16[224,5248]{1,0:T(8,128)(2,1)S(1)} %collective-permute-done.7.refs_0_.near_ref), channel_id=1, source_target_pairs={{0,32},{32,0},{64,96},{96,64},{128,160},{160,128},{192,224},{224,1... | collective-permute-start | bytes 7053320 | tf_op jit(solution)/shard_map/ppermute | solution.py:367
  73.2 4.0 %collective-permute-start.9 = (f32[64,128]{1,0:T(8,128)S(1)}, f32[64,128]{1,0:T(8,128)S(1)}, u32[]{:S(2)}, u32[]{:S(2)}) collective-permute-start(f32[64,128]{1,0:T(8,128)S(1)} %get-tuple-element.49.own_ref), channel_id=1, source_target_pairs={{0,16},{1,17},{2,18},{3,19},{4,20},{5,21},{6,22},{7,23},{8,24},{9,... | collective-permute-start | bytes 98312 | tf_op jit(solution)/shard_map/ppermute | solution.py:358
  77.2 0.0 copy-done.1
  77.2 1.6 %shard_map.119.own_ref = f32[256,128]{1,0:T(8,128)S(1)} custom-call(bf16[256,4096]{1,0:T(8,128)(2,1)S(1)} %get-tuple-element.48.grad_ref, bf16[448,4096]{1,0:T(8,128)(2,1)S(1)} %copy-done.1, f32[256,448]{1,0:T(8,128)S(1)} %get-tuple-element.53.activated_ref, f32[256,448]{1,0:T(8,128)S(1)} %get-tuple-element.37.slope_ref, bf16[64,448]{1,0:T(8,128)(2,1)S(1)} %bitcast.23, ...), custom_call_target="tpu_custom_call" | custom-call | flops 939524096 | bytes 6799360 | tf_op jit(solution)/shard_map/pallas_call | solution.py:60
  78.8 0.6 collective-permute-done.9.other_ref
  79.3 0.1 shard_map.121
  79.4 0.3 shard_map.118
  79.7 0.0 collective-permute-done.8.other_ref
  79.8 1.6 %shard_map.120.total_ref = f32[256,128]{1,0:T(8,128)S(1)} custom-call(bf16[256,4096]{1,0:T(8,128)(2,1)S(1)} %get-tuple-element.48.grad_ref, bf16[224,5248]{1,0:T(8,128)(2,1)S(1)} %collective-permute-done.7.refs_0_.near_ref, bf16[224,5248]{1,0:T(8,128)(2,1)S(1)} %collective-permute-done.8.other_ref, f32[256,448]{1,0:T(8,128)S(1)} %get-tuple-element.51.activated_ref, ...), custom_call_target="tpu_custom_call" | custom-call | flops 939524096 | bytes 7847936 | tf_op jit(solution)/shard_map/pallas_call | solution.py:60
  81.4 0.3 shard_map.122
  81.7 20.2 %all_to_all.20 = f32[32,24,128]{2,1,0:T(8,128)S(1)} all-to-all(f32[32,24,128]{2,1,0:T(8,128)S(1)} %shard_map.122), channel_id=1, replica_groups=mesh['dp'=16,'mp'=32] {'mp'}, dimensions={0} | all-to-all | bytes 786432 | tf_op jit(solution)/shard_map/all_to_all | solution.py:396
  102.0 0.1 reshape.29
  102.1 0.1 reshape.30
  102.2 0.1 multiply_reduce_fusion
  102.3 16.2 %all_to_all.21 = f32[32,1,128]{2,1,0:T(1,128)S(1)} all-to-all(f32[32,1,128]{2,1,0:T(1,128)S(1)} %broadcast_in_dim.9), channel_id=1, replica_groups=mesh['dp'=16,'mp'=32] {'mp'}, dimensions={0} | all-to-all | bytes 32768 | tf_op jit(solution)/shard_map/all_to_all | solution.py:405
  118.5 17.2 %all_to_all.22 = f32[16,1,128]{2,1,0:T(1,128)S(1)} all-to-all(f32[16,1,128]{2,1,0:T(1,128)S(1)} %broadcast_in_dim.20), channel_id=1, replica_groups=mesh['dp'=16,'mp'=32] {'dp'}, dimensions={0} | all-to-all | bytes 16384 | tf_op jit(solution)/shard_map/all_to_all | solution.py:405
  135.7 0.7 fusion
  (10 shorter events, 0.1 us)
Async XLA Ops:
  0.0 7.5 %copy-start.3 = (bf16[512,448]{0,1:T(8,128)(2,1)S(1)}, bf16[512,448]{0,1:T(8,128)(2,1)}, u32[]{:S(2)}) copy-start(bf16[512,448]{0,1:T(8,128)(2,1)} %param.13) | copy-start | bytes 1376260
  0.0 7.5 %copy-start.2 = (bf16[512,448]{0,1:T(8,128)(2,1)S(1)}, bf16[512,448]{0,1:T(8,128)(2,1)}, u32[]{:S(2)}) copy-start(bf16[512,448]{0,1:T(8,128)(2,1)} %param.12) | copy-start | bytes 1376260
  0.0 7.5 %copy-start.5 = (bf16[448,64]{0,1:T(8,128)(2,1)S(1)}, bf16[448,64]{0,1:T(8,128)(2,1)}, u32[]{:S(2)}) copy-start(bf16[448,64]{0,1:T(8,128)(2,1)} %param.19) | copy-start | bytes 172036
  0.0 7.5 %copy-start.4 = (bf16[448,64]{0,1:T(8,128)(2,1)S(1)}, bf16[448,64]{0,1:T(8,128)(2,1)}, u32[]{:S(2)}) copy-start(bf16[448,64]{0,1:T(8,128)(2,1)} %param.18) | copy-start | bytes 172036
  2.7 12.6 %all-to-all-start = ((bf16[4,640,128]{2,1,0:T(8,128)(2,1)}), bf16[4,640,128]{2,1,0:T(8,128)(2,1)}, u32[]{:S(2)}, u32[]{:S(2)}) async-start(bf16[4,640,128]{2,1,0:T(8,128)(2,1)} %shard_map.109), calls=%async_computation | async-start | bytes 1310720 | tf_op jit(solution)/shard_map/all_to_all | solution.py:310
  7.6 2.0 %copy-start = (bf16[448,4096]{1,0:T(8,128)(2,1)S(1)}, bf16[448,4096]{1,0:T(8,128)(2,1)}, u32[]{:S(2)}) copy-start(bf16[448,4096]{1,0:T(8,128)(2,1)} %w_ref.1) | copy-start | bytes 11010052
  11.3 54.3 %collective-permute-start.7 = (bf16[224,5248]{1,0:T(8,128)(2,1)}, bf16[224,5248]{1,0:T(8,128)(2,1)S(1)}, u32[]{:S(2)}, u32[]{:S(2)}) collective-permute-start(bf16[224,5248]{1,0:T(8,128)(2,1)} %shard_map.110), channel_id=1, source_target_pairs={{0,8},{1,9},{2,10},{3,11},{4,12},{5,13},{6,14},{7,15},{8,0},{9,1},... | collective-permute-start | bytes 7053320 | tf_op jit(solution)/shard_map/ppermute | solution.py:311
  16.4 18.8 %collective-permute-start = (bf16[4,320,128]{2,1,0:T(8,128)(2,1)S(1)}, bf16[4,320,128]{2,1,0:T(8,128)(2,1)S(1)}, u32[]{:S(2)}, u32[]{:S(2)}) collective-permute-start(bf16[4,320,128]{2,1,0:T(8,128)(2,1)S(1)} %get-tuple-element.33.block_ref), channel_id=1, source_target_pairs={{0,1},{1,2},{2,3},{3,4},{4,5},{5,6},{6,7},{7,0},{8,9},{9,10},{10,1... | collective-permute-start | bytes 983048 | tf_op jit(solution)/shard_map/ppermute | solution.py:326
  23.0 14.2 %collective-permute-start.2 = (bf16[4,320,128]{2,1,0:T(8,128)(2,1)S(1)}, bf16[4,320,128]{2,1,0:T(8,128)(2,1)S(1)}, u32[]{:S(2)}, u32[]{:S(2)}) collective-permute-start(bf16[4,320,128]{2,1,0:T(8,128)(2,1)S(1)} %get-tuple-element.33.block_ref), channel_id=1, source_target_pairs={{0,7},{1,0},{2,1},{3,2},{4,3},{5,4},{6,5},{7,6},{8,15},{9,8},{10,9... | collective-permute-start | bytes 983048 | tf_op jit(solution)/shard_map/ppermute | solution.py:326
  35.2 9.0 %collective-permute-start.1 = (bf16[4,320,128]{2,1,0:T(8,128)(2,1)S(1)}, bf16[4,320,128]{2,1,0:T(8,128)(2,1)S(1)}, u32[]{:S(2)}, u32[]{:S(2)}) collective-permute-start(bf16[4,320,128]{2,1,0:T(8,128)(2,1)S(1)} %collective-permute-done.refs_0_), channel_id=1, source_target_pairs={{0,1},{1,2},{2,3},{3,4},{4,5},{5,6},{6,7},{7,0},{8,9},{9,10},{10,1... | collective-permute-start | bytes 983048 | tf_op jit(solution)/shard_map/ppermute | solution.py:331
  37.2 9.0 %collective-permute-start.4 = (bf16[4,320,128]{2,1,0:T(8,128)(2,1)S(1)}, bf16[4,320,128]{2,1,0:T(8,128)(2,1)S(1)}, u32[]{:S(2)}, u32[]{:S(2)}) collective-permute-start(bf16[4,320,128]{2,1,0:T(8,128)(2,1)S(1)} %collective-permute-done.2.refs_1_), channel_id=1, source_target_pairs={{0,7},{1,0},{2,1},{3,2},{4,3},{5,4},{6,5},{7,6},{8,15},{9,8},{10,9... | collective-permute-start | bytes 983048 | tf_op jit(solution)/shard_map/ppermute | solution.py:331
  44.3 9.0 %collective-permute-start.3 = (bf16[4,320,128]{2,1,0:T(8,128)(2,1)S(1)}, bf16[4,320,128]{2,1,0:T(8,128)(2,1)S(1)}, u32[]{:S(2)}, u32[]{:S(2)}) collective-permute-start(bf16[4,320,128]{2,1,0:T(8,128)(2,1)S(1)} %collective-permute-done.1.refs_0_), channel_id=1, source_target_pairs={{0,1},{1,2},{2,3},{3,4},{4,5},{5,6},{6,7},{7,0},{8,9},{9,10},{10,1... | collective-permute-start | bytes 983048 | tf_op jit(solution)/shard_map/ppermute | solution.py:343
  46.2 8.6 %collective-permute-start.5 = (bf16[4,320,128]{2,1,0:T(8,128)(2,1)S(1)}, bf16[4,320,128]{2,1,0:T(8,128)(2,1)S(1)}, u32[]{:S(2)}, u32[]{:S(2)}) collective-permute-start(bf16[4,320,128]{2,1,0:T(8,128)(2,1)S(1)} %collective-permute-done.4.refs_1_), channel_id=1, source_target_pairs={{0,7},{1,0},{2,1},{3,2},{4,3},{5,4},{6,5},{7,6},{8,15},{9,8},{10,9... | collective-permute-start | bytes 983048 | tf_op jit(solution)/shard_map/ppermute | solution.py:343
  54.8 9.5 %collective-permute-start.6 = (bf16[4,320,128]{2,1,0:T(8,128)(2,1)S(1)}, bf16[4,320,128]{2,1,0:T(8,128)(2,1)S(1)}, u32[]{:S(2)}, u32[]{:S(2)}) collective-permute-start(bf16[4,320,128]{2,1,0:T(8,128)(2,1)S(1)} %collective-permute-done.3.refs_0_), channel_id=1, source_target_pairs={{0,1},{1,2},{2,3},{3,4},{4,5},{5,6},{6,7},{7,0},{8,9},{9,10},{10,1... | collective-permute-start | bytes 983048 | tf_op jit(solution)/shard_map/ppermute | solution.py:348
  56.7 7.6 %copy-start.6 = (s32[1,512]{1,0:T(1,128)S(1)}, s32[1,512]{1,0:T(1,128)}, u32[]{:S(2)}) copy-start(s32[1,512]{1,0:T(1,128)} %ids_ref.3) | copy-start | bytes 6148
  56.7 20.5 %copy-start.1 = (bf16[448,4096]{1,0:T(8,128)(2,1)S(1)}, bf16[448,4096]{1,0:T(8,128)(2,1)}, u32[]{:S(2)}) copy-start(bf16[448,4096]{1,0:T(8,128)(2,1)} %w_ref.1) | copy-start | bytes 11010052
  65.6 14.2 %collective-permute-start.8 = (bf16[224,5248]{1,0:T(8,128)(2,1)S(1)}, bf16[224,5248]{1,0:T(8,128)(2,1)S(1)}, u32[]{:S(2)}, u32[]{:S(2)}) collective-permute-start(bf16[224,5248]{1,0:T(8,128)(2,1)S(1)} %collective-permute-done.7.refs_0_.near_ref), channel_id=1, source_target_pairs={{0,32},{32,0},{64,96},{96,64},{128,160},{160,128},{192,224},{224,1... | collective-permute-start | bytes 7053320 | tf_op jit(solution)/shard_map/ppermute | solution.py:367
  73.2 6.2 %collective-permute-start.9 = (f32[64,128]{1,0:T(8,128)S(1)}, f32[64,128]{1,0:T(8,128)S(1)}, u32[]{:S(2)}, u32[]{:S(2)}) collective-permute-start(f32[64,128]{1,0:T(8,128)S(1)} %get-tuple-element.49.own_ref), channel_id=1, source_target_pairs={{0,16},{1,17},{2,18},{3,19},{4,20},{5,21},{6,22},{7,23},{8,24},{9,... | collective-permute-start | bytes 98312 | tf_op jit(solution)/shard_map/ppermute | solution.py:358

commit v6 on v5

--- a/solution.py
+++ b/solution.py
@@ -218,7 +218,7 @@
         (jax.ShapeDtypeStruct(grad.shape, BF16), jax.ShapeDtypeStruct(both.shape, F32)),
         [VMEM] * 4,
         (up, down, grad, both),
-        7000000000,
+        6000000000,
         {2: 0, 3: 1},
     )
 
@@ -344,7 +344,7 @@
     grad, both = add_pair(2, up, down, grad, both)
     next_up = tie(next_up, grad)
 
-    up, down = lax.optimization_barrier((next_up, next_down))
+    up, down = next_up, next_down
     far = lax.ppermute(up, "mp", z_shift(1))
     grad, both = add_pair(3, up, down, grad, both)
     grad, in_factor, down_raw = call(
@@ -363,7 +363,7 @@
         (grad, w_down, activated, slope, proj_gate.T, proj_upward.T),
         2 * half * hidden * features,
     )
-    near = tie(near, in_factor)
+    near, other_factor, own_factors = lax.optimization_barrier((near, other_factor, own_factors))
     other = lax.ppermute(near, "dp", cores)
     lent_activated, lent_slope = call(
         lambda *refs: lent_kernel(features, *refs),

time: 137 us -> 135 us (0.985)
  blocking collectives: 53.6 us -> 49.1 us
  starting transfers between devices: 49.8 us -> 51.5 us
    ppermute x1, waiting for transfers between devices: 0.01 us -> 3.68 us  [per_device(): other = lax.ppermute(near, 'dp', cores)]
    all_to_all x1, blocking collectives: 20.2 us -> 16.7 us  [per_device(): got = jnp.sum(lax.all_to_all(sent, 'mp', 0, 0), axis=0)]
    ppermute x1, starting transfers between devices: 7.57 us -> 9.16 us  [per_device(): other = lax.ppermute(near, 'dp', cores)]
    ppermute x3, waiting for transfers between devices: 1.49 us -> 0.01 us  [per_device(): lax.ppermute(down, 'mp', z_shift(-1))]
  transfers between devices with their start and end apart: 11 -> 11, of which waited for: 8 -> 7; matrix products, arithmetic and copies ran while one was open for 0% -> 0% of each run, Pallas kernels for 5% -> 5%
where the time goes in v6:
time: 135 us
  starting transfers between devices  51.5 us (38%)
  blocking collectives  49.1 us (36%)
  waiting for transfers between devices  20 us (15%)
  Pallas kernels  10.8 us (8%)
  local copies, waits for them, and re-layouts  2.27 us (2%)
    all_to_all x2, blocking collectives, per_device(): lax.all_to_all(jnp.broadcast_to(squares, (size, 1, 128)), axis, 0, 0)  32.3 us
    ppermute x3, starting transfers between devices, per_device(): lax.ppermute(down, 'mp', z_shift(-1))  17.7 us
    all_to_all x1, blocking collectives, per_device(): got = jnp.sum(lax.all_to_all(sent, 'mp', 0, 0), axis=0)  16.7 us
    pallas_call x14, Pallas kernels, call(): pl.pallas_call(kernel, out_shape=out_shape, in_specs=specs, out_specs=out...  10.8 us
    ppermute x3, starting transfers between devices, per_device(): lax.ppermute(up, 'mp', z_shift(1))  10.4 us
    ppermute x1, starting transfers between devices, per_device(): other = lax.ppermute(near, 'dp', cores)  9.16 us
    ppermute x3, waiting for transfers between devices, per_device(): lax.ppermute(up, 'mp', z_shift(1))  7.91 us
    ppermute x1, waiting for transfers between devices, per_device(): far = lax.ppermute(up, 'mp', z_shift(1))  6.88 us
  transfers between devices with their start and end apart: 11, of which 7 were waited for; matrix products, arithmetic and copies ran while one was open for 0% of the time, Pallas kernels for 5%

profile of v6, /device:TPU:1, one launch (start us, length us, event | category | flops | bytes accessed | tf_op | source)
XLA Modules:
  0.0 134.7 jit_solution(5336813656233617132)
XLA Ops:
  0.0 0.0 copy-start.2
  0.0 0.0 copy-start.3
  0.0 0.0 copy-start.4
  0.0 0.0 copy-start.5
  0.0 2.7 %shard_map.109 = bf16[4,640,128]{2,1,0:T(8,128)(2,1)} custom-call(bf16[512,128]{1,0:T(8,128)(2,1)} %input_hbm.1, bf16[512,128]{1,0:T(8,128)(2,1)} %grad_hbm.1, bf16[448,512]{1,0:T(8,128)(2,1)} %bitcast.16, bf16[448,512]{1,0:T(8,128)(2,1)} %bitcast.19, bf16[64,128]{1,0:T(8,128)(2,1)} %bitcast.30, bf16[64,128]{1,0:T(8,128)(2,1)} %proj_out_hbm.1, ...), custom_call_target="tpu_custom_call" | custom-call | flops 46137344 | bytes 1269760 | tf_op jit(solution)/shard_map/pallas_call | solution.py:60
  2.7 4.9 %all-to-all-start = ((bf16[4,640,128]{2,1,0:T(8,128)(2,1)}), bf16[4,640,128]{2,1,0:T(8,128)(2,1)}, u32[]{:S(2)}, u32[]{:S(2)}) async-start(bf16[4,640,128]{2,1,0:T(8,128)(2,1)} %shard_map.109), calls=%async_computation | async-start | bytes 1310720 | tf_op jit(solution)/shard_map/all_to_all | solution.py:310
  7.5 0.0 copy-done.2
  7.5 0.0 copy-done.3
  7.5 0.0 copy-done.4
  7.6 0.0 copy-done.5
  7.6 0.0 copy-start
  7.6 2.0 %copy-done = bf16[448,4096]{1,0:T(8,128)(2,1)S(1)} copy-done((bf16[448,4096]{1,0:T(8,128)(2,1)S(1)}, bf16[448,4096]{1,0:T(8,128)(2,1)}, u32[]{:S(2)}) %copy-start) | copy-done | bytes 3670040
  9.6 1.7 %shard_map.110 = bf16[224,5248]{1,0:T(8,128)(2,1)} custom-call(bf16[448,4096]{1,0:T(8,128)(2,1)S(1)} %copy-done, bf16[448,512]{1,0:T(8,128)(2,1)S(1)} %bitcast.17, bf16[448,512]{1,0:T(8,128)(2,1)S(1)} %bitcast.20, bf16[64,448]{1,0:T(8,128)(2,1)S(1)} %bitcast.22, bf16[64,448]{1,0:T(8,128)(2,1)S(1)} %bitcast.24), custom_call_target="tpu_custom_call" | custom-call | flops 1835008 | bytes 4702208 | tf_op jit(solution)/shard_map/pallas_call | solution.py:60
  11.3 3.4 %collective-permute-start.7 = (bf16[224,5248]{1,0:T(8,128)(2,1)}, bf16[224,5248]{1,0:T(8,128)(2,1)S(1)}, u32[]{:S(2)}, u32[]{:S(2)}) collective-permute-start(bf16[224,5248]{1,0:T(8,128)(2,1)} %shard_map.110), channel_id=1, source_target_pairs={{0,8},{1,9},{2,10},{3,11},{4,12},{5,13},{6,14},{7,15},{8,0},{9,1},... | collective-permute-start | bytes 7053320 | tf_op jit(solution)/shard_map/ppermute | solution.py:311
  14.7 0.6 all-to-all-done.got_ref
  15.3 1.1 shard_map.111
  16.4 6.6 %collective-permute-start = (bf16[4,320,128]{2,1,0:T(8,128)(2,1)S(1)}, bf16[4,320,128]{2,1,0:T(8,128)(2,1)S(1)}, u32[]{:S(2)}, u32[]{:S(2)}) collective-permute-start(bf16[4,320,128]{2,1,0:T(8,128)(2,1)S(1)} %get-tuple-element.33.block_ref), channel_id=1, source_target_pairs={{0,1},{1,2},{2,3},{3,4},{4,5},{5,6},{6,7},{7,0},{8,9},{9,10},{10,1... | collective-permute-start | bytes 983048 | tf_op jit(solution)/shard_map/ppermute | solution.py:326
  23.0 8.6 %collective-permute-start.2 = (bf16[4,320,128]{2,1,0:T(8,128)(2,1)S(1)}, bf16[4,320,128]{2,1,0:T(8,128)(2,1)S(1)}, u32[]{:S(2)}, u32[]{:S(2)}) collective-permute-start(bf16[4,320,128]{2,1,0:T(8,128)(2,1)S(1)} %get-tuple-element.33.block_ref), channel_id=1, source_target_pairs={{0,7},{1,0},{2,1},{3,2},{4,3},{5,4},{6,5},{7,6},{8,15},{9,8},{10,9... | collective-permute-start | bytes 983048 | tf_op jit(solution)/shard_map/ppermute | solution.py:326
  31.6 0.3 shard_map.114
  31.9 0.1 shard_map.112.refs_2_
  32.0 3.3 %collective-permute-done.refs_0_ = bf16[4,320,128]{2,1,0:T(8,128)(2,1)S(1)} collective-permute-done((bf16[4,320,128]{2,1,0:T(8,128)(2,1)S(1)}, bf16[4,320,128]{2,1,0:T(8,128)(2,1)S(1)}, u32[]{:S(2)}, u32[]{:S(2)}) %collective-permute-start) | collective-permute-done | bytes 327712 | tf_op jit(solution)/shard_map/ppermute | solution.py:326
  35.2 1.9 %collective-permute-start.1 = (bf16[4,320,128]{2,1,0:T(8,128)(2,1)S(1)}, bf16[4,320,128]{2,1,0:T(8,128)(2,1)S(1)}, u32[]{:S(2)}, u32[]{:S(2)}) collective-permute-start(bf16[4,320,128]{2,1,0:T(8,128)(2,1)S(1)} %collective-permute-done.refs_0_), channel_id=1, source_target_pairs={{0,1},{1,2},{2,3},{3,4},{4,5},{5,6},{6,7},{7,0},{8,9},{9,10},{10,1... | collective-permute-start | bytes 983048 | tf_op jit(solution)/shard_map/ppermute | solution.py:331
  37.1 0.0 collective-permute-done.2.refs_1_
  37.2 4.6 %collective-permute-start.4 = (bf16[4,320,128]{2,1,0:T(8,128)(2,1)S(1)}, bf16[4,320,128]{2,1,0:T(8,128)(2,1)S(1)}, u32[]{:S(2)}, u32[]{:S(2)}) collective-permute-start(bf16[4,320,128]{2,1,0:T(8,128)(2,1)S(1)} %collective-permute-done.2.refs_1_), channel_id=1, source_target_pairs={{0,7},{1,0},{2,1},{3,2},{4,3},{5,4},{6,5},{7,6},{8,15},{9,8},{10,9... | collective-permute-start | bytes 983048 | tf_op jit(solution)/shard_map/ppermute | solution.py:331
  41.7 0.2 shard_map.113
  41.9 2.3 %collective-permute-done.1.refs_0_ = bf16[4,320,128]{2,1,0:T(8,128)(2,1)S(1)} collective-permute-done((bf16[4,320,128]{2,1,0:T(8,128)(2,1)S(1)}, bf16[4,320,128]{2,1,0:T(8,128)(2,1)S(1)}, u32[]{:S(2)}, u32[]{:S(2)}) %collective-permute-start.1) | collective-permute-done | bytes 327712 | tf_op jit(solution)/shard_map/ppermute | solution.py:331
  44.3 1.9 %collective-permute-start.3 = (bf16[4,320,128]{2,1,0:T(8,128)(2,1)S(1)}, bf16[4,320,128]{2,1,0:T(8,128)(2,1)S(1)}, u32[]{:S(2)}, u32[]{:S(2)}) collective-permute-start(bf16[4,320,128]{2,1,0:T(8,128)(2,1)S(1)} %collective-permute-done.1.refs_0_), channel_id=1, source_target_pairs={{0,1},{1,2},{2,3},{3,4},{4,5},{5,6},{6,7},{7,0},{8,9},{9,10},{10,1... | collective-permute-start | bytes 983048 | tf_op jit(solution)/shard_map/ppermute | solution.py:343
  46.2 0.0 collective-permute-done.4.refs_1_
  46.2 4.6 %collective-permute-start.6 = (bf16[4,320,128]{2,1,0:T(8,128)(2,1)S(1)}, bf16[4,320,128]{2,1,0:T(8,128)(2,1)S(1)}, u32[]{:S(2)}, u32[]{:S(2)}) collective-permute-start(bf16[4,320,128]{2,1,0:T(8,128)(2,1)S(1)} %collective-permute-done.4.refs_1_), channel_id=1, source_target_pairs={{0,7},{1,0},{2,1},{3,2},{4,3},{5,4},{6,5},{7,6},{8,15},{9,8},{10,9... | collective-permute-start | bytes 983048 | tf_op jit(solution)/shard_map/ppermute | solution.py:343
  50.8 0.2 shard_map.115
  50.9 2.3 %collective-permute-done.3.refs_0_ = bf16[4,320,128]{2,1,0:T(8,128)(2,1)S(1)} collective-permute-done((bf16[4,320,128]{2,1,0:T(8,128)(2,1)S(1)}, bf16[4,320,128]{2,1,0:T(8,128)(2,1)S(1)}, u32[]{:S(2)}, u32[]{:S(2)}) %collective-permute-start.3) | collective-permute-done | bytes 327712 | tf_op jit(solution)/shard_map/ppermute | solution.py:343
  53.3 1.9 %collective-permute-start.5 = (bf16[4,320,128]{2,1,0:T(8,128)(2,1)S(1)}, bf16[4,320,128]{2,1,0:T(8,128)(2,1)S(1)}, u32[]{:S(2)}, u32[]{:S(2)}) collective-permute-start(bf16[4,320,128]{2,1,0:T(8,128)(2,1)S(1)} %collective-permute-done.3.refs_0_), channel_id=1, source_target_pairs={{0,1},{1,2},{2,3},{3,4},{4,5},{5,6},{6,7},{7,0},{8,9},{9,10},{10,1... | collective-permute-start | bytes 983048 | tf_op jit(solution)/shard_map/ppermute | solution.py:348
  55.2 0.0 collective-permute-done.6.refs_1_
  55.2 0.0 copy-start.6
  55.2 0.0 copy-start.1
  55.2 0.2 shard_map.116
  55.4 6.9 %collective-permute-done.5.block_ref = bf16[4,320,128]{2,1,0:T(8,128)(2,1)S(1)} collective-permute-done((bf16[4,320,128]{2,1,0:T(8,128)(2,1)S(1)}, bf16[4,320,128]{2,1,0:T(8,128)(2,1)S(1)}, u32[]{:S(2)}, u32[]{:S(2)}) %collective-permute-start.5) | collective-permute-done | bytes 327712 | tf_op jit(solution)/shard_map/ppermute | solution.py:348
  62.3 0.0 copy-done.6
  62.3 0.5 shard_map.117
  62.8 4.1 %collective-permute-start.8 = (f32[64,128]{1,0:T(8,128)S(1)}, f32[64,128]{1,0:T(8,128)S(1)}, u32[]{:S(2)}, u32[]{:S(2)}) collective-permute-start(f32[64,128]{1,0:T(8,128)S(1)} %get-tuple-element.47.own_ref), channel_id=1, source_target_pairs={{0,16},{1,17},{2,18},{3,19},{4,20},{5,21},{6,22},{7,23},{8,24},{9,... | collective-permute-start | bytes 98312 | tf_op jit(solution)/shard_map/ppermute | solution.py:358
  66.9 0.0 copy-done.1
  66.9 1.6 %shard_map.118.own_ref = f32[256,128]{1,0:T(8,128)S(1)} custom-call(bf16[256,4096]{1,0:T(8,128)(2,1)S(1)} %get-tuple-element.46.grad_ref, bf16[448,4096]{1,0:T(8,128)(2,1)S(1)} %copy-done.1, f32[256,448]{1,0:T(8,128)S(1)} %get-tuple-element.48.activated_ref, f32[256,448]{1,0:T(8,128)S(1)} %get-tuple-element.37.slope_ref, bf16[64,448]{1,0:T(8,128)(2,1)S(1)} %bitcast.23, ...), custom_call_target="tpu_custom_call" | custom-call | flops 939524096 | bytes 6799360 | tf_op jit(solution)/shard_map/pallas_call | solution.py:60
  68.5 0.9 collective-permute-done.8.other_ref
  69.3 0.0 collective-permute-done.7.refs_0_.near_ref
  69.3 9.2 %collective-permute-start.9 = (bf16[224,5248]{1,0:T(8,128)(2,1)S(1)}, bf16[224,5248]{1,0:T(8,128)(2,1)S(1)}, u32[]{:S(2)}, u32[]{:S(2)}) collective-permute-start(bf16[224,5248]{1,0:T(8,128)(2,1)S(1)} %collective-permute-done.7.refs_0_.near_ref), channel_id=1, source_target_pairs={{0,32},{32,0},{64,96},{96,64},{128,160},{160,128},{192,224},{224,1... | collective-permute-start | bytes 7053320 | tf_op jit(solution)/shard_map/ppermute | solution.py:367
  78.5 0.1 shard_map.121
  78.7 0.3 shard_map.119
  79.0 3.7 %collective-permute-done.9.other_ref = bf16[224,5248]{1,0:T(8,128)(2,1)S(1)} collective-permute-done((bf16[224,5248]{1,0:T(8,128)(2,1)S(1)}, bf16[224,5248]{1,0:T(8,128)(2,1)S(1)}, u32[]{:S(2)}, u32[]{:S(2)}) %collective-permute-start.9) | collective-permute-done | bytes 2351136 | tf_op jit(solution)/shard_map/ppermute | solution.py:367
  82.6 1.6 %shard_map.120.total_ref = f32[256,128]{1,0:T(8,128)S(1)} custom-call(bf16[256,4096]{1,0:T(8,128)(2,1)S(1)} %get-tuple-element.46.grad_ref, bf16[224,5248]{1,0:T(8,128)(2,1)S(1)} %collective-permute-done.7.refs_0_.near_ref, bf16[224,5248]{1,0:T(8,128)(2,1)S(1)} %collective-permute-done.9.other_ref, f32[256,448]{1,0:T(8,128)S(1)} %get-tuple-element.50.activated_ref, ...), custom_call_target="tpu_custom_call" | custom-call | flops 939524096 | bytes 7847936 | tf_op jit(solution)/shard_map/pallas_call | solution.py:60
  84.3 0.3 shard_map.122
  84.6 16.7 %all_to_all.20 = f32[32,24,128]{2,1,0:T(8,128)S(1)} all-to-all(f32[32,24,128]{2,1,0:T(8,128)S(1)} %shard_map.122), channel_id=1, replica_groups=mesh['dp'=16,'mp'=32] {'mp'}, dimensions={0} | all-to-all | bytes 786432 | tf_op jit(solution)/shard_map/all_to_all | solution.py:396
  101.3 0.1 reshape.29
  101.4 0.1 reshape.30
  101.5 0.1 multiply_reduce_fusion
  101.7 16.0 %all_to_all.21 = f32[32,1,128]{2,1,0:T(1,128)S(1)} all-to-all(f32[32,1,128]{2,1,0:T(1,128)S(1)} %broadcast_in_dim.9), channel_id=1, replica_groups=mesh['dp'=16,'mp'=32] {'mp'}, dimensions={0} | all-to-all | bytes 32768 | tf_op jit(solution)/shard_map/all_to_all | solution.py:405
  117.7 16.3 %all_to_all.22 = f32[16,1,128]{2,1,0:T(1,128)S(1)} all-to-all(f32[16,1,128]{2,1,0:T(1,128)S(1)} %broadcast_in_dim.20), channel_id=1, replica_groups=mesh['dp'=16,'mp'=32] {'dp'}, dimensions={0} | all-to-all | bytes 16384 | tf_op jit(solution)/shard_map/all_to_all | solution.py:405
  134.1 0.7 fusion
  (10 shorter events, 0.1 us)
Async XLA Ops:
  0.0 7.5 %copy-start.2 = (bf16[512,448]{0,1:T(8,128)(2,1)S(1)}, bf16[512,448]{0,1:T(8,128)(2,1)}, u32[]{:S(2)}) copy-start(bf16[512,448]{0,1:T(8,128)(2,1)} %param.12) | copy-start | bytes 1376260
  0.0 7.5 %copy-start.3 = (bf16[512,448]{0,1:T(8,128)(2,1)S(1)}, bf16[512,448]{0,1:T(8,128)(2,1)}, u32[]{:S(2)}) copy-start(bf16[512,448]{0,1:T(8,128)(2,1)} %param.13) | copy-start | bytes 1376260
  0.0 7.5 %copy-start.4 = (bf16[448,64]{0,1:T(8,128)(2,1)S(1)}, bf16[448,64]{0,1:T(8,128)(2,1)}, u32[]{:S(2)}) copy-start(bf16[448,64]{0,1:T(8,128)(2,1)} %param.18) | copy-start | bytes 172036
  0.0 7.5 %copy-start.5 = (bf16[448,64]{0,1:T(8,128)(2,1)S(1)}, bf16[448,64]{0,1:T(8,128)(2,1)}, u32[]{:S(2)}) copy-start(bf16[448,64]{0,1:T(8,128)(2,1)} %param.19) | copy-start | bytes 172036
  2.7 12.6 %all-to-all-start = ((bf16[4,640,128]{2,1,0:T(8,128)(2,1)}), bf16[4,640,128]{2,1,0:T(8,128)(2,1)}, u32[]{:S(2)}, u32[]{:S(2)}) async-start(bf16[4,640,128]{2,1,0:T(8,128)(2,1)} %shard_map.109), calls=%async_computation | async-start | bytes 1310720 | tf_op jit(solution)/shard_map/all_to_all | solution.py:310
  7.6 2.0 %copy-start = (bf16[448,4096]{1,0:T(8,128)(2,1)S(1)}, bf16[448,4096]{1,0:T(8,128)(2,1)}, u32[]{:S(2)}) copy-start(bf16[448,4096]{1,0:T(8,128)(2,1)} %w_ref.1) | copy-start | bytes 11010052
  11.3 58.0 %collective-permute-start.7 = (bf16[224,5248]{1,0:T(8,128)(2,1)}, bf16[224,5248]{1,0:T(8,128)(2,1)S(1)}, u32[]{:S(2)}, u32[]{:S(2)}) collective-permute-start(bf16[224,5248]{1,0:T(8,128)(2,1)} %shard_map.110), channel_id=1, source_target_pairs={{0,8},{1,9},{2,10},{3,11},{4,12},{5,13},{6,14},{7,15},{8,0},{9,1},... | collective-permute-start | bytes 7053320 | tf_op jit(solution)/shard_map/ppermute | solution.py:311
  16.4 18.8 %collective-permute-start = (bf16[4,320,128]{2,1,0:T(8,128)(2,1)S(1)}, bf16[4,320,128]{2,1,0:T(8,128)(2,1)S(1)}, u32[]{:S(2)}, u32[]{:S(2)}) collective-permute-start(bf16[4,320,128]{2,1,0:T(8,128)(2,1)S(1)} %get-tuple-element.33.block_ref), channel_id=1, source_target_pairs={{0,1},{1,2},{2,3},{3,4},{4,5},{5,6},{6,7},{7,0},{8,9},{9,10},{10,1... | collective-permute-start | bytes 983048 | tf_op jit(solution)/shard_map/ppermute | solution.py:326
  23.0 14.2 %collective-permute-start.2 = (bf16[4,320,128]{2,1,0:T(8,128)(2,1)S(1)}, bf16[4,320,128]{2,1,0:T(8,128)(2,1)S(1)}, u32[]{:S(2)}, u32[]{:S(2)}) collective-permute-start(bf16[4,320,128]{2,1,0:T(8,128)(2,1)S(1)} %get-tuple-element.33.block_ref), channel_id=1, source_target_pairs={{0,7},{1,0},{2,1},{3,2},{4,3},{5,4},{6,5},{7,6},{8,15},{9,8},{10,9... | collective-permute-start | bytes 983048 | tf_op jit(solution)/shard_map/ppermute | solution.py:326
  35.2 9.0 %collective-permute-start.1 = (bf16[4,320,128]{2,1,0:T(8,128)(2,1)S(1)}, bf16[4,320,128]{2,1,0:T(8,128)(2,1)S(1)}, u32[]{:S(2)}, u32[]{:S(2)}) collective-permute-start(bf16[4,320,128]{2,1,0:T(8,128)(2,1)S(1)} %collective-permute-done.refs_0_), channel_id=1, source_target_pairs={{0,1},{1,2},{2,3},{3,4},{4,5},{5,6},{6,7},{7,0},{8,9},{9,10},{10,1... | collective-permute-start | bytes 983048 | tf_op jit(solution)/shard_map/ppermute | solution.py:331
  37.2 9.0 %collective-permute-start.4 = (bf16[4,320,128]{2,1,0:T(8,128)(2,1)S(1)}, bf16[4,320,128]{2,1,0:T(8,128)(2,1)S(1)}, u32[]{:S(2)}, u32[]{:S(2)}) collective-permute-start(bf16[4,320,128]{2,1,0:T(8,128)(2,1)S(1)} %collective-permute-done.2.refs_1_), channel_id=1, source_target_pairs={{0,7},{1,0},{2,1},{3,2},{4,3},{5,4},{6,5},{7,6},{8,15},{9,8},{10,9... | collective-permute-start | bytes 983048 | tf_op jit(solution)/shard_map/ppermute | solution.py:331
  44.3 9.0 %collective-permute-start.3 = (bf16[4,320,128]{2,1,0:T(8,128)(2,1)S(1)}, bf16[4,320,128]{2,1,0:T(8,128)(2,1)S(1)}, u32[]{:S(2)}, u32[]{:S(2)}) collective-permute-start(bf16[4,320,128]{2,1,0:T(8,128)(2,1)S(1)} %collective-permute-done.1.refs_0_), channel_id=1, source_target_pairs={{0,1},{1,2},{2,3},{3,4},{4,5},{5,6},{6,7},{7,0},{8,9},{9,10},{10,1... | collective-permute-start | bytes 983048 | tf_op jit(solution)/shard_map/ppermute | solution.py:343
  46.2 9.0 %collective-permute-start.6 = (bf16[4,320,128]{2,1,0:T(8,128)(2,1)S(1)}, bf16[4,320,128]{2,1,0:T(8,128)(2,1)S(1)}, u32[]{:S(2)}, u32[]{:S(2)}) collective-permute-start(bf16[4,320,128]{2,1,0:T(8,128)(2,1)S(1)} %collective-permute-done.4.refs_1_), channel_id=1, source_target_pairs={{0,7},{1,0},{2,1},{3,2},{4,3},{5,4},{6,5},{7,6},{8,15},{9,8},{10,9... | collective-permute-start | bytes 983048 | tf_op jit(solution)/shard_map/ppermute | solution.py:343
  53.3 9.0 %collective-permute-start.5 = (bf16[4,320,128]{2,1,0:T(8,128)(2,1)S(1)}, bf16[4,320,128]{2,1,0:T(8,128)(2,1)S(1)}, u32[]{:S(2)}, u32[]{:S(2)}) collective-permute-start(bf16[4,320,128]{2,1,0:T(8,128)(2,1)S(1)} %collective-permute-done.3.refs_0_), channel_id=1, source_target_pairs={{0,1},{1,2},{2,3},{3,4},{4,5},{5,6},{6,7},{7,0},{8,9},{9,10},{10,1... | collective-permute-start | bytes 983048 | tf_op jit(solution)/shard_map/ppermute | solution.py:348
  55.2 7.1 %copy-start.6 = (s32[1,512]{1,0:T(1,128)S(1)}, s32[1,512]{1,0:T(1,128)}, u32[]{:S(2)}) copy-start(s32[1,512]{1,0:T(1,128)} %ids_ref.3) | copy-start | bytes 6148
  55.2 11.7 %copy-start.1 = (bf16[448,4096]{1,0:T(8,128)(2,1)S(1)}, bf16[448,4096]{1,0:T(8,128)(2,1)}, u32[]{:S(2)}) copy-start(bf16[448,4096]{1,0:T(8,128)(2,1)} %w_ref.1) | copy-start | bytes 11010052
  62.8 6.6 %collective-permute-start.8 = (f32[64,128]{1,0:T(8,128)S(1)}, f32[64,128]{1,0:T(8,128)S(1)}, u32[]{:S(2)}, u32[]{:S(2)}) collective-permute-start(f32[64,128]{1,0:T(8,128)S(1)} %get-tuple-element.47.own_ref), channel_id=1, source_target_pairs={{0,16},{1,17},{2,18},{3,19},{4,20},{5,21},{6,22},{7,23},{8,24},{9,... | collective-permute-start | bytes 98312 | tf_op jit(solution)/shard_map/ppermute | solution.py:358
  69.3 13.3 %collective-permute-start.9 = (bf16[224,5248]{1,0:T(8,128)(2,1)S(1)}, bf16[224,5248]{1,0:T(8,128)(2,1)S(1)}, u32[]{:S(2)}, u32[]{:S(2)}) collective-permute-start(bf16[224,5248]{1,0:T(8,128)(2,1)S(1)} %collective-permute-done.7.refs_0_.near_ref), channel_id=1, source_target_pairs={{0,32},{32,0},{64,96},{96,64},{128,160},{160,128},{192,224},{224,1... | collective-permute-start | bytes 7053320 | tf_op jit(solution)/shard_map/ppermute | solution.py:367

commit v7 on v6

--- a/solution.py
+++ b/solution.py
@@ -111,11 +111,11 @@
         sent_ref[x] = jnp.concatenate([*own, *halves(factors[:, x * share : (x + 1) * share])], axis=0)
 
 
-def lend_kernel(w_hbm, gate_ref, up_ref, gate_proj, up_proj, lent_ref, sems):
+def lend_kernel(w_ref, gate_ref, up_ref, gate_proj, up_proj, lent_ref):
     _, _, own, core = place()
-    rows, features = lent_ref.shape[0], w_hbm.shape[1]
+    rows, features = lent_ref.shape[0], w_ref.shape[1]
     half = gate_ref.shape[1] // 2
-    copies = fetch([(w_hbm.at[span(core, rows)], lent_ref.at[:, :features])], sems)
+    lent_ref[:, :features] = w_ref[span(core, rows)]
     gate, up = quarters(gate_ref, 1 - own), quarters(up_ref, 1 - own)
     for k in range(2):
         part, first = slice(k * rows, (k + 1) * rows), features + k * 2 * half
@@ -124,7 +124,6 @@
     proj = jnp.concatenate([gate_proj[...], up_proj[...]], axis=0).astype(F32).T.astype(BF16)
     proj = jnp.where(core == 0, proj[:rows].astype(F32), proj[rows:].astype(F32))
     lent_ref[:, features + 4 * half :] = proj.astype(BF16)
-    wait(copies)
 
 
 def split_kernel(got_ref, block_ref, both_ref, hid_ref):
@@ -250,8 +249,9 @@
     wide = total.shape[1]
     product = product[:, :wide] + product[:, wide:] + mm(low_ref[...], high)
     devices = sent_ref.shape[0]
-    sent_ref[:, : 2 * SEQ_DEV] = product.reshape(devices, 2 * SEQ_DEV, wide)
-    sent_ref[:, 2 * SEQ_DEV :] = down_ref[...]
+    product = product.reshape(devices, 2 * SEQ_DEV, wide)
+    parts = [product] + [part.astype(F32) for part in halves(down_ref[...])]
+    sent_ref[...] = jnp.concatenate(parts, axis=1).astype(BF16)
 
 
 def per_device(
@@ -302,10 +302,9 @@
     lent = call(
         lend_kernel,
         shape((hidden // 2, features + 4 * half + 2 * rank), BF16),
-        [HBM] + [VMEM] * 4,
+        [VMEM] * 5,
         (lent_w, gate_turned, up_turned, proj_gate.T, proj_upward.T),
         w_down.size,
-        scratch=[pltpu.SemaphoreType.DMA((1,))],
     )
     got = lax.all_to_all(sent, "mp", 0, 0, axis_index_groups=X_GROUPS)
     near = lax.ppermute(lent, "mp", PARTNER)
@@ -388,13 +387,14 @@
     )
     sent = call(
         last_kernel,
-        shape((mp_size, 3 * SEQ_DEV, 2 * rank)),
+        shape((mp_size, 4 * SEQ_DEV, 2 * rank), BF16),
         [VMEM] * 4,
         (total, high, low, down_raw),
         6 * high.size * rank,
     )
-    got = jnp.sum(lax.all_to_all(sent, "mp", 0, 0), axis=0)
-    paired, down_raw = got[: 2 * SEQ_DEV], got[2 * SEQ_DEV :]
+    got = jnp.sum(lax.all_to_all(sent, "mp", 0, 0).astype(F32), axis=0)
+    paired = got[: 2 * SEQ_DEV]
+    down_raw = got[2 * SEQ_DEV : 3 * SEQ_DEV] + got[3 * SEQ_DEV :]
     paired = paired.reshape(2, SEQ_DEV, 2, rank).transpose(1, 2, 0, 3).reshape(SEQ_DEV, 2, 2 * rank)
     raw = jnp.concatenate([paired, down_raw[:, None]], axis=1)
 

time: 135 us -> 133 us (0.985)
  blocking collectives: 49.1 us -> 46.4 us
    all_to_all x1, blocking collectives: 16.7 us -> 14.7 us  [per_device(): got = jnp.sum(lax.all_to_all(sent, 'mp', 0, 0).astype(F32), axis=0)]
where the time goes in v7:
time: 133 us; the launch traced here: 132 us
  starting transfers between devices  51.5 us (39%)
  blocking collectives  46.4 us (35%)
  waiting for transfers between devices  20 us (15%)
  Pallas kernels  10.7 us (8%)
  local copies, waits for them, and re-layouts  2.26 us (2%)
    all_to_all x2, blocking collectives, per_device(): lax.all_to_all(jnp.broadcast_to(squares, (size, 1, 128)), axis, 0, 0)  31.6 us
    ppermute x3, starting transfers between devices, per_device(): lax.ppermute(down, 'mp', z_shift(-1))  17.7 us
    all_to_all x1, blocking collectives, per_device(): got = jnp.sum(lax.all_to_all(sent, 'mp', 0, 0).astype(F32), axis=0)  14.7 us
    pallas_call x14, Pallas kernels, call(): pl.pallas_call(kernel, out_shape=out_shape, in_specs=specs, out_specs=out...  10.7 us
    ppermute x3, starting transfers between devices, per_device(): lax.ppermute(up, 'mp', z_shift(1))  10.4 us
    ppermute x1, starting transfers between devices, per_device(): other = lax.ppermute(near, 'dp', cores)  9.16 us
    ppermute x3, waiting for transfers between devices, per_device(): lax.ppermute(up, 'mp', z_shift(1))  7.91 us
    ppermute x1, waiting for transfers between devices, per_device(): far = lax.ppermute(up, 'mp', z_shift(1))  6.88 us
  transfers between devices with their start and end apart: 11, of which 7 were waited for; matrix products, arithmetic and copies ran while one was open for 0% of the time, Pallas kernels for 5%

profile of v7, /device:TPU:1, one launch (start us, length us, event | category | flops | bytes accessed | tf_op | source)
XLA Modules:
  0.0 132.0 jit_solution(17377865249940437388)
XLA Ops:
  0.0 0.0 copy-start.2
  0.0 0.0 copy-start.3
  0.0 0.0 copy-start.4
  0.0 0.0 copy-start.5
  0.0 2.7 %shard_map.109 = bf16[4,640,128]{2,1,0:T(8,128)(2,1)} custom-call(bf16[512,128]{1,0:T(8,128)(2,1)} %input_hbm.1, bf16[512,128]{1,0:T(8,128)(2,1)} %grad_hbm.1, bf16[448,512]{1,0:T(8,128)(2,1)} %bitcast.16, bf16[448,512]{1,0:T(8,128)(2,1)} %bitcast.19, bf16[64,128]{1,0:T(8,128)(2,1)} %bitcast.30, bf16[64,128]{1,0:T(8,128)(2,1)} %proj_out_hbm.1, ...), custom_call_target="tpu_custom_call" | custom-call | flops 46137344 | bytes 1269760 | tf_op jit(solution)/shard_map/pallas_call | solution.py:60
  2.7 4.9 %all-to-all-start = ((bf16[4,640,128]{2,1,0:T(8,128)(2,1)}), bf16[4,640,128]{2,1,0:T(8,128)(2,1)}, u32[]{:S(2)}, u32[]{:S(2)}) async-start(bf16[4,640,128]{2,1,0:T(8,128)(2,1)} %shard_map.109), calls=%async_computation | async-start | bytes 1310720 | tf_op jit(solution)/shard_map/all_to_all | solution.py:309
  7.5 0.0 copy-done.2
  7.5 0.0 copy-done.3
  7.5 0.0 copy-done.4
  7.6 0.0 copy-done.5
  7.6 0.0 copy-start
  7.6 2.0 %copy-done = bf16[448,4096]{1,0:T(8,128)(2,1)S(1)} copy-done((bf16[448,4096]{1,0:T(8,128)(2,1)S(1)}, bf16[448,4096]{1,0:T(8,128)(2,1)}, u32[]{:S(2)}) %copy-start) | copy-done | bytes 3670040
  9.6 1.6 %shard_map.110 = bf16[224,5248]{1,0:T(8,128)(2,1)} custom-call(bf16[448,4096]{1,0:T(8,128)(2,1)S(1)} %copy-done, bf16[448,512]{1,0:T(8,128)(2,1)S(1)} %bitcast.17, bf16[448,512]{1,0:T(8,128)(2,1)S(1)} %bitcast.20, bf16[64,448]{1,0:T(8,128)(2,1)S(1)} %bitcast.22, bf16[64,448]{1,0:T(8,128)(2,1)S(1)} %bitcast.24), custom_call_target="tpu_custom_call" | custom-call | flops 1835008 | bytes 4702208 | tf_op jit(solution)/shard_map/pallas_call | solution.py:60
  11.2 3.4 %collective-permute-start.7 = (bf16[224,5248]{1,0:T(8,128)(2,1)}, bf16[224,5248]{1,0:T(8,128)(2,1)S(1)}, u32[]{:S(2)}, u32[]{:S(2)}) collective-permute-start(bf16[224,5248]{1,0:T(8,128)(2,1)} %shard_map.110), channel_id=1, source_target_pairs={{0,8},{1,9},{2,10},{3,11},{4,12},{5,13},{6,14},{7,15},{8,0},{9,1},... | collective-permute-start | bytes 7053320 | tf_op jit(solution)/shard_map/ppermute | solution.py:310
  14.6 0.7 all-to-all-done.got_ref
  15.3 1.1 shard_map.111
  16.4 6.6 %collective-permute-start = (bf16[4,320,128]{2,1,0:T(8,128)(2,1)S(1)}, bf16[4,320,128]{2,1,0:T(8,128)(2,1)S(1)}, u32[]{:S(2)}, u32[]{:S(2)}) collective-permute-start(bf16[4,320,128]{2,1,0:T(8,128)(2,1)S(1)} %get-tuple-element.33.block_ref), channel_id=1, source_target_pairs={{0,1},{1,2},{2,3},{3,4},{4,5},{5,6},{6,7},{7,0},{8,9},{9,10},{10,1... | collective-permute-start | bytes 983048 | tf_op jit(solution)/shard_map/ppermute | solution.py:325
  23.0 8.6 %collective-permute-start.2 = (bf16[4,320,128]{2,1,0:T(8,128)(2,1)S(1)}, bf16[4,320,128]{2,1,0:T(8,128)(2,1)S(1)}, u32[]{:S(2)}, u32[]{:S(2)}) collective-permute-start(bf16[4,320,128]{2,1,0:T(8,128)(2,1)S(1)} %get-tuple-element.33.block_ref), channel_id=1, source_target_pairs={{0,7},{1,0},{2,1},{3,2},{4,3},{5,4},{6,5},{7,6},{8,15},{9,8},{10,9... | collective-permute-start | bytes 983048 | tf_op jit(solution)/shard_map/ppermute | solution.py:325
  31.6 0.3 shard_map.114
  31.9 0.1 shard_map.112.refs_2_
  32.0 3.3 %collective-permute-done.refs_0_ = bf16[4,320,128]{2,1,0:T(8,128)(2,1)S(1)} collective-permute-done((bf16[4,320,128]{2,1,0:T(8,128)(2,1)S(1)}, bf16[4,320,128]{2,1,0:T(8,128)(2,1)S(1)}, u32[]{:S(2)}, u32[]{:S(2)}) %collective-permute-start) | collective-permute-done | bytes 327712 | tf_op jit(solution)/shard_map/ppermute | solution.py:325
  35.2 1.9 %collective-permute-start.1 = (bf16[4,320,128]{2,1,0:T(8,128)(2,1)S(1)}, bf16[4,320,128]{2,1,0:T(8,128)(2,1)S(1)}, u32[]{:S(2)}, u32[]{:S(2)}) collective-permute-start(bf16[4,320,128]{2,1,0:T(8,128)(2,1)S(1)} %collective-permute-done.refs_0_), channel_id=1, source_target_pairs={{0,1},{1,2},{2,3},{3,4},{4,5},{5,6},{6,7},{7,0},{8,9},{9,10},{10,1... | collective-permute-start | bytes 983048 | tf_op jit(solution)/shard_map/ppermute | solution.py:330
  37.1 0.0 collective-permute-done.2.refs_1_
  37.2 4.6 %collective-permute-start.4 = (bf16[4,320,128]{2,1,0:T(8,128)(2,1)S(1)}, bf16[4,320,128]{2,1,0:T(8,128)(2,1)S(1)}, u32[]{:S(2)}, u32[]{:S(2)}) collective-permute-start(bf16[4,320,128]{2,1,0:T(8,128)(2,1)S(1)} %collective-permute-done.2.refs_1_), channel_id=1, source_target_pairs={{0,7},{1,0},{2,1},{3,2},{4,3},{5,4},{6,5},{7,6},{8,15},{9,8},{10,9... | collective-permute-start | bytes 983048 | tf_op jit(solution)/shard_map/ppermute | solution.py:330
  41.7 0.2 shard_map.113
  41.9 2.3 %collective-permute-done.1.refs_0_ = bf16[4,320,128]{2,1,0:T(8,128)(2,1)S(1)} collective-permute-done((bf16[4,320,128]{2,1,0:T(8,128)(2,1)S(1)}, bf16[4,320,128]{2,1,0:T(8,128)(2,1)S(1)}, u32[]{:S(2)}, u32[]{:S(2)}) %collective-permute-start.1) | collective-permute-done | bytes 327712 | tf_op jit(solution)/shard_map/ppermute | solution.py:330
  44.3 1.9 %collective-permute-start.3 = (bf16[4,320,128]{2,1,0:T(8,128)(2,1)S(1)}, bf16[4,320,128]{2,1,0:T(8,128)(2,1)S(1)}, u32[]{:S(2)}, u32[]{:S(2)}) collective-permute-start(bf16[4,320,128]{2,1,0:T(8,128)(2,1)S(1)} %collective-permute-done.1.refs_0_), channel_id=1, source_target_pairs={{0,1},{1,2},{2,3},{3,4},{4,5},{5,6},{6,7},{7,0},{8,9},{9,10},{10,1... | collective-permute-start | bytes 983048 | tf_op jit(solution)/shard_map/ppermute | solution.py:342
  46.2 0.0 collective-permute-done.4.refs_1_
  46.2 4.6 %collective-permute-start.6 = (bf16[4,320,128]{2,1,0:T(8,128)(2,1)S(1)}, bf16[4,320,128]{2,1,0:T(8,128)(2,1)S(1)}, u32[]{:S(2)}, u32[]{:S(2)}) collective-permute-start(bf16[4,320,128]{2,1,0:T(8,128)(2,1)S(1)} %collective-permute-done.4.refs_1_), channel_id=1, source_target_pairs={{0,7},{1,0},{2,1},{3,2},{4,3},{5,4},{6,5},{7,6},{8,15},{9,8},{10,9... | collective-permute-start | bytes 983048 | tf_op jit(solution)/shard_map/ppermute | solution.py:342
  50.8 0.2 shard_map.115
  50.9 2.3 %collective-permute-done.3.refs_0_ = bf16[4,320,128]{2,1,0:T(8,128)(2,1)S(1)} collective-permute-done((bf16[4,320,128]{2,1,0:T(8,128)(2,1)S(1)}, bf16[4,320,128]{2,1,0:T(8,128)(2,1)S(1)}, u32[]{:S(2)}, u32[]{:S(2)}) %collective-permute-start.3) | collective-permute-done | bytes 327712 | tf_op jit(solution)/shard_map/ppermute | solution.py:342
  53.3 1.9 %collective-permute-start.5 = (bf16[4,320,128]{2,1,0:T(8,128)(2,1)S(1)}, bf16[4,320,128]{2,1,0:T(8,128)(2,1)S(1)}, u32[]{:S(2)}, u32[]{:S(2)}) collective-permute-start(bf16[4,320,128]{2,1,0:T(8,128)(2,1)S(1)} %collective-permute-done.3.refs_0_), channel_id=1, source_target_pairs={{0,1},{1,2},{2,3},{3,4},{4,5},{5,6},{6,7},{7,0},{8,9},{9,10},{10,1... | collective-permute-start | bytes 983048 | tf_op jit(solution)/shard_map/ppermute | solution.py:347
  55.2 0.0 collective-permute-done.6.refs_1_
  55.2 0.0 copy-start.6
  55.2 0.0 copy-start.1
  55.2 0.2 shard_map.116
  55.4 6.9 %collective-permute-done.5.block_ref = bf16[4,320,128]{2,1,0:T(8,128)(2,1)S(1)} collective-permute-done((bf16[4,320,128]{2,1,0:T(8,128)(2,1)S(1)}, bf16[4,320,128]{2,1,0:T(8,128)(2,1)S(1)}, u32[]{:S(2)}, u32[]{:S(2)}) %collective-permute-start.5) | collective-permute-done | bytes 327712 | tf_op jit(solution)/shard_map/ppermute | solution.py:347
  62.3 0.0 copy-done.6
  62.3 0.5 shard_map.117
  62.8 4.1 %collective-permute-start.8 = (f32[64,128]{1,0:T(8,128)S(1)}, f32[64,128]{1,0:T(8,128)S(1)}, u32[]{:S(2)}, u32[]{:S(2)}) collective-permute-start(f32[64,128]{1,0:T(8,128)S(1)} %get-tuple-element.47.own_ref), channel_id=1, source_target_pairs={{0,16},{1,17},{2,18},{3,19},{4,20},{5,21},{6,22},{7,23},{8,24},{9,... | collective-permute-start | bytes 98312 | tf_op jit(solution)/shard_map/ppermute | solution.py:357
  66.9 0.0 copy-done.1
  66.9 1.6 %shard_map.118.own_ref = f32[256,128]{1,0:T(8,128)S(1)} custom-call(bf16[256,4096]{1,0:T(8,128)(2,1)S(1)} %get-tuple-element.46.grad_ref, bf16[448,4096]{1,0:T(8,128)(2,1)S(1)} %copy-done.1, f32[256,448]{1,0:T(8,128)S(1)} %get-tuple-element.48.activated_ref, f32[256,448]{1,0:T(8,128)S(1)} %get-tuple-element.37.slope_ref, bf16[64,448]{1,0:T(8,128)(2,1)S(1)} %bitcast.23, ...), custom_call_target="tpu_custom_call" | custom-call | flops 939524096 | bytes 6799360 | tf_op jit(solution)/shard_map/pallas_call | solution.py:60
  68.5 0.9 collective-permute-done.8.other_ref
  69.3 0.0 collective-permute-done.7.refs_0_.near_ref
  69.3 9.2 %collective-permute-start.9 = (bf16[224,5248]{1,0:T(8,128)(2,1)S(1)}, bf16[224,5248]{1,0:T(8,128)(2,1)S(1)}, u32[]{:S(2)}, u32[]{:S(2)}) collective-permute-start(bf16[224,5248]{1,0:T(8,128)(2,1)S(1)} %collective-permute-done.7.refs_0_.near_ref), channel_id=1, source_target_pairs={{0,32},{32,0},{64,96},{96,64},{128,160},{160,128},{192,224},{224,1... | collective-permute-start | bytes 7053320 | tf_op jit(solution)/shard_map/ppermute | solution.py:366
  78.5 0.1 shard_map.121
  78.7 0.3 shard_map.119
  79.0 3.7 %collective-permute-done.9.other_ref = bf16[224,5248]{1,0:T(8,128)(2,1)S(1)} collective-permute-done((bf16[224,5248]{1,0:T(8,128)(2,1)S(1)}, bf16[224,5248]{1,0:T(8,128)(2,1)S(1)}, u32[]{:S(2)}, u32[]{:S(2)}) %collective-permute-start.9) | collective-permute-done | bytes 2351136 | tf_op jit(solution)/shard_map/ppermute | solution.py:366
  82.6 1.6 %shard_map.120.total_ref = f32[256,128]{1,0:T(8,128)S(1)} custom-call(bf16[256,4096]{1,0:T(8,128)(2,1)S(1)} %get-tuple-element.46.grad_ref, bf16[224,5248]{1,0:T(8,128)(2,1)S(1)} %collective-permute-done.7.refs_0_.near_ref, bf16[224,5248]{1,0:T(8,128)(2,1)S(1)} %collective-permute-done.9.other_ref, f32[256,448]{1,0:T(8,128)S(1)} %get-tuple-element.50.activated_ref, ...), custom_call_target="tpu_custom_call" | custom-call | flops 939524096 | bytes 7847936 | tf_op jit(solution)/shard_map/pallas_call | solution.py:60
  84.3 0.3 shard_map.122
  84.6 14.7 %all_to_all.20 = bf16[32,32,128]{2,1,0:T(8,128)(2,1)S(1)} all-to-all(bf16[32,32,128]{2,1,0:T(8,128)(2,1)S(1)} %shard_map.122), channel_id=1, replica_groups=mesh['dp'=16,'mp'=32] {'mp'}, dimensions={0} | all-to-all | bytes 524288 | tf_op jit(solution)/shard_map/all_to_all | solution.py:395
  99.4 0.1 reshape.29
  99.5 0.1 reshape.30
  99.5 0.1 multiply_reduce_fusion
  99.7 15.2 %all_to_all.21 = f32[32,1,128]{2,1,0:T(1,128)S(1)} all-to-all(f32[32,1,128]{2,1,0:T(1,128)S(1)} %broadcast_in_dim.9), channel_id=1, replica_groups=mesh['dp'=16,'mp'=32] {'mp'}, dimensions={0} | all-to-all | bytes 32768 | tf_op jit(solution)/shard_map/all_to_all | solution.py:405
  114.9 16.5 %all_to_all.22 = f32[16,1,128]{2,1,0:T(1,128)S(1)} all-to-all(f32[16,1,128]{2,1,0:T(1,128)S(1)} %broadcast_in_dim.20), channel_id=1, replica_groups=mesh['dp'=16,'mp'=32] {'dp'}, dimensions={0} | all-to-all | bytes 16384 | tf_op jit(solution)/shard_map/all_to_all | solution.py:405
  131.4 0.7 fusion
  (10 shorter events, 0.1 us)
Async XLA Ops:
  0.0 7.5 %copy-start.2 = (bf16[512,448]{0,1:T(8,128)(2,1)S(1)}, bf16[512,448]{0,1:T(8,128)(2,1)}, u32[]{:S(2)}) copy-start(bf16[512,448]{0,1:T(8,128)(2,1)} %param.12) | copy-start | bytes 1376260
  0.0 7.5 %copy-start.3 = (bf16[512,448]{0,1:T(8,128)(2,1)S(1)}, bf16[512,448]{0,1:T(8,128)(2,1)}, u32[]{:S(2)}) copy-start(bf16[512,448]{0,1:T(8,128)(2,1)} %param.13) | copy-start | bytes 1376260
  0.0 7.5 %copy-start.4 = (bf16[448,64]{0,1:T(8,128)(2,1)S(1)}, bf16[448,64]{0,1:T(8,128)(2,1)}, u32[]{:S(2)}) copy-start(bf16[448,64]{0,1:T(8,128)(2,1)} %param.18) | copy-start | bytes 172036
  0.0 7.5 %copy-start.5 = (bf16[448,64]{0,1:T(8,128)(2,1)S(1)}, bf16[448,64]{0,1:T(8,128)(2,1)}, u32[]{:S(2)}) copy-start(bf16[448,64]{0,1:T(8,128)(2,1)} %param.19) | copy-start | bytes 172036
  2.7 12.6 %all-to-all-start = ((bf16[4,640,128]{2,1,0:T(8,128)(2,1)}), bf16[4,640,128]{2,1,0:T(8,128)(2,1)}, u32[]{:S(2)}, u32[]{:S(2)}) async-start(bf16[4,640,128]{2,1,0:T(8,128)(2,1)} %shard_map.109), calls=%async_computation | async-start | bytes 1310720 | tf_op jit(solution)/shard_map/all_to_all | solution.py:309
  7.6 2.0 %copy-start = (bf16[448,4096]{1,0:T(8,128)(2,1)S(1)}, bf16[448,4096]{1,0:T(8,128)(2,1)}, u32[]{:S(2)}) copy-start(bf16[448,4096]{1,0:T(8,128)(2,1)} %w_ref.2) | copy-start | bytes 11010052
  11.2 58.1 %collective-permute-start.7 = (bf16[224,5248]{1,0:T(8,128)(2,1)}, bf16[224,5248]{1,0:T(8,128)(2,1)S(1)}, u32[]{:S(2)}, u32[]{:S(2)}) collective-permute-start(bf16[224,5248]{1,0:T(8,128)(2,1)} %shard_map.110), channel_id=1, source_target_pairs={{0,8},{1,9},{2,10},{3,11},{4,12},{5,13},{6,14},{7,15},{8,0},{9,1},... | collective-permute-start | bytes 7053320 | tf_op jit(solution)/shard_map/ppermute | solution.py:310
  16.4 18.8 %collective-permute-start = (bf16[4,320,128]{2,1,0:T(8,128)(2,1)S(1)}, bf16[4,320,128]{2,1,0:T(8,128)(2,1)S(1)}, u32[]{:S(2)}, u32[]{:S(2)}) collective-permute-start(bf16[4,320,128]{2,1,0:T(8,128)(2,1)S(1)} %get-tuple-element.33.block_ref), channel_id=1, source_target_pairs={{0,1},{1,2},{2,3},{3,4},{4,5},{5,6},{6,7},{7,0},{8,9},{9,10},{10,1... | collective-permute-start | bytes 983048 | tf_op jit(solution)/shard_map/ppermute | solution.py:325
  23.0 14.2 %collective-permute-start.2 = (bf16[4,320,128]{2,1,0:T(8,128)(2,1)S(1)}, bf16[4,320,128]{2,1,0:T(8,128)(2,1)S(1)}, u32[]{:S(2)}, u32[]{:S(2)}) collective-permute-start(bf16[4,320,128]{2,1,0:T(8,128)(2,1)S(1)} %get-tuple-element.33.block_ref), channel_id=1, source_target_pairs={{0,7},{1,0},{2,1},{3,2},{4,3},{5,4},{6,5},{7,6},{8,15},{9,8},{10,9... | collective-permute-start | bytes 983048 | tf_op jit(solution)/shard_map/ppermute | solution.py:325
  35.2 9.0 %collective-permute-start.1 = (bf16[4,320,128]{2,1,0:T(8,128)(2,1)S(1)}, bf16[4,320,128]{2,1,0:T(8,128)(2,1)S(1)}, u32[]{:S(2)}, u32[]{:S(2)}) collective-permute-start(bf16[4,320,128]{2,1,0:T(8,128)(2,1)S(1)} %collective-permute-done.refs_0_), channel_id=1, source_target_pairs={{0,1},{1,2},{2,3},{3,4},{4,5},{5,6},{6,7},{7,0},{8,9},{9,10},{10,1... | collective-permute-start | bytes 983048 | tf_op jit(solution)/shard_map/ppermute | solution.py:330
  37.2 9.0 %collective-permute-start.4 = (bf16[4,320,128]{2,1,0:T(8,128)(2,1)S(1)}, bf16[4,320,128]{2,1,0:T(8,128)(2,1)S(1)}, u32[]{:S(2)}, u32[]{:S(2)}) collective-permute-start(bf16[4,320,128]{2,1,0:T(8,128)(2,1)S(1)} %collective-permute-done.2.refs_1_), channel_id=1, source_target_pairs={{0,7},{1,0},{2,1},{3,2},{4,3},{5,4},{6,5},{7,6},{8,15},{9,8},{10,9... | collective-permute-start | bytes 983048 | tf_op jit(solution)/shard_map/ppermute | solution.py:330
  44.3 9.0 %collective-permute-start.3 = (bf16[4,320,128]{2,1,0:T(8,128)(2,1)S(1)}, bf16[4,320,128]{2,1,0:T(8,128)(2,1)S(1)}, u32[]{:S(2)}, u32[]{:S(2)}) collective-permute-start(bf16[4,320,128]{2,1,0:T(8,128)(2,1)S(1)} %collective-permute-done.1.refs_0_), channel_id=1, source_target_pairs={{0,1},{1,2},{2,3},{3,4},{4,5},{5,6},{6,7},{7,0},{8,9},{9,10},{10,1... | collective-permute-start | bytes 983048 | tf_op jit(solution)/shard_map/ppermute | solution.py:342
  46.2 9.0 %collective-permute-start.6 = (bf16[4,320,128]{2,1,0:T(8,128)(2,1)S(1)}, bf16[4,320,128]{2,1,0:T(8,128)(2,1)S(1)}, u32[]{:S(2)}, u32[]{:S(2)}) collective-permute-start(bf16[4,320,128]{2,1,0:T(8,128)(2,1)S(1)} %collective-permute-done.4.refs_1_), channel_id=1, source_target_pairs={{0,7},{1,0},{2,1},{3,2},{4,3},{5,4},{6,5},{7,6},{8,15},{9,8},{10,9... | collective-permute-start | bytes 983048 | tf_op jit(solution)/shard_map/ppermute | solution.py:342
  53.3 9.0 %collective-permute-start.5 = (bf16[4,320,128]{2,1,0:T(8,128)(2,1)S(1)}, bf16[4,320,128]{2,1,0:T(8,128)(2,1)S(1)}, u32[]{:S(2)}, u32[]{:S(2)}) collective-permute-start(bf16[4,320,128]{2,1,0:T(8,128)(2,1)S(1)} %collective-permute-done.3.refs_0_), channel_id=1, source_target_pairs={{0,1},{1,2},{2,3},{3,4},{4,5},{5,6},{6,7},{7,0},{8,9},{9,10},{10,1... | collective-permute-start | bytes 983048 | tf_op jit(solution)/shard_map/ppermute | solution.py:347
  55.2 7.1 %copy-start.6 = (s32[1,512]{1,0:T(1,128)S(1)}, s32[1,512]{1,0:T(1,128)}, u32[]{:S(2)}) copy-start(s32[1,512]{1,0:T(1,128)} %ids_ref.3) | copy-start | bytes 6148
  55.2 11.7 %copy-start.1 = (bf16[448,4096]{1,0:T(8,128)(2,1)S(1)}, bf16[448,4096]{1,0:T(8,128)(2,1)}, u32[]{:S(2)}) copy-start(bf16[448,4096]{1,0:T(8,128)(2,1)} %w_ref.2) | copy-start | bytes 11010052
  62.8 6.6 %collective-permute-start.8 = (f32[64,128]{1,0:T(8,128)S(1)}, f32[64,128]{1,0:T(8,128)S(1)}, u32[]{:S(2)}, u32[]{:S(2)}) collective-permute-start(f32[64,128]{1,0:T(8,128)S(1)} %get-tuple-element.47.own_ref), channel_id=1, source_target_pairs={{0,16},{1,17},{2,18},{3,19},{4,20},{5,21},{6,22},{7,23},{8,24},{9,... | collective-permute-start | bytes 98312 | tf_op jit(solution)/shard_map/ppermute | solution.py:357
  69.3 13.3 %collective-permute-start.9 = (bf16[224,5248]{1,0:T(8,128)(2,1)S(1)}, bf16[224,5248]{1,0:T(8,128)(2,1)S(1)}, u32[]{:S(2)}, u32[]{:S(2)}) collective-permute-start(bf16[224,5248]{1,0:T(8,128)(2,1)S(1)} %collective-permute-done.7.refs_0_.near_ref), channel_id=1, source_target_pairs={{0,32},{32,0},{64,96},{96,64},{128,160},{160,128},{192,224},{224,1... | collective-permute-start | bytes 7053320 | tf_op jit(solution)/shard_map/ppermute | solution.py:366

commit v8 on v7

--- a/solution.py
+++ b/solution.py
@@ -362,21 +362,21 @@
         (grad, w_down, activated, slope, proj_gate.T, proj_upward.T),
         2 * half * hidden * features,
     )
-    near, other_factor, own_factors = lax.optimization_barrier((near, other_factor, own_factors))
+    near = tie(near, in_factor)
     other = lax.ppermute(near, "dp", cores)
     lent_activated, lent_slope = call(
         lambda *refs: lent_kernel(features, *refs),
         (shape((half, hidden)), shape((half, hidden))),
         [VMEM],
         (near,),
-        lent.size,
+        20000000000,
     )
     high, low = call(
         left_kernel,
         (shape((rank * SEQ_DEV, half), BF16), shape((rank * SEQ_DEV, half), BF16)),
         [VMEM] * 3,
         (in_factor, other_factor, seq_ids),
-        SEQ_DEV * half * rank,
+        20000000000,
     )
     total = call(
         partner_kernel,

time: 133 us -> 134 us (level)
  blocking collectives: 46.4 us -> 49.7 us
  Pallas kernels: 10.7 us -> 13 us
  waiting for transfers between devices: 20 us -> 17.7 us
  starting transfers between devices: 51.5 us -> 49.5 us
    all_to_all x1, blocking collectives: 14.7 us -> 18.1 us  [per_device(): got = jnp.sum(lax.all_to_all(sent, 'mp', 0, 0).astype(F32), axis=0)]
    pallas_call x14, Pallas kernels: 10.7 us -> 13 us  [call(): pl.pallas_call(kernel, out_shape=out_shape, in_specs=specs, out_specs=out...]
    ppermute x1, waiting for transfers between devices: 3.68 us -> 2.23 us  [per_device(): other = lax.ppermute(near, 'dp', cores)]
  transfers between devices with their start and end apart: 11 -> 11, of which waited for: 7 -> 6; matrix products, arithmetic and copies ran while one was open for 0% -> 0% of each run, Pallas kernels for 5% -> 5%
where the time goes in v8:
time: 134 us; the launch traced here: 133 us
  blocking collectives  49.7 us (37%)
  starting transfers between devices  49.5 us (37%)
  waiting for transfers between devices  17.7 us (13%)
  Pallas kernels  13 us (10%)
  local copies, waits for them, and re-layouts  2.26 us (2%)
    all_to_all x2, blocking collectives, per_device(): lax.all_to_all(jnp.broadcast_to(squares, (size, 1, 128)), axis, 0, 0)  31.6 us
    all_to_all x1, blocking collectives, per_device(): got = jnp.sum(lax.all_to_all(sent, 'mp', 0, 0).astype(F32), axis=0)  18.1 us
    ppermute x3, starting transfers between devices, per_device(): lax.ppermute(down, 'mp', z_shift(-1))  17.7 us
    pallas_call x14, Pallas kernels, call(): pl.pallas_call(kernel, out_shape=out_shape, in_specs=specs, out_specs=out...  13 us
    ppermute x3, starting transfers between devices, per_device(): lax.ppermute(up, 'mp', z_shift(1))  10.2 us
    ppermute x3, waiting for transfers between devices, per_device(): lax.ppermute(up, 'mp', z_shift(1))  7.99 us
    ppermute x1, starting transfers between devices, per_device(): other = lax.ppermute(near, 'dp', cores)  7.83 us
    ppermute x1, waiting for transfers between devices, per_device(): far = lax.ppermute(up, 'mp', z_shift(1))  6.88 us
  transfers between devices with their start and end apart: 11, of which 6 were waited for; matrix products, arithmetic and copies ran while one was open for 0% of the time, Pallas kernels for 5%

profile of v8, /device:TPU:1, one launch (start us, length us, event | category | flops | bytes accessed | tf_op | source)
XLA Modules:
  0.0 133.3 jit_solution(12618224116777960056)
XLA Ops:
  0.0 0.0 copy-start.3
  0.0 0.0 copy-start.2
  0.0 0.0 copy-start.5
  0.0 0.0 copy-start.4
  0.0 2.7 %shard_map.109 = bf16[4,640,128]{2,1,0:T(8,128)(2,1)} custom-call(bf16[512,128]{1,0:T(8,128)(2,1)} %input_hbm.1, bf16[512,128]{1,0:T(8,128)(2,1)} %grad_hbm.1, bf16[448,512]{1,0:T(8,128)(2,1)} %bitcast.16, bf16[448,512]{1,0:T(8,128)(2,1)} %bitcast.19, bf16[64,128]{1,0:T(8,128)(2,1)} %bitcast.30, bf16[64,128]{1,0:T(8,128)(2,1)} %proj_out_hbm.1, ...), custom_call_target="tpu_custom_call" | custom-call | flops 46137344 | bytes 1269760 | tf_op jit(solution)/shard_map/pallas_call | solution.py:60
  2.7 4.9 %all-to-all-start = ((bf16[4,640,128]{2,1,0:T(8,128)(2,1)}), bf16[4,640,128]{2,1,0:T(8,128)(2,1)S(1)}, u32[]{:S(2)}, u32[]{:S(2)}) async-start(bf16[4,640,128]{2,1,0:T(8,128)(2,1)} %shard_map.109), calls=%async_computation | async-start | bytes 1310720 | tf_op jit(solution)/shard_map/all_to_all | solution.py:309
  7.5 0.0 copy-done.3
  7.6 0.0 copy-done.2
  7.6 0.0 copy-done.5
  7.6 0.0 copy-done.4
  7.6 0.0 copy-start
  7.6 2.0 %copy-done = bf16[448,4096]{1,0:T(8,128)(2,1)S(1)} copy-done((bf16[448,4096]{1,0:T(8,128)(2,1)S(1)}, bf16[448,4096]{1,0:T(8,128)(2,1)}, u32[]{:S(2)}) %copy-start) | copy-done | bytes 3670040
  9.6 1.6 %shard_map.110 = bf16[224,5248]{1,0:T(8,128)(2,1)} custom-call(bf16[448,4096]{1,0:T(8,128)(2,1)S(1)} %copy-done, bf16[448,512]{1,0:T(8,128)(2,1)S(1)} %bitcast.17, bf16[448,512]{1,0:T(8,128)(2,1)S(1)} %bitcast.20, bf16[64,448]{1,0:T(8,128)(2,1)S(1)} %bitcast.22, bf16[64,448]{1,0:T(8,128)(2,1)S(1)} %bitcast.24), custom_call_target="tpu_custom_call" | custom-call | flops 1835008 | bytes 4702208 | tf_op jit(solution)/shard_map/pallas_call | solution.py:60
  11.2 3.4 %collective-permute-start.7 = (bf16[224,5248]{1,0:T(8,128)(2,1)}, bf16[224,5248]{1,0:T(8,128)(2,1)}, u32[]{:S(2)}, u32[]{:S(2)}) collective-permute-start(bf16[224,5248]{1,0:T(8,128)(2,1)} %shard_map.110), channel_id=1, source_target_pairs={{0,8},{1,9},{2,10},{3,11},{4,12},{5,13},{6,14},{7,15},{8,0},{9,1},... | collective-permute-start | bytes 7053320 | tf_op jit(solution)/shard_map/ppermute | solution.py:310
  14.6 0.6 all-to-all-done.got_ref
  15.2 0.1 shard_map.111
  15.2 6.3 %collective-permute-start = (bf16[4,320,128]{2,1,0:T(8,128)(2,1)S(1)}, bf16[4,320,128]{2,1,0:T(8,128)(2,1)S(1)}, u32[]{:S(2)}, u32[]{:S(2)}) collective-permute-start(bf16[4,320,128]{2,1,0:T(8,128)(2,1)S(1)} %get-tuple-element.31.block_ref), channel_id=1, source_target_pairs={{0,1},{1,2},{2,3},{3,4},{4,5},{5,6},{6,7},{7,0},{8,9},{9,10},{10,1... | collective-permute-start | bytes 983048 | tf_op jit(solution)/shard_map/ppermute | solution.py:325
  21.6 8.6 %collective-permute-start.2 = (bf16[4,320,128]{2,1,0:T(8,128)(2,1)S(1)}, bf16[4,320,128]{2,1,0:T(8,128)(2,1)S(1)}, u32[]{:S(2)}, u32[]{:S(2)}) collective-permute-start(bf16[4,320,128]{2,1,0:T(8,128)(2,1)S(1)} %get-tuple-element.31.block_ref), channel_id=1, source_target_pairs={{0,7},{1,0},{2,1},{3,2},{4,3},{5,4},{6,5},{7,6},{8,15},{9,8},{10,9... | collective-permute-start | bytes 983048 | tf_op jit(solution)/shard_map/ppermute | solution.py:325
  30.2 0.3 shard_map.114
  30.5 0.1 shard_map.112.refs_2_
  30.6 3.3 %collective-permute-done.refs_0_ = bf16[4,320,128]{2,1,0:T(8,128)(2,1)S(1)} collective-permute-done((bf16[4,320,128]{2,1,0:T(8,128)(2,1)S(1)}, bf16[4,320,128]{2,1,0:T(8,128)(2,1)S(1)}, u32[]{:S(2)}, u32[]{:S(2)}) %collective-permute-start) | collective-permute-done | bytes 327712 | tf_op jit(solution)/shard_map/ppermute | solution.py:325
  33.9 1.9 %collective-permute-start.1 = (bf16[4,320,128]{2,1,0:T(8,128)(2,1)S(1)}, bf16[4,320,128]{2,1,0:T(8,128)(2,1)S(1)}, u32[]{:S(2)}, u32[]{:S(2)}) collective-permute-start(bf16[4,320,128]{2,1,0:T(8,128)(2,1)S(1)} %collective-permute-done.refs_0_), channel_id=1, source_target_pairs={{0,1},{1,2},{2,3},{3,4},{4,5},{5,6},{6,7},{7,0},{8,9},{9,10},{10,1... | collective-permute-start | bytes 983048 | tf_op jit(solution)/shard_map/ppermute | solution.py:330
  35.8 0.0 collective-permute-done.2.refs_1_
  35.8 4.6 %collective-permute-start.4 = (bf16[4,320,128]{2,1,0:T(8,128)(2,1)S(1)}, bf16[4,320,128]{2,1,0:T(8,128)(2,1)S(1)}, u32[]{:S(2)}, u32[]{:S(2)}) collective-permute-start(bf16[4,320,128]{2,1,0:T(8,128)(2,1)S(1)} %collective-permute-done.2.refs_1_), channel_id=1, source_target_pairs={{0,7},{1,0},{2,1},{3,2},{4,3},{5,4},{6,5},{7,6},{8,15},{9,8},{10,9... | collective-permute-start | bytes 983048 | tf_op jit(solution)/shard_map/ppermute | solution.py:330
  40.4 0.2 shard_map.113
  40.6 2.3 %collective-permute-done.1.refs_0_ = bf16[4,320,128]{2,1,0:T(8,128)(2,1)S(1)} collective-permute-done((bf16[4,320,128]{2,1,0:T(8,128)(2,1)S(1)}, bf16[4,320,128]{2,1,0:T(8,128)(2,1)S(1)}, u32[]{:S(2)}, u32[]{:S(2)}) %collective-permute-start.1) | collective-permute-done | bytes 327712 | tf_op jit(solution)/shard_map/ppermute | solution.py:330
  42.9 1.9 %collective-permute-start.3 = (bf16[4,320,128]{2,1,0:T(8,128)(2,1)S(1)}, bf16[4,320,128]{2,1,0:T(8,128)(2,1)S(1)}, u32[]{:S(2)}, u32[]{:S(2)}) collective-permute-start(bf16[4,320,128]{2,1,0:T(8,128)(2,1)S(1)} %collective-permute-done.1.refs_0_), channel_id=1, source_target_pairs={{0,1},{1,2},{2,3},{3,4},{4,5},{5,6},{6,7},{7,0},{8,9},{9,10},{10,1... | collective-permute-start | bytes 983048 | tf_op jit(solution)/shard_map/ppermute | solution.py:342
  44.9 0.0 collective-permute-done.4.refs_1_
  44.9 4.6 %collective-permute-start.6 = (bf16[4,320,128]{2,1,0:T(8,128)(2,1)S(1)}, bf16[4,320,128]{2,1,0:T(8,128)(2,1)S(1)}, u32[]{:S(2)}, u32[]{:S(2)}) collective-permute-start(bf16[4,320,128]{2,1,0:T(8,128)(2,1)S(1)} %collective-permute-done.4.refs_1_), channel_id=1, source_target_pairs={{0,7},{1,0},{2,1},{3,2},{4,3},{5,4},{6,5},{7,6},{8,15},{9,8},{10,9... | collective-permute-start | bytes 983048 | tf_op jit(solution)/shard_map/ppermute | solution.py:342
  49.4 0.2 shard_map.115
  49.6 2.3 %collective-permute-done.3.refs_0_ = bf16[4,320,128]{2,1,0:T(8,128)(2,1)S(1)} collective-permute-done((bf16[4,320,128]{2,1,0:T(8,128)(2,1)S(1)}, bf16[4,320,128]{2,1,0:T(8,128)(2,1)S(1)}, u32[]{:S(2)}, u32[]{:S(2)}) %collective-permute-start.3) | collective-permute-done | bytes 327712 | tf_op jit(solution)/shard_map/ppermute | solution.py:342
  52.0 1.9 %collective-permute-start.5 = (bf16[4,320,128]{2,1,0:T(8,128)(2,1)S(1)}, bf16[4,320,128]{2,1,0:T(8,128)(2,1)S(1)}, u32[]{:S(2)}, u32[]{:S(2)}) collective-permute-start(bf16[4,320,128]{2,1,0:T(8,128)(2,1)S(1)} %collective-permute-done.3.refs_0_), channel_id=1, source_target_pairs={{0,1},{1,2},{2,3},{3,4},{4,5},{5,6},{6,7},{7,0},{8,9},{9,10},{10,1... | collective-permute-start | bytes 983048 | tf_op jit(solution)/shard_map/ppermute | solution.py:347
  53.9 0.0 collective-permute-done.6.refs_1_
  53.9 0.0 copy-start.6
  53.9 0.0 copy-start.1
  53.9 0.2 shard_map.116
  54.1 6.9 %collective-permute-done.5.block_ref = bf16[4,320,128]{2,1,0:T(8,128)(2,1)S(1)} collective-permute-done((bf16[4,320,128]{2,1,0:T(8,128)(2,1)S(1)}, bf16[4,320,128]{2,1,0:T(8,128)(2,1)S(1)}, u32[]{:S(2)}, u32[]{:S(2)}) %collective-permute-start.5) | collective-permute-done | bytes 327712 | tf_op jit(solution)/shard_map/ppermute | solution.py:347
  61.0 0.0 copy-done.6
  61.0 0.5 shard_map.117
  61.4 3.7 %collective-permute-start.9 = (f32[64,128]{1,0:T(8,128)S(1)}, f32[64,128]{1,0:T(8,128)S(1)}, u32[]{:S(2)}, u32[]{:S(2)}) collective-permute-start(f32[64,128]{1,0:T(8,128)S(1)} %get-tuple-element.45.own_ref), channel_id=1, source_target_pairs={{0,16},{1,17},{2,18},{3,19},{4,20},{5,21},{6,22},{7,23},{8,24},{9,... | collective-permute-start | bytes 98312 | tf_op jit(solution)/shard_map/ppermute | solution.py:357
  65.1 0.0 copy-done.1
  65.2 1.6 %shard_map.119.own_ref = f32[256,128]{1,0:T(8,128)S(1)} custom-call(bf16[256,4096]{1,0:T(8,128)(2,1)S(1)} %get-tuple-element.44.grad_ref, bf16[448,4096]{1,0:T(8,128)(2,1)S(1)} %copy-done.1, f32[256,448]{1,0:T(8,128)S(1)} %get-tuple-element.49.activated_ref, f32[256,448]{1,0:T(8,128)S(1)} %get-tuple-element.35.slope_ref, bf16[64,448]{1,0:T(8,128)(2,1)S(1)} %bitcast.23, ...), custom_call_target="tpu_custom_call" | custom-call | flops 939524096 | bytes 6799360 | tf_op jit(solution)/shard_map/pallas_call | solution.py:60
  66.7 0.0 collective-permute-done.7.refs_0_.near_ref
  66.7 7.8 %collective-permute-start.8 = (bf16[224,5248]{1,0:T(8,128)(2,1)}, bf16[224,5248]{1,0:T(8,128)(2,1)S(1)}, u32[]{:S(2)}, u32[]{:S(2)}) collective-permute-start(bf16[224,5248]{1,0:T(8,128)(2,1)} %collective-permute-done.7.refs_0_.near_ref), channel_id=1, source_target_pairs={{0,32},{32,0},{64,96},{96,64},{128,160},{160,128},{192,224},{224,1... | collective-permute-start | bytes 7053320 | tf_op jit(solution)/shard_map/ppermute | solution.py:366
  74.6 0.0 collective-permute-done.9.other_ref
  74.6 0.1 shard_map.121
  74.7 1.9 %shard_map.118 = (f32[256,448]{1,0:T(8,128)S(1)}, f32[256,448]{1,0:T(8,128)S(1)}) custom-call(bf16[224,5248]{1,0:T(8,128)(2,1)} %collective-permute-done.7.refs_0_.near_ref), custom_call_target="tpu_custom_call" | custom-call | flops 20000000000 | bytes 2351104 | tf_op jit(solution)/shard_map/pallas_call | solution.py:60
  76.7 2.2 %collective-permute-done.8.other_ref = bf16[224,5248]{1,0:T(8,128)(2,1)S(1)} collective-permute-done((bf16[224,5248]{1,0:T(8,128)(2,1)}, bf16[224,5248]{1,0:T(8,128)(2,1)S(1)}, u32[]{:S(2)}, u32[]{:S(2)}) %collective-permute-start.8) | collective-permute-done | bytes 2351136 | tf_op jit(solution)/shard_map/ppermute | solution.py:366
  78.9 3.3 %shard_map.120.total_ref = f32[256,128]{1,0:T(8,128)S(1)} custom-call(bf16[256,4096]{1,0:T(8,128)(2,1)S(1)} %get-tuple-element.44.grad_ref, bf16[224,5248]{1,0:T(8,128)(2,1)} %collective-permute-done.7.refs_0_.near_ref, bf16[224,5248]{1,0:T(8,128)(2,1)S(1)} %collective-permute-done.8.other_ref, f32[256,448]{1,0:T(8,128)S(1)} %get-tuple-element.47.activated_ref, ...), custom_call_target="tpu_custom_call" | custom-call | flops 939524096 | bytes 7847936 | tf_op jit(solution)/shard_map/pallas_call | solution.py:60
  82.2 0.3 shard_map.122
  82.5 18.1 %all_to_all.20 = bf16[32,32,128]{2,1,0:T(8,128)(2,1)S(1)} all-to-all(bf16[32,32,128]{2,1,0:T(8,128)(2,1)S(1)} %shard_map.122), channel_id=1, replica_groups=mesh['dp'=16,'mp'=32] {'mp'}, dimensions={0} | all-to-all | bytes 524288 | tf_op jit(solution)/shard_map/all_to_all | solution.py:395
  100.7 0.1 reshape.29
  100.8 0.1 reshape.30
  100.8 0.1 multiply_reduce_fusion
  101.0 15.2 %all_to_all.21 = f32[32,1,128]{2,1,0:T(1,128)S(1)} all-to-all(f32[32,1,128]{2,1,0:T(1,128)S(1)} %broadcast_in_dim.9), channel_id=1, replica_groups=mesh['dp'=16,'mp'=32] {'mp'}, dimensions={0} | all-to-all | bytes 32768 | tf_op jit(solution)/shard_map/all_to_all | solution.py:405
  116.2 16.5 %all_to_all.22 = f32[16,1,128]{2,1,0:T(1,128)S(1)} all-to-all(f32[16,1,128]{2,1,0:T(1,128)S(1)} %broadcast_in_dim.20), channel_id=1, replica_groups=mesh['dp'=16,'mp'=32] {'dp'}, dimensions={0} | all-to-all | bytes 16384 | tf_op jit(solution)/shard_map/all_to_all | solution.py:405
  132.7 0.7 fusion
  (10 shorter events, 0.1 us)
Async XLA Ops:
  0.0 7.6 %copy-start.3 = (bf16[512,448]{0,1:T(8,128)(2,1)S(1)}, bf16[512,448]{0,1:T(8,128)(2,1)}, u32[]{:S(2)}) copy-start(bf16[512,448]{0,1:T(8,128)(2,1)} %param.13) | copy-start | bytes 1376260
  0.0 7.6 %copy-start.2 = (bf16[512,448]{0,1:T(8,128)(2,1)S(1)}, bf16[512,448]{0,1:T(8,128)(2,1)}, u32[]{:S(2)}) copy-start(bf16[512,448]{0,1:T(8,128)(2,1)} %param.12) | copy-start | bytes 1376260
  0.0 7.6 %copy-start.5 = (bf16[448,64]{0,1:T(8,128)(2,1)S(1)}, bf16[448,64]{0,1:T(8,128)(2,1)}, u32[]{:S(2)}) copy-start(bf16[448,64]{0,1:T(8,128)(2,1)} %param.19) | copy-start | bytes 172036
  0.0 7.6 %copy-start.4 = (bf16[448,64]{0,1:T(8,128)(2,1)S(1)}, bf16[448,64]{0,1:T(8,128)(2,1)}, u32[]{:S(2)}) copy-start(bf16[448,64]{0,1:T(8,128)(2,1)} %param.18) | copy-start | bytes 172036
  2.7 12.5 %all-to-all-start = ((bf16[4,640,128]{2,1,0:T(8,128)(2,1)}), bf16[4,640,128]{2,1,0:T(8,128)(2,1)S(1)}, u32[]{:S(2)}, u32[]{:S(2)}) async-start(bf16[4,640,128]{2,1,0:T(8,128)(2,1)} %shard_map.109), calls=%async_computation | async-start | bytes 1310720 | tf_op jit(solution)/shard_map/all_to_all | solution.py:309
  7.6 2.0 %copy-start = (bf16[448,4096]{1,0:T(8,128)(2,1)S(1)}, bf16[448,4096]{1,0:T(8,128)(2,1)}, u32[]{:S(2)}) copy-start(bf16[448,4096]{1,0:T(8,128)(2,1)} %w_ref.2) | copy-start | bytes 11010052
  11.2 55.5 %collective-permute-start.7 = (bf16[224,5248]{1,0:T(8,128)(2,1)}, bf16[224,5248]{1,0:T(8,128)(2,1)}, u32[]{:S(2)}, u32[]{:S(2)}) collective-permute-start(bf16[224,5248]{1,0:T(8,128)(2,1)} %shard_map.110), channel_id=1, source_target_pairs={{0,8},{1,9},{2,10},{3,11},{4,12},{5,13},{6,14},{7,15},{8,0},{9,1},... | collective-permute-start | bytes 7053320 | tf_op jit(solution)/shard_map/ppermute | solution.py:310
  15.2 18.7 %collective-permute-start = (bf16[4,320,128]{2,1,0:T(8,128)(2,1)S(1)}, bf16[4,320,128]{2,1,0:T(8,128)(2,1)S(1)}, u32[]{:S(2)}, u32[]{:S(2)}) collective-permute-start(bf16[4,320,128]{2,1,0:T(8,128)(2,1)S(1)} %get-tuple-element.31.block_ref), channel_id=1, source_target_pairs={{0,1},{1,2},{2,3},{3,4},{4,5},{5,6},{6,7},{7,0},{8,9},{9,10},{10,1... | collective-permute-start | bytes 983048 | tf_op jit(solution)/shard_map/ppermute | solution.py:325
  21.6 14.2 %collective-permute-start.2 = (bf16[4,320,128]{2,1,0:T(8,128)(2,1)S(1)}, bf16[4,320,128]{2,1,0:T(8,128)(2,1)S(1)}, u32[]{:S(2)}, u32[]{:S(2)}) collective-permute-start(bf16[4,320,128]{2,1,0:T(8,128)(2,1)S(1)} %get-tuple-element.31.block_ref), channel_id=1, source_target_pairs={{0,7},{1,0},{2,1},{3,2},{4,3},{5,4},{6,5},{7,6},{8,15},{9,8},{10,9... | collective-permute-start | bytes 983048 | tf_op jit(solution)/shard_map/ppermute | solution.py:325
  33.9 9.0 %collective-permute-start.1 = (bf16[4,320,128]{2,1,0:T(8,128)(2,1)S(1)}, bf16[4,320,128]{2,1,0:T(8,128)(2,1)S(1)}, u32[]{:S(2)}, u32[]{:S(2)}) collective-permute-start(bf16[4,320,128]{2,1,0:T(8,128)(2,1)S(1)} %collective-permute-done.refs_0_), channel_id=1, source_target_pairs={{0,1},{1,2},{2,3},{3,4},{4,5},{5,6},{6,7},{7,0},{8,9},{9,10},{10,1... | collective-permute-start | bytes 983048 | tf_op jit(solution)/shard_map/ppermute | solution.py:330
  35.8 9.0 %collective-permute-start.4 = (bf16[4,320,128]{2,1,0:T(8,128)(2,1)S(1)}, bf16[4,320,128]{2,1,0:T(8,128)(2,1)S(1)}, u32[]{:S(2)}, u32[]{:S(2)}) collective-permute-start(bf16[4,320,128]{2,1,0:T(8,128)(2,1)S(1)} %collective-permute-done.2.refs_1_), channel_id=1, source_target_pairs={{0,7},{1,0},{2,1},{3,2},{4,3},{5,4},{6,5},{7,6},{8,15},{9,8},{10,9... | collective-permute-start | bytes 983048 | tf_op jit(solution)/shard_map/ppermute | solution.py:330
  42.9 9.0 %collective-permute-start.3 = (bf16[4,320,128]{2,1,0:T(8,128)(2,1)S(1)}, bf16[4,320,128]{2,1,0:T(8,128)(2,1)S(1)}, u32[]{:S(2)}, u32[]{:S(2)}) collective-permute-start(bf16[4,320,128]{2,1,0:T(8,128)(2,1)S(1)} %collective-permute-done.1.refs_0_), channel_id=1, source_target_pairs={{0,1},{1,2},{2,3},{3,4},{4,5},{5,6},{6,7},{7,0},{8,9},{9,10},{10,1... | collective-permute-start | bytes 983048 | tf_op jit(solution)/shard_map/ppermute | solution.py:342
  44.9 9.0 %collective-permute-start.6 = (bf16[4,320,128]{2,1,0:T(8,128)(2,1)S(1)}, bf16[4,320,128]{2,1,0:T(8,128)(2,1)S(1)}, u32[]{:S(2)}, u32[]{:S(2)}) collective-permute-start(bf16[4,320,128]{2,1,0:T(8,128)(2,1)S(1)} %collective-permute-done.4.refs_1_), channel_id=1, source_target_pairs={{0,7},{1,0},{2,1},{3,2},{4,3},{5,4},{6,5},{7,6},{8,15},{9,8},{10,9... | collective-permute-start | bytes 983048 | tf_op jit(solution)/shard_map/ppermute | solution.py:342
  52.0 9.0 %collective-permute-start.5 = (bf16[4,320,128]{2,1,0:T(8,128)(2,1)S(1)}, bf16[4,320,128]{2,1,0:T(8,128)(2,1)S(1)}, u32[]{:S(2)}, u32[]{:S(2)}) collective-permute-start(bf16[4,320,128]{2,1,0:T(8,128)(2,1)S(1)} %collective-permute-done.3.refs_0_), channel_id=1, source_target_pairs={{0,1},{1,2},{2,3},{3,4},{4,5},{5,6},{6,7},{7,0},{8,9},{9,10},{10,1... | collective-permute-start | bytes 983048 | tf_op jit(solution)/shard_map/ppermute | solution.py:347
  53.9 7.1 %copy-start.6 = (s32[1,512]{1,0:T(1,128)S(1)}, s32[1,512]{1,0:T(1,128)}, u32[]{:S(2)}) copy-start(s32[1,512]{1,0:T(1,128)} %ids_ref.3) | copy-start | bytes 6148
  53.9 11.3 %copy-start.1 = (bf16[448,4096]{1,0:T(8,128)(2,1)S(1)}, bf16[448,4096]{1,0:T(8,128)(2,1)}, u32[]{:S(2)}) copy-start(bf16[448,4096]{1,0:T(8,128)(2,1)} %w_ref.2) | copy-start | bytes 11010052
  61.4 13.1 %collective-permute-start.9 = (f32[64,128]{1,0:T(8,128)S(1)}, f32[64,128]{1,0:T(8,128)S(1)}, u32[]{:S(2)}, u32[]{:S(2)}) collective-permute-start(f32[64,128]{1,0:T(8,128)S(1)} %get-tuple-element.45.own_ref), channel_id=1, source_target_pairs={{0,16},{1,17},{2,18},{3,19},{4,20},{5,21},{6,22},{7,23},{8,24},{9,... | collective-permute-start | bytes 98312 | tf_op jit(solution)/shard_map/ppermute | solution.py:357
  66.7 12.2 %collective-permute-start.8 = (bf16[224,5248]{1,0:T(8,128)(2,1)}, bf16[224,5248]{1,0:T(8,128)(2,1)S(1)}, u32[]{:S(2)}, u32[]{:S(2)}) collective-permute-start(bf16[224,5248]{1,0:T(8,128)(2,1)} %collective-permute-done.7.refs_0_.near_ref), channel_id=1, source_target_pairs={{0,32},{32,0},{64,96},{96,64},{128,160},{160,128},{192,224},{224,1... | collective-permute-start | bytes 7053320 | tf_op jit(solution)/shard_map/ppermute | solution.py:366

commit v9 on v7

--- a/solution.py
+++ b/solution.py
@@ -250,8 +250,7 @@
     product = product[:, :wide] + product[:, wide:] + mm(low_ref[...], high)
     devices = sent_ref.shape[0]
     product = product.reshape(devices, 2 * SEQ_DEV, wide)
-    parts = [product] + [part.astype(F32) for part in halves(down_ref[...])]
-    sent_ref[...] = jnp.concatenate(parts, axis=1).astype(BF16)
+    sent_ref[...] = jnp.concatenate([product, down_ref[...]], axis=1).astype(BF16)
 
 
 def per_device(
@@ -387,14 +386,13 @@
     )
     sent = call(
         last_kernel,
-        shape((mp_size, 4 * SEQ_DEV, 2 * rank), BF16),
+        shape((mp_size, 3 * SEQ_DEV, 2 * rank), BF16),
         [VMEM] * 4,
         (total, high, low, down_raw),
         6 * high.size * rank,
     )
     got = jnp.sum(lax.all_to_all(sent, "mp", 0, 0).astype(F32), axis=0)
-    paired = got[: 2 * SEQ_DEV]
-    down_raw = got[2 * SEQ_DEV : 3 * SEQ_DEV] + got[3 * SEQ_DEV :]
+    paired, down_raw = got[: 2 * SEQ_DEV], got[2 * SEQ_DEV :]
     paired = paired.reshape(2, SEQ_DEV, 2, rank).transpose(1, 2, 0, 3).reshape(SEQ_DEV, 2, 2 * rank)
     raw = jnp.concatenate([paired, down_raw[:, None]], axis=1)
 

time: 133 us -> 131 us (0.985)
  blocking collectives: 46.4 us -> 44.9 us
where the time goes in v9:
time: 131 us
  starting transfers between devices  51.5 us (39%)
  blocking collectives  44.9 us (34%)
  waiting for transfers between devices  20 us (15%)
  Pallas kernels  10.7 us (8%)
  local copies, waits for them, and re-layouts  2.27 us (2%)
    all_to_all x2, blocking collectives, per_device(): lax.all_to_all(jnp.broadcast_to(squares, (size, 1, 128)), axis, 0, 0)  30.5 us
    ppermute x3, starting transfers between devices, per_device(): lax.ppermute(down, 'mp', z_shift(-1))  17.7 us
    all_to_all x1, blocking collectives, per_device(): got = jnp.sum(lax.all_to_all(sent, 'mp', 0, 0).astype(F32), axis=0)  14.4 us
    pallas_call x14, Pallas kernels, call(): pl.pallas_call(kernel, out_shape=out_shape, in_specs=specs, out_specs=out...  10.7 us
    ppermute x3, starting transfers between devices, per_device(): lax.ppermute(up, 'mp', z_shift(1))  10.4 us
    ppermute x1, starting transfers between devices, per_device(): other = lax.ppermute(near, 'dp', cores)  9.16 us
    ppermute x3, waiting for transfers between devices, per_device(): lax.ppermute(up, 'mp', z_shift(1))  7.91 us
    ppermute x1, waiting for transfers between devices, per_device(): far = lax.ppermute(up, 'mp', z_shift(1))  6.88 us
  transfers between devices with their start and end apart: 11, of which 7 were waited for; matrix products, arithmetic and copies ran while one was open for 0% of the time, Pallas kernels for 5%

profile of v9, /device:TPU:1, one launch (start us, length us, event | category | flops | bytes accessed | tf_op | source)
XLA Modules:
  0.0 130.6 jit_solution(14183512351406860354)
XLA Ops:
  0.0 0.0 copy-start.2
  0.0 0.0 copy-start.3
  0.0 0.0 copy-start.4
  0.0 0.0 copy-start.5
  0.0 2.7 %shard_map.109 = bf16[4,640,128]{2,1,0:T(8,128)(2,1)} custom-call(bf16[512,128]{1,0:T(8,128)(2,1)} %input_hbm.1, bf16[512,128]{1,0:T(8,128)(2,1)} %grad_hbm.1, bf16[448,512]{1,0:T(8,128)(2,1)} %bitcast.16, bf16[448,512]{1,0:T(8,128)(2,1)} %bitcast.19, bf16[64,128]{1,0:T(8,128)(2,1)} %bitcast.30, bf16[64,128]{1,0:T(8,128)(2,1)} %proj_out_hbm.1, ...), custom_call_target="tpu_custom_call" | custom-call | flops 46137344 | bytes 1269760 | tf_op jit(solution)/shard_map/pallas_call | solution.py:60
  2.7 4.9 %all-to-all-start = ((bf16[4,640,128]{2,1,0:T(8,128)(2,1)}), bf16[4,640,128]{2,1,0:T(8,128)(2,1)}, u32[]{:S(2)}, u32[]{:S(2)}) async-start(bf16[4,640,128]{2,1,0:T(8,128)(2,1)} %shard_map.109), calls=%async_computation | async-start | bytes 1310720 | tf_op jit(solution)/shard_map/all_to_all | solution.py:308
  7.5 0.0 copy-done.2
  7.5 0.0 copy-done.3
  7.5 0.0 copy-done.4
  7.6 0.0 copy-done.5
  7.6 0.0 copy-start
  7.6 2.0 %copy-done = bf16[448,4096]{1,0:T(8,128)(2,1)S(1)} copy-done((bf16[448,4096]{1,0:T(8,128)(2,1)S(1)}, bf16[448,4096]{1,0:T(8,128)(2,1)}, u32[]{:S(2)}) %copy-start) | copy-done | bytes 3670040
  9.6 1.6 %shard_map.110 = bf16[224,5248]{1,0:T(8,128)(2,1)} custom-call(bf16[448,4096]{1,0:T(8,128)(2,1)S(1)} %copy-done, bf16[448,512]{1,0:T(8,128)(2,1)S(1)} %bitcast.17, bf16[448,512]{1,0:T(8,128)(2,1)S(1)} %bitcast.20, bf16[64,448]{1,0:T(8,128)(2,1)S(1)} %bitcast.22, bf16[64,448]{1,0:T(8,128)(2,1)S(1)} %bitcast.24), custom_call_target="tpu_custom_call" | custom-call | flops 1835008 | bytes 4702208 | tf_op jit(solution)/shard_map/pallas_call | solution.py:60
  11.2 3.4 %collective-permute-start.7 = (bf16[224,5248]{1,0:T(8,128)(2,1)}, bf16[224,5248]{1,0:T(8,128)(2,1)S(1)}, u32[]{:S(2)}, u32[]{:S(2)}) collective-permute-start(bf16[224,5248]{1,0:T(8,128)(2,1)} %shard_map.110), channel_id=1, source_target_pairs={{0,8},{1,9},{2,10},{3,11},{4,12},{5,13},{6,14},{7,15},{8,0},{9,1},... | collective-permute-start | bytes 7053320 | tf_op jit(solution)/shard_map/ppermute | solution.py:309
  14.6 0.7 all-to-all-done.got_ref
  15.3 1.1 shard_map.111
  16.4 6.6 %collective-permute-start = (bf16[4,320,128]{2,1,0:T(8,128)(2,1)S(1)}, bf16[4,320,128]{2,1,0:T(8,128)(2,1)S(1)}, u32[]{:S(2)}, u32[]{:S(2)}) collective-permute-start(bf16[4,320,128]{2,1,0:T(8,128)(2,1)S(1)} %get-tuple-element.33.block_ref), channel_id=1, source_target_pairs={{0,1},{1,2},{2,3},{3,4},{4,5},{5,6},{6,7},{7,0},{8,9},{9,10},{10,1... | collective-permute-start | bytes 983048 | tf_op jit(solution)/shard_map/ppermute | solution.py:324
  23.0 8.6 %collective-permute-start.2 = (bf16[4,320,128]{2,1,0:T(8,128)(2,1)S(1)}, bf16[4,320,128]{2,1,0:T(8,128)(2,1)S(1)}, u32[]{:S(2)}, u32[]{:S(2)}) collective-permute-start(bf16[4,320,128]{2,1,0:T(8,128)(2,1)S(1)} %get-tuple-element.33.block_ref), channel_id=1, source_target_pairs={{0,7},{1,0},{2,1},{3,2},{4,3},{5,4},{6,5},{7,6},{8,15},{9,8},{10,9... | collective-permute-start | bytes 983048 | tf_op jit(solution)/shard_map/ppermute | solution.py:324
  31.6 0.3 shard_map.114
  31.9 0.1 shard_map.112.refs_2_
  32.0 3.3 %collective-permute-done.refs_0_ = bf16[4,320,128]{2,1,0:T(8,128)(2,1)S(1)} collective-permute-done((bf16[4,320,128]{2,1,0:T(8,128)(2,1)S(1)}, bf16[4,320,128]{2,1,0:T(8,128)(2,1)S(1)}, u32[]{:S(2)}, u32[]{:S(2)}) %collective-permute-start) | collective-permute-done | bytes 327712 | tf_op jit(solution)/shard_map/ppermute | solution.py:324
  35.2 1.9 %collective-permute-start.1 = (bf16[4,320,128]{2,1,0:T(8,128)(2,1)S(1)}, bf16[4,320,128]{2,1,0:T(8,128)(2,1)S(1)}, u32[]{:S(2)}, u32[]{:S(2)}) collective-permute-start(bf16[4,320,128]{2,1,0:T(8,128)(2,1)S(1)} %collective-permute-done.refs_0_), channel_id=1, source_target_pairs={{0,1},{1,2},{2,3},{3,4},{4,5},{5,6},{6,7},{7,0},{8,9},{9,10},{10,1... | collective-permute-start | bytes 983048 | tf_op jit(solution)/shard_map/ppermute | solution.py:329
  37.1 0.0 collective-permute-done.2.refs_1_
  37.2 4.6 %collective-permute-start.4 = (bf16[4,320,128]{2,1,0:T(8,128)(2,1)S(1)}, bf16[4,320,128]{2,1,0:T(8,128)(2,1)S(1)}, u32[]{:S(2)}, u32[]{:S(2)}) collective-permute-start(bf16[4,320,128]{2,1,0:T(8,128)(2,1)S(1)} %collective-permute-done.2.refs_1_), channel_id=1, source_target_pairs={{0,7},{1,0},{2,1},{3,2},{4,3},{5,4},{6,5},{7,6},{8,15},{9,8},{10,9... | collective-permute-start | bytes 983048 | tf_op jit(solution)/shard_map/ppermute | solution.py:329
  41.7 0.2 shard_map.113
  41.9 2.3 %collective-permute-done.1.refs_0_ = bf16[4,320,128]{2,1,0:T(8,128)(2,1)S(1)} collective-permute-done((bf16[4,320,128]{2,1,0:T(8,128)(2,1)S(1)}, bf16[4,320,128]{2,1,0:T(8,128)(2,1)S(1)}, u32[]{:S(2)}, u32[]{:S(2)}) %collective-permute-start.1) | collective-permute-done | bytes 327712 | tf_op jit(solution)/shard_map/ppermute | solution.py:329
  44.3 1.9 %collective-permute-start.3 = (bf16[4,320,128]{2,1,0:T(8,128)(2,1)S(1)}, bf16[4,320,128]{2,1,0:T(8,128)(2,1)S(1)}, u32[]{:S(2)}, u32[]{:S(2)}) collective-permute-start(bf16[4,320,128]{2,1,0:T(8,128)(2,1)S(1)} %collective-permute-done.1.refs_0_), channel_id=1, source_target_pairs={{0,1},{1,2},{2,3},{3,4},{4,5},{5,6},{6,7},{7,0},{8,9},{9,10},{10,1... | collective-permute-start | bytes 983048 | tf_op jit(solution)/shard_map/ppermute | solution.py:341
  46.2 0.0 collective-permute-done.4.refs_1_
  46.2 4.6 %collective-permute-start.6 = (bf16[4,320,128]{2,1,0:T(8,128)(2,1)S(1)}, bf16[4,320,128]{2,1,0:T(8,128)(2,1)S(1)}, u32[]{:S(2)}, u32[]{:S(2)}) collective-permute-start(bf16[4,320,128]{2,1,0:T(8,128)(2,1)S(1)} %collective-permute-done.4.refs_1_), channel_id=1, source_target_pairs={{0,7},{1,0},{2,1},{3,2},{4,3},{5,4},{6,5},{7,6},{8,15},{9,8},{10,9... | collective-permute-start | bytes 983048 | tf_op jit(solution)/shard_map/ppermute | solution.py:341
  50.8 0.2 shard_map.115
  50.9 2.3 %collective-permute-done.3.refs_0_ = bf16[4,320,128]{2,1,0:T(8,128)(2,1)S(1)} collective-permute-done((bf16[4,320,128]{2,1,0:T(8,128)(2,1)S(1)}, bf16[4,320,128]{2,1,0:T(8,128)(2,1)S(1)}, u32[]{:S(2)}, u32[]{:S(2)}) %collective-permute-start.3) | collective-permute-done | bytes 327712 | tf_op jit(solution)/shard_map/ppermute | solution.py:341
  53.3 1.9 %collective-permute-start.5 = (bf16[4,320,128]{2,1,0:T(8,128)(2,1)S(1)}, bf16[4,320,128]{2,1,0:T(8,128)(2,1)S(1)}, u32[]{:S(2)}, u32[]{:S(2)}) collective-permute-start(bf16[4,320,128]{2,1,0:T(8,128)(2,1)S(1)} %collective-permute-done.3.refs_0_), channel_id=1, source_target_pairs={{0,1},{1,2},{2,3},{3,4},{4,5},{5,6},{6,7},{7,0},{8,9},{9,10},{10,1... | collective-permute-start | bytes 983048 | tf_op jit(solution)/shard_map/ppermute | solution.py:346
  55.2 0.0 collective-permute-done.6.refs_1_
  55.2 0.0 copy-start.6
  55.2 0.0 copy-start.1
  55.2 0.2 shard_map.116
  55.4 6.9 %collective-permute-done.5.block_ref = bf16[4,320,128]{2,1,0:T(8,128)(2,1)S(1)} collective-permute-done((bf16[4,320,128]{2,1,0:T(8,128)(2,1)S(1)}, bf16[4,320,128]{2,1,0:T(8,128)(2,1)S(1)}, u32[]{:S(2)}, u32[]{:S(2)}) %collective-permute-start.5) | collective-permute-done | bytes 327712 | tf_op jit(solution)/shard_map/ppermute | solution.py:346
  62.3 0.0 copy-done.6
  62.3 0.5 shard_map.117
  62.8 4.1 %collective-permute-start.8 = (f32[64,128]{1,0:T(8,128)S(1)}, f32[64,128]{1,0:T(8,128)S(1)}, u32[]{:S(2)}, u32[]{:S(2)}) collective-permute-start(f32[64,128]{1,0:T(8,128)S(1)} %get-tuple-element.47.own_ref), channel_id=1, source_target_pairs={{0,16},{1,17},{2,18},{3,19},{4,20},{5,21},{6,22},{7,23},{8,24},{9,... | collective-permute-start | bytes 98312 | tf_op jit(solution)/shard_map/ppermute | solution.py:356
  66.9 0.0 copy-done.1
  66.9 1.6 %shard_map.118.own_ref = f32[256,128]{1,0:T(8,128)S(1)} custom-call(bf16[256,4096]{1,0:T(8,128)(2,1)S(1)} %get-tuple-element.46.grad_ref, bf16[448,4096]{1,0:T(8,128)(2,1)S(1)} %copy-done.1, f32[256,448]{1,0:T(8,128)S(1)} %get-tuple-element.48.activated_ref, f32[256,448]{1,0:T(8,128)S(1)} %get-tuple-element.37.slope_ref, bf16[64,448]{1,0:T(8,128)(2,1)S(1)} %bitcast.23, ...), custom_call_target="tpu_custom_call" | custom-call | flops 939524096 | bytes 6799360 | tf_op jit(solution)/shard_map/pallas_call | solution.py:60
  68.5 0.9 collective-permute-done.8.other_ref
  69.3 0.0 collective-permute-done.7.refs_0_.near_ref
  69.3 9.2 %collective-permute-start.9 = (bf16[224,5248]{1,0:T(8,128)(2,1)S(1)}, bf16[224,5248]{1,0:T(8,128)(2,1)S(1)}, u32[]{:S(2)}, u32[]{:S(2)}) collective-permute-start(bf16[224,5248]{1,0:T(8,128)(2,1)S(1)} %collective-permute-done.7.refs_0_.near_ref), channel_id=1, source_target_pairs={{0,32},{32,0},{64,96},{96,64},{128,160},{160,128},{192,224},{224,1... | collective-permute-start | bytes 7053320 | tf_op jit(solution)/shard_map/ppermute | solution.py:365
  78.5 0.1 shard_map.121
  78.7 0.3 shard_map.119
  79.0 3.7 %collective-permute-done.9.other_ref = bf16[224,5248]{1,0:T(8,128)(2,1)S(1)} collective-permute-done((bf16[224,5248]{1,0:T(8,128)(2,1)S(1)}, bf16[224,5248]{1,0:T(8,128)(2,1)S(1)}, u32[]{:S(2)}, u32[]{:S(2)}) %collective-permute-start.9) | collective-permute-done | bytes 2351136 | tf_op jit(solution)/shard_map/ppermute | solution.py:365
  82.6 1.6 %shard_map.120.total_ref = f32[256,128]{1,0:T(8,128)S(1)} custom-call(bf16[256,4096]{1,0:T(8,128)(2,1)S(1)} %get-tuple-element.46.grad_ref, bf16[224,5248]{1,0:T(8,128)(2,1)S(1)} %collective-permute-done.7.refs_0_.near_ref, bf16[224,5248]{1,0:T(8,128)(2,1)S(1)} %collective-permute-done.9.other_ref, f32[256,448]{1,0:T(8,128)S(1)} %get-tuple-element.50.activated_ref, ...), custom_call_target="tpu_custom_call" | custom-call | flops 939524096 | bytes 7847936 | tf_op jit(solution)/shard_map/pallas_call | solution.py:60
  84.3 0.3 shard_map.122
  84.6 14.4 %all_to_all.20 = bf16[32,24,128]{2,1,0:T(8,128)(2,1)S(1)} all-to-all(bf16[32,24,128]{2,1,0:T(8,128)(2,1)S(1)} %shard_map.122), channel_id=1, replica_groups=mesh['dp'=16,'mp'=32] {'mp'}, dimensions={0} | all-to-all | bytes 393216 | tf_op jit(solution)/shard_map/all_to_all | solution.py:394
  99.1 0.1 reshape.29
  99.2 0.1 reshape.30
  99.2 0.1 multiply_reduce_fusion
  99.4 13.9 %all_to_all.21 = f32[32,1,128]{2,1,0:T(1,128)S(1)} all-to-all(f32[32,1,128]{2,1,0:T(1,128)S(1)} %broadcast_in_dim.9), channel_id=1, replica_groups=mesh['dp'=16,'mp'=32] {'mp'}, dimensions={0} | all-to-all | bytes 32768 | tf_op jit(solution)/shard_map/all_to_all | solution.py:403
  113.3 16.6 %all_to_all.22 = f32[16,1,128]{2,1,0:T(1,128)S(1)} all-to-all(f32[16,1,128]{2,1,0:T(1,128)S(1)} %broadcast_in_dim.20), channel_id=1, replica_groups=mesh['dp'=16,'mp'=32] {'dp'}, dimensions={0} | all-to-all | bytes 16384 | tf_op jit(solution)/shard_map/all_to_all | solution.py:403
  130.0 0.7 fusion
  (10 shorter events, 0.1 us)
Async XLA Ops:
  0.0 7.5 %copy-start.2 = (bf16[512,448]{0,1:T(8,128)(2,1)S(1)}, bf16[512,448]{0,1:T(8,128)(2,1)}, u32[]{:S(2)}) copy-start(bf16[512,448]{0,1:T(8,128)(2,1)} %param.12) | copy-start | bytes 1376260
  0.0 7.5 %copy-start.3 = (bf16[512,448]{0,1:T(8,128)(2,1)S(1)}, bf16[512,448]{0,1:T(8,128)(2,1)}, u32[]{:S(2)}) copy-start(bf16[512,448]{0,1:T(8,128)(2,1)} %param.13) | copy-start | bytes 1376260
  0.0 7.5 %copy-start.4 = (bf16[448,64]{0,1:T(8,128)(2,1)S(1)}, bf16[448,64]{0,1:T(8,128)(2,1)}, u32[]{:S(2)}) copy-start(bf16[448,64]{0,1:T(8,128)(2,1)} %param.18) | copy-start | bytes 172036
  0.0 7.5 %copy-start.5 = (bf16[448,64]{0,1:T(8,128)(2,1)S(1)}, bf16[448,64]{0,1:T(8,128)(2,1)}, u32[]{:S(2)}) copy-start(bf16[448,64]{0,1:T(8,128)(2,1)} %param.19) | copy-start | bytes 172036
  2.7 12.6 %all-to-all-start = ((bf16[4,640,128]{2,1,0:T(8,128)(2,1)}), bf16[4,640,128]{2,1,0:T(8,128)(2,1)}, u32[]{:S(2)}, u32[]{:S(2)}) async-start(bf16[4,640,128]{2,1,0:T(8,128)(2,1)} %shard_map.109), calls=%async_computation | async-start | bytes 1310720 | tf_op jit(solution)/shard_map/all_to_all | solution.py:308
  7.6 2.0 %copy-start = (bf16[448,4096]{1,0:T(8,128)(2,1)S(1)}, bf16[448,4096]{1,0:T(8,128)(2,1)}, u32[]{:S(2)}) copy-start(bf16[448,4096]{1,0:T(8,128)(2,1)} %w_ref.2) | copy-start | bytes 11010052
  11.2 58.1 %collective-permute-start.7 = (bf16[224,5248]{1,0:T(8,128)(2,1)}, bf16[224,5248]{1,0:T(8,128)(2,1)S(1)}, u32[]{:S(2)}, u32[]{:S(2)}) collective-permute-start(bf16[224,5248]{1,0:T(8,128)(2,1)} %shard_map.110), channel_id=1, source_target_pairs={{0,8},{1,9},{2,10},{3,11},{4,12},{5,13},{6,14},{7,15},{8,0},{9,1},... | collective-permute-start | bytes 7053320 | tf_op jit(solution)/shard_map/ppermute | solution.py:309
  16.4 18.8 %collective-permute-start = (bf16[4,320,128]{2,1,0:T(8,128)(2,1)S(1)}, bf16[4,320,128]{2,1,0:T(8,128)(2,1)S(1)}, u32[]{:S(2)}, u32[]{:S(2)}) collective-permute-start(bf16[4,320,128]{2,1,0:T(8,128)(2,1)S(1)} %get-tuple-element.33.block_ref), channel_id=1, source_target_pairs={{0,1},{1,2},{2,3},{3,4},{4,5},{5,6},{6,7},{7,0},{8,9},{9,10},{10,1... | collective-permute-start | bytes 983048 | tf_op jit(solution)/shard_map/ppermute | solution.py:324
  23.0 14.2 %collective-permute-start.2 = (bf16[4,320,128]{2,1,0:T(8,128)(2,1)S(1)}, bf16[4,320,128]{2,1,0:T(8,128)(2,1)S(1)}, u32[]{:S(2)}, u32[]{:S(2)}) collective-permute-start(bf16[4,320,128]{2,1,0:T(8,128)(2,1)S(1)} %get-tuple-element.33.block_ref), channel_id=1, source_target_pairs={{0,7},{1,0},{2,1},{3,2},{4,3},{5,4},{6,5},{7,6},{8,15},{9,8},{10,9... | collective-permute-start | bytes 983048 | tf_op jit(solution)/shard_map/ppermute | solution.py:324
  35.2 9.0 %collective-permute-start.1 = (bf16[4,320,128]{2,1,0:T(8,128)(2,1)S(1)}, bf16[4,320,128]{2,1,0:T(8,128)(2,1)S(1)}, u32[]{:S(2)}, u32[]{:S(2)}) collective-permute-start(bf16[4,320,128]{2,1,0:T(8,128)(2,1)S(1)} %collective-permute-done.refs_0_), channel_id=1, source_target_pairs={{0,1},{1,2},{2,3},{3,4},{4,5},{5,6},{6,7},{7,0},{8,9},{9,10},{10,1... | collective-permute-start | bytes 983048 | tf_op jit(solution)/shard_map/ppermute | solution.py:329
  37.2 9.0 %collective-permute-start.4 = (bf16[4,320,128]{2,1,0:T(8,128)(2,1)S(1)}, bf16[4,320,128]{2,1,0:T(8,128)(2,1)S(1)}, u32[]{:S(2)}, u32[]{:S(2)}) collective-permute-start(bf16[4,320,128]{2,1,0:T(8,128)(2,1)S(1)} %collective-permute-done.2.refs_1_), channel_id=1, source_target_pairs={{0,7},{1,0},{2,1},{3,2},{4,3},{5,4},{6,5},{7,6},{8,15},{9,8},{10,9... | collective-permute-start | bytes 983048 | tf_op jit(solution)/shard_map/ppermute | solution.py:329
  44.3 9.0 %collective-permute-start.3 = (bf16[4,320,128]{2,1,0:T(8,128)(2,1)S(1)}, bf16[4,320,128]{2,1,0:T(8,128)(2,1)S(1)}, u32[]{:S(2)}, u32[]{:S(2)}) collective-permute-start(bf16[4,320,128]{2,1,0:T(8,128)(2,1)S(1)} %collective-permute-done.1.refs_0_), channel_id=1, source_target_pairs={{0,1},{1,2},{2,3},{3,4},{4,5},{5,6},{6,7},{7,0},{8,9},{9,10},{10,1... | collective-permute-start | bytes 983048 | tf_op jit(solution)/shard_map/ppermute | solution.py:341
  46.2 9.0 %collective-permute-start.6 = (bf16[4,320,128]{2,1,0:T(8,128)(2,1)S(1)}, bf16[4,320,128]{2,1,0:T(8,128)(2,1)S(1)}, u32[]{:S(2)}, u32[]{:S(2)}) collective-permute-start(bf16[4,320,128]{2,1,0:T(8,128)(2,1)S(1)} %collective-permute-done.4.refs_1_), channel_id=1, source_target_pairs={{0,7},{1,0},{2,1},{3,2},{4,3},{5,4},{6,5},{7,6},{8,15},{9,8},{10,9... | collective-permute-start | bytes 983048 | tf_op jit(solution)/shard_map/ppermute | solution.py:341
  53.3 9.0 %collective-permute-start.5 = (bf16[4,320,128]{2,1,0:T(8,128)(2,1)S(1)}, bf16[4,320,128]{2,1,0:T(8,128)(2,1)S(1)}, u32[]{:S(2)}, u32[]{:S(2)}) collective-permute-start(bf16[4,320,128]{2,1,0:T(8,128)(2,1)S(1)} %collective-permute-done.3.refs_0_), channel_id=1, source_target_pairs={{0,1},{1,2},{2,3},{3,4},{4,5},{5,6},{6,7},{7,0},{8,9},{9,10},{10,1... | collective-permute-start | bytes 983048 | tf_op jit(solution)/shard_map/ppermute | solution.py:346
  55.2 7.1 %copy-start.6 = (s32[1,512]{1,0:T(1,128)S(1)}, s32[1,512]{1,0:T(1,128)}, u32[]{:S(2)}) copy-start(s32[1,512]{1,0:T(1,128)} %ids_ref.3) | copy-start | bytes 6148
  55.2 11.7 %copy-start.1 = (bf16[448,4096]{1,0:T(8,128)(2,1)S(1)}, bf16[448,4096]{1,0:T(8,128)(2,1)}, u32[]{:S(2)}) copy-start(bf16[448,4096]{1,0:T(8,128)(2,1)} %w_ref.2) | copy-start | bytes 11010052
  62.8 6.6 %collective-permute-start.8 = (f32[64,128]{1,0:T(8,128)S(1)}, f32[64,128]{1,0:T(8,128)S(1)}, u32[]{:S(2)}, u32[]{:S(2)}) collective-permute-start(f32[64,128]{1,0:T(8,128)S(1)} %get-tuple-element.47.own_ref), channel_id=1, source_target_pairs={{0,16},{1,17},{2,18},{3,19},{4,20},{5,21},{6,22},{7,23},{8,24},{9,... | collective-permute-start | bytes 98312 | tf_op jit(solution)/shard_map/ppermute | solution.py:356
  69.3 13.3 %collective-permute-start.9 = (bf16[224,5248]{1,0:T(8,128)(2,1)S(1)}, bf16[224,5248]{1,0:T(8,128)(2,1)S(1)}, u32[]{:S(2)}, u32[]{:S(2)}) collective-permute-start(bf16[224,5248]{1,0:T(8,128)(2,1)S(1)} %collective-permute-done.7.refs_0_.near_ref), channel_id=1, source_target_pairs={{0,32},{32,0},{64,96},{96,64},{128,160},{160,128},{192,224},{224,1... | collective-permute-start | bytes 7053320 | tf_op jit(solution)/shard_map/ppermute | solution.py:365
